TPU v7x, 32 devices: a whole 2x2x4 slice. The times are simulated.
32 devices in a mesh: group: 2 (over x), wide: 16 (over z, y, core).
Axes of the slice: x: 2, y: 2, z: 4, core: 2. Of those that a mesh axis runs over, the one named last changes fastest.
Arguments:
- visibilities: float32 [6144, 2, 128], P(('group', 'wide')), parts along dimension 0, may hold values from -6 to 6
- offsets: float32 [6144, 2, 128], P(('group', 'wide')), parts along dimension 0, may hold values from 2 to 30
- vis_count: int32 [6144], P(('group', 'wide')), parts along dimension 0, may hold values from 1 to 128, 294912 in all
- owner: int32 [6144], P(('group', 'wide')), parts along dimension 0, may hold values from 0 to 15, as said below
- tile_row: int32 [6144], P(('group', 'wide')), parts along dimension 0, may hold values from 0 to 7
- tile_col: int32 [6144], P(('group', 'wide')), parts along dimension 0, may hold values from 0 to 127
Outputs:
- image: float32 [2, 8192, 4096], P(None, 'group', 'wide'), parts along dimension 1
There are 2 independent parts, one for each index of `group`. A program takes and returns all parts, laid end to end along the dimension named above; each array names one. Nothing has to cross between parts.
Inputs may be any that keep to these rules, and one draw needn't show every extreme that they name: At most 36 subgrids of one device have the same owner; in every draw one owner receives exactly 36 subgrids from every device. `vis_count`: the live visibilities of a subgrid are the first ones of its slots; some subgrid has all 128 live; over each part along group the counts sum to 294912.
All inputs are finite; a program needn't handle non-finite values.
Results may differ from a plain program's by a relative error of at most 0.0003.
Values sent between devices are 32-bit elements; how exact they have to be, the bound alone decides.
No kernel may reach another device: no remote copies, remote signals or barrier semaphores. Data moves between devices by JAX's collectives and lax.ppermute only.
A program may use at most 128 MiB of HBM per device.

v0:
```python
import math

import jax
import jax.numpy as jnp
from jax import lax
from jax.sharding import PartitionSpec as P

SUB = 32
VIS = 128
SUB_DEV = 192
GRID = 4096
FA = 128


highest = lax.Precision.HIGHEST


def cplx_einsum(pattern, left_real, left_imag, right_real, right_imag):

    def single(first, second):
        return jnp.einsum(pattern, first, second, precision=highest)

    return (
        single(left_real, right_real) - single(left_imag, right_imag),
        single(left_real, right_imag) + single(left_imag, right_real),
    )


def dft_table(length, factor):
    indices = jnp.arange(length)
    phase_int = indices[:, None] * indices[None, :] % length
    angles = -2.0 * math.pi / length * phase_int.astype(jnp.float32)
    return (jnp.cos(angles) * factor, jnp.sin(angles) * factor)


def twiddle_table():
    outer_size = GRID // FA
    phase_int = jnp.arange(outer_size)[:, None] * jnp.arange(FA)[None, :] % GRID
    angles = -2.0 * math.pi / GRID * phase_int.astype(jnp.float32)
    return (jnp.cos(angles), jnp.sin(angles))


def subgrid_spectra(samples, counts):
    subgrid_count = samples.shape[0]
    position = (jnp.arange(SUB, dtype=jnp.float32) - SUB // 2) / SUB
    live_mask = jnp.where(jnp.arange(VIS)[None, :] < counts[:, None], 1.0 / math.sqrt(VIS), 0.0)
    vis_real = samples[:, 0] * live_mask
    vis_imag = samples[:, 1] * live_mask
    angle_u = 2.0 * math.pi * samples[:, 2, :, None] * position
    angle_v = 2.0 * math.pi * samples[:, 3, :, None] * position
    cos_u, sin_u = (jnp.cos(angle_u), jnp.sin(angle_u))
    cos_v, sin_v = (jnp.cos(angle_v), jnp.sin(angle_v))
    table_real, table_imag = dft_table(SUB, 1.0 / math.sqrt(SUB))
    weight_real = vis_real[:, :, None] * cos_u - vis_imag[:, :, None] * sin_u
    weight_imag = vis_real[:, :, None] * sin_u + vis_imag[:, :, None] * cos_u
    pixel_real, pixel_imag = cplx_einsum("nki,nkj->nij", weight_real, weight_imag, cos_v, sin_v)
    half_real, half_imag = cplx_einsum(
        "nij,ip->npj", pixel_real, pixel_imag, table_real, table_imag
    )
    spec_real, spec_imag = cplx_einsum("npj,jq->npq", half_real, half_imag, table_real, table_imag)
    return jnp.stack([spec_real, spec_imag], axis=1).reshape(subgrid_count, 2 * SUB * SUB)


def transform_last(real_x, imag_x):
    row_count = real_x.shape[0]
    outer_size = GRID // FA
    outer_real, outer_imag = dft_table(outer_size, 1.0 / math.sqrt(outer_size))
    inner_real, inner_imag = dft_table(FA, 1.0 / math.sqrt(FA))
    twist_real, twist_imag = twiddle_table()
    first_real, first_imag = cplx_einsum(
        "rqn,qk->rkn",
        real_x.reshape(row_count, outer_size, FA),
        imag_x.reshape(row_count, outer_size, FA),
        outer_real,
        outer_imag,
    )
    turned_real = first_real * twist_real - first_imag * twist_imag
    turned_imag = first_real * twist_imag + first_imag * twist_real
    final_real, final_imag = cplx_einsum(
        "rkn,nm->rmk", turned_real, turned_imag, inner_real, inner_imag
    )
    return (final_real.reshape(row_count, GRID), final_imag.reshape(row_count, GRID))


def transform_first(real_x, imag_x):
    col_count = real_x.shape[1]
    outer_size = GRID // FA
    outer_real, outer_imag = dft_table(outer_size, 1.0 / math.sqrt(outer_size))
    inner_real, inner_imag = dft_table(FA, 1.0 / math.sqrt(FA))
    twist_real, twist_imag = twiddle_table()
    first_real, first_imag = cplx_einsum(
        "qnc,qk->knc",
        real_x.reshape(outer_size, FA, col_count),
        imag_x.reshape(outer_size, FA, col_count),
        outer_real,
        outer_imag,
    )
    turned_real = first_real * twist_real[:, :, None] - first_imag * twist_imag[:, :, None]
    turned_imag = first_real * twist_imag[:, :, None] + first_imag * twist_real[:, :, None]
    final_real, final_imag = cplx_einsum(
        "knc,nm->mkc", turned_real, turned_imag, inner_real, inner_imag
    )
    return (final_real.reshape(GRID, col_count), final_imag.reshape(GRID, col_count))


def per_device(visibilities, offsets, vis_count, owner, tile_row, tile_col):
    owners = lax.axis_size("wide")
    capacity = 3 * SUB_DEV // owners
    band_tiles = GRID // (SUB * owners)
    tile_cols = GRID // SUB
    spectrum_size = 2 * SUB * SUB
    samples = jnp.concatenate([visibilities, offsets], axis=1)
    tile_ids = (tile_row * tile_cols + tile_col).astype(jnp.float32)
    onehot = (owner[:, None] == jnp.arange(owners)[None, :]).astype(jnp.int32)
    ranked = jnp.cumsum(onehot, axis=0) - 1
    slot_of = jnp.sum(ranked * onehot, axis=1)
    local_spectra = subgrid_spectra(samples, vis_count.astype(jnp.float32))
    packed = (
        jnp.zeros((owners, capacity, spectrum_size), jnp.float32)
        .at[owner, slot_of]
        .set(local_spectra)
    )
    labels = jnp.zeros((owners, capacity), jnp.float32).at[owner, slot_of].set(tile_ids)
    got_spectra, got_ids = (
        lax.all_to_all(packed, "wide", split_axis=0, concat_axis=0, tiled=True),
        lax.all_to_all(labels, "wide", split_axis=0, concat_axis=0, tiled=True),
    )
    received = got_spectra.reshape(-1, spectrum_size)
    tile_index = got_ids.reshape(-1).astype(jnp.int32)
    grid_tiles = (
        jnp.zeros((band_tiles * tile_cols, spectrum_size), jnp.float32).at[tile_index].add(received)
    )
    grid_band = grid_tiles.reshape(band_tiles, tile_cols, 2, SUB, SUB).transpose(2, 0, 3, 1, 4)
    grid_band = grid_band.reshape(2, band_tiles * SUB, GRID)
    row_real, row_imag = transform_last(grid_band[0], grid_band[1])
    column_band = lax.all_to_all(
        jnp.stack([row_real, row_imag]), "wide", split_axis=2, concat_axis=1, tiled=True
    )
    out_real, out_imag = transform_first(column_band[0], column_band[1])
    return jnp.stack([out_real, out_imag])


def solution(mesh):
    placed = (
        P(("group", "wide"), None, None),
        P(("group", "wide"), None, None),
        P(("group", "wide")),
        P(("group", "wide")),
        P(("group", "wide")),
        P(("group", "wide")),
    )
    return jax.shard_map(
        per_device, mesh=mesh, in_specs=placed, out_specs=P(None, "group", "wide"), check_vma=False
    )
```

profile of v0, /device:TPU:13, one launch (start us, length us, event | category | flops | bytes accessed | tf_op | source)
XLA Modules:
  0.0 782.7 jit_solution(1957485155887494097)
XLA Ops:
  4.3 27.5 %scatter_fusion = f32[16,36]{1,0:T(8,128)} fusion(f32[16,36]{1,0:T(8,128)} %broadcast_in_dim.17, s32[192]{0:T(256)S(1)} %bitcast.127, f32[192]{0:T(256)S(1)} %add_convert_fusion), kind=kCustom, calls=%fused_computation | custom fusion | bytes 3840 | tf_op jit(solution)/shard_map/scatter | solution.py:123
  41.5 28.1 %fusion.4 = f32[192,32,32]{2,1,0:T(8,128)} fusion(f32[192,128]{1,0:T(8,128)S(1)} %bitcast.147, f32[192,128]{1,0:T(8,128)S(1)} %get-tuple-element.18, f32[32]{0:T(128)S(1)} %add_multiply_fusion, f32[192,128]{1,0:T(8,128)S(1)} %bitcast.143, f32[192,128]{1,0:T(8,128)S(1)} %get-tuple-element.17), kind=kOutput, calls=%fused_computation.13 | convolution fusion | flops 305922048 | bytes 1179776 | tf_op jit(solution)/shard_map/nki,nkj->nij/dot_general | solution.py:21
  69.6 27.0 %fusion.5 = f32[192,32,32]{2,1,0:T(8,128)S(1)} fusion(f32[192,128]{1,0:T(8,128)S(1)} %bitcast.148, f32[192,128]{1,0:T(8,128)S(1)} %get-tuple-element.18, f32[32]{0:T(128)S(1)} %add_multiply_fusion, f32[192,128]{1,0:T(8,128)S(1)} %bitcast.144, f32[192,128]{1,0:T(8,128)S(1)} %get-tuple-element.17), kind=kOutput, calls=%fused_computation.14 | convolution fusion | flops 305922048 | bytes 1179776 | tf_op jit(solution)/shard_map/nki,nkj->nij/dot_general | solution.py:21
  96.6 28.3 %fusion.56 = f32[192,32,32]{2,1,0:T(8,128)} fusion(f32[192,32,32]{2,1,0:T(8,128)S(1)} %fusion.5, f32[192,128]{1,0:T(8,128)S(1)} %bitcast.149, f32[192,128]{1,0:T(8,128)S(1)} %get-tuple-element.18, f32[32]{0:T(128)S(1)} %add_multiply_fusion, f32[192,128]{1,0:T(8,128)S(1)} %bitcast.145, f32[192,128]{1,0:T(8,128)S(1)} %get-tuple-element.17), kind=kOutput, calls=%fused_computation.58 | convolution fusion | flops 306118656 | bytes 1966208 | tf_op jit(solution)/shard_map/nki,nkj->nij/dot_general | solution.py:21
  130.5 28.3 %fusion.59 = f32[192,32,32]{2,1,0:T(8,128)} fusion(f32[192,32,32]{2,1,0:T(8,128)S(1)} %copy-done.7, f32[192,128]{1,0:T(8,128)S(1)} %bitcast.150, f32[192,128]{1,0:T(8,128)S(1)} %get-tuple-element.18, f32[32]{0:T(128)S(1)} %add_multiply_fusion, f32[192,128]{1,0:T(8,128)S(1)} %bitcast.146, f32[192,128]{1,0:T(8,128)S(1)} %get-tuple-element.17), kind=kOutput, calls=%fused_computation.59 | convolution fusion | flops 306118656 | bytes 1966208 | tf_op jit(solution)/shard_map/nki,nkj->nij/dot_general | solution.py:21
  176.1 34.3 %scatter_fusion.1 = f32[16,36,2048]{2,0,1:T(8,128)} fusion(f32[16,36,2048]{2,0,1:T(8,128)} %broadcast_in_dim.19, s32[192]{0:T(256)S(1)} %bitcast.128, f32[192,2048]{1,0:T(8,128)S(1)} %copy-done.6), kind=kCustom, calls=%fused_computation.1 | custom fusion | bytes 4720128 | tf_op jit(solution)/shard_map/scatter | solution.py:121
  210.4 7.5 copy.145
  224.0 114.7 %all-to-all-done.1 = f32[16,36,2048]{2,1,0:T(8,128)} async-done(((f32[16,36,2048]{2,1,0:T(8,128)}), f32[16,36,2048]{2,1,0:T(8,128)}, u32[]{:S(2)}, u32[]{:S(2)}) %all-to-all-start.1) | async-done | bytes 4718624 | tf_op jit(solution)/shard_map/all_to_all | solution.py:125
  344.0 18.6 %scatter_custom_fusion.2 = f32[1024,2048]{1,0:T(8,128)} fusion(s32[576]{0:T(1024)S(1)} %fusion.158, f32[576,2048]{1,0:T(8,128)} %reshape.253, f32[]{:T(128)} %constant.88.clone.1), kind=kCustom, calls=%fused_computation.23 | custom fusion | flops 1179648 | bytes 8389120 | tf_op jit(solution)/shard_map/scatter-add | solution.py:131
  362.5 9.7 %copy.146 = f32[1024,2048]{0,1:T(8,128)} copy(f32[1024,2048]{1,0:T(8,128)} %scatter_custom_fusion.2) | data formatting | bytes 16777216 | tf_op jit(solution)/shard_map/scatter-add | solution.py:131
  381.5 10.5 %copy.147 = f32[1,8,32,128,32]{4,3,2,1,0:T(8,128)} copy(f32[1,8,32,128,32]{3,1,4,2,0:T(8,128)} %get-tuple-element.12) | data formatting | bytes 8388608 | tf_op jit(solution)/shard_map/slice | solution.py:135
  392.0 12.0 %reshape_squeeze.12 = f32[256,32,128]{2,1,0:T(8,128)} reshape(f32[1,8,32,128,32]{4,3,2,1,0:T(8,128)} %copy.147) | data formatting | bytes 8388608 | tf_op jit(solution)/shard_map/reshape;squeeze | solution.py:72
  404.0 8.0 %fusion.132 = f32[32,256,128]{2,0,1:T(8,128)} fusion(f32[256,32,128]{2,1,0:T(8,128)} %reshape_squeeze.12), kind=kOutput, calls=%fused_computation.145 | convolution fusion | flops 402668544 | bytes 8388608 | tf_op jit(solution)/shard_map/rqn,qk->rkn/dot_general | solution.py:21
  417.1 10.5 %copy.148 = f32[1,8,32,128,32]{4,3,2,1,0:T(8,128)} copy(f32[1,8,32,128,32]{3,1,4,2,0:T(8,128)} %get-tuple-element.11) | data formatting | bytes 8388608 | tf_op jit(solution)/shard_map/slice | solution.py:135
  427.6 12.1 %reshape_squeeze.13 = f32[256,32,128]{2,1,0:T(8,128)} reshape(f32[1,8,32,128,32]{4,3,2,1,0:T(8,128)} %copy.148) | data formatting | bytes 8388608 | tf_op jit(solution)/shard_map/reshape;squeeze | solution.py:73
  439.7 7.9 %convolution_add_fusion = f32[32,256,128]{2,0,1:T(8,128)S(1)} fusion(f32[32,256,128]{2,0,1:T(8,128)} %fusion.132, f32[256,32,128]{2,1,0:T(8,128)} %reshape_squeeze.13), kind=kOutput, calls=%fused_computation.55 | convolution fusion | flops 403717120 | bytes 12582912 | tf_op jit(solution)/shard_map/rqn,qk->rkn/dot_general | solution.py:21
  452.8 6.4 fusion.26
  465.5 6.6 subtract_bitcast_fusion
  483.9 23.4 %copy.155 = f32[2,256,4096]{1,0,2:T(2,128)} copy(f32[2,256,4096]{1,2,0:T(8,128)S(1)} %pad_maximum_fusion) | data formatting | bytes 16777216 | tf_op jit(solution)/shard_map/stack | solution.py:137
  512.4 182.2 %all-to-all-done.2 = f32[2,256,4096]{1,0,2:T(2,128)} async-done(((f32[2,256,4096]{1,0,2:T(2,128)}), f32[2,256,4096]{1,0,2:T(2,128)}, u32[]{:S(2)}, u32[]{:S(2)}) %all-to-all-start.2) | async-done | bytes 8388640 | tf_op jit(solution)/shard_map/all_to_all | solution.py:136
  707.9 10.1 %fusion.18 = f32[32,128,256]{2,0,1:T(8,128)} fusion(f32[32,128,256]{2,1,0:T(8,128)} %bitcast.131), kind=kOutput, calls=%fused_computation.33 | convolution fusion | flops 402668544 | bytes 8388608 | tf_op jit(solution)/shard_map/qnc,qk->knc/dot_general | solution.py:21
  718.0 7.0 fusion.20
  730.7 10.0 %fusion.44 = f32[32,128,256]{2,0,1:T(8,128)S(1)} fusion(f32[32,128,256]{2,0,1:T(8,128)} %fusion.20, f32[32,128,256]{2,1,0:T(8,128)} %bitcast.129), kind=kOutput, calls=%fused_computation.51 | convolution fusion | flops 403717120 | bytes 12582912 | tf_op jit(solution)/shard_map/qnc,qk->knc/dot_general | solution.py:21
  740.7 7.8 %multiply_subtract_fusion = (f32[32,128,256]{2,0,1:T(8,128)S(1)}, f32[32,128,256]{2,0,1:T(8,128)S(1)}) fusion(f32[32,128,256]{2,0,1:T(8,128)S(1)} %fusion.44, f32[32,128]{0,1:T(8,128)S(1)} %copy.164, f32[32,128]{0,1:T(8,128)S(1)} %copy.161, f32[32,128,256]{2,0,1:T(8,128)S(1)} %copy-done.5, f32[32,128,256]{2,1,0:T(8,128)S(1)} %bitcast.130), kind=kOutput, calls=%fused_computation.18 | convolution fusion | flops 410008576 | bytes 21004288 | tf_op jit(solution)/shard_map/qnc,qk->knc/dot_general | solution.py:21
  (78 shorter events, 143.5 us)
Async XLA Ops:
  31.8 186.0 %all-to-all-start = ((f32[16,1,36]{2,1,0:T(1,128)}), f32[16,1,36]{2,1,0:T(1,128)S(1)}, u32[]{:S(2)}, u32[]{:S(2)}) async-start(f32[16,1,36]{2,1,0:T(1,128)} %bitcast.7), calls=%async_computation | async-start | bytes 16384 | tf_op jit(solution)/shard_map/all_to_all | solution.py:126
  128.3 2.2 copy-start.7
  173.4 2.7 copy-start.6
  217.8 120.9 %all-to-all-start.1 = ((f32[16,36,2048]{2,1,0:T(8,128)}), f32[16,36,2048]{2,1,0:T(8,128)}, u32[]{:S(2)}, u32[]{:S(2)}) async-start(f32[16,36,2048]{2,1,0:T(8,128)} %copy.145), calls=%async_computation.1 | async-start | bytes 10485760 | tf_op jit(solution)/shard_map/all_to_all | solution.py:125
  404.0 8.0 %copy-start.2 = (f32[256,32,128]{2,1,0:T(8,128)S(1)}, f32[256,32,128]{2,1,0:T(8,128)}, u32[]{:S(2)}) copy-start(f32[256,32,128]{2,1,0:T(8,128)} %reshape_squeeze.12) | copy-start | bytes 12582916
  439.7 8.0 %copy-start = (f32[256,32,128]{2,1,0:T(8,128)S(1)}, f32[256,32,128]{2,1,0:T(8,128)}, u32[]{:S(2)}) copy-start(f32[256,32,128]{2,1,0:T(8,128)} %reshape_squeeze.13) | copy-start | bytes 12582916
  439.7 8.0 %copy-start.4 = (f32[32,256,128]{2,0,1:T(8,128)S(1)}, f32[32,256,128]{2,0,1:T(8,128)}, u32[]{:S(2)}) copy-start(f32[32,256,128]{2,0,1:T(8,128)} %fusion.143) | copy-start | bytes 12582916
  507.3 187.3 %all-to-all-start.2 = ((f32[2,256,4096]{1,0,2:T(2,128)}), f32[2,256,4096]{1,0,2:T(2,128)}, u32[]{:S(2)}, u32[]{:S(2)}) async-start(f32[2,256,4096]{1,0,2:T(2,128)} %copy.155), calls=%async_computation.2 | async-start | bytes 16777216 | tf_op jit(solution)/shard_map/all_to_all | solution.py:136
  707.9 10.1 %copy-start.3 = (f32[1,16,256,256]{3,2,1,0:T(8,128)S(1)}, f32[1,16,256,256]{3,2,1,0:T(8,128)}, u32[]{:S(2)}) copy-start(f32[1,16,256,256]{3,2,1,0:T(8,128)} %copy.159) | copy-start | bytes 12582916
  730.7 10.0 %copy-start.1 = (f32[1,16,256,256]{3,2,1,0:T(8,128)S(1)}, f32[1,16,256,256]{3,2,1,0:T(8,128)}, u32[]{:S(2)}) copy-start(f32[1,16,256,256]{3,2,1,0:T(8,128)} %copy.157) | copy-start | bytes 12582916
  730.7 10.0 %copy-start.5 = (f32[32,128,256]{2,0,1:T(8,128)S(1)}, f32[32,128,256]{2,0,1:T(8,128)}, u32[]{:S(2)}) copy-start(f32[32,128,256]{2,0,1:T(8,128)} %fusion.18) | copy-start | bytes 12582916
where the time goes:
time: 791 us; the launch traced here: 783 us
  waiting for transfers between devices  297 us (38%)
  matrix products  234 us (30%)
  local copies, waits for them, and re-layouts  204 us (26%)
  other arithmetic  29 us (4%)
  starting transfers between devices  17.3 us (2%)
    dot_general x28, matrix products, single(): return jnp.einsum(pattern, first, second, precision=highest)  234 us
    all_to_all x1, waiting for transfers between devices, per_device(): lax.all_to_all(jnp.stack([row_real, row_imag]), 'wide', split_axis=2, con...  182 us
    all_to_all x1, waiting for transfers between devices, per_device(): lax.all_to_all(packed, 'wide', split_axis=0, concat_axis=0, tiled=True)  115 us
    scatter x2, local copies, waits for them, and re-layouts, per_device(): packed = jnp.zeros((owners, capacity, spectrum_size), jnp.float32).at[own...  41.7 us
    scatter x1, local copies, waits for them, and re-layouts, per_device(): jnp.zeros((owners, capacity), jnp.float32).at[owner, slot_of].set(tile_ids)  27.5 us
    slice x3, local copies, waits for them, and re-layouts, per_device(): row_real, row_imag = transform_last(grid_band[0], grid_band[1])  24.8 us
    another operation x1, local copies, waits for them, and re-layouts, per_device(): jnp.stack([row_real, row_imag])  23.4 us
    scatter-add x1, other arithmetic, per_device(): jnp.zeros((band_tiles * tile_cols, spectrum_size), jnp.float32)  18.6 us
  transfers between devices with their start and end apart: 3, of which 2 were waited for; matrix products, arithmetic and copies ran while one was open for 23% of the time, Pallas kernels for 0%

commit v1 on v0

v1 whole, which is shorter than its diff:
```python
import functools
import math

import jax
import jax.numpy as jnp
import ml_dtypes
import numpy as np
from jax import lax
from jax.experimental import pallas as pl
from jax.experimental.pallas import tpu as pltpu
from jax.sharding import PartitionSpec as P

SUB = 32
GRID = 4096
LANES = 128
FB = GRID // LANES
BATCH = 8
CORES = 2

BF16 = jnp.bfloat16
F32 = jnp.float32


def split_np(table):
    table = table.astype(np.float32)
    high = table.astype(ml_dtypes.bfloat16)
    low = (table - high.astype(np.float32)).astype(ml_dtypes.bfloat16)
    return high, low


def embed(phase):
    angle = -2.0 * np.pi * (phase % GRID) / GRID
    real, imag = np.cos(angle), np.sin(angle)
    top = np.concatenate([real, -imag], axis=-1)
    bottom = np.concatenate([imag, real], axis=-1)
    return split_np(np.concatenate([top, bottom], axis=-2))


@functools.cache
def row_table():
    q = np.arange(FB)[:, None, None]
    m = np.arange(LANES)[None, :, None]
    t = np.arange(LANES)[None, None, :]
    return embed(m * (FB * t + q))


@functools.cache
def column_table():
    first = np.arange(FB)[:, None, None]
    outer = np.arange(LANES)[None, :, None]
    inner = np.arange(LANES)[None, None, :]
    return embed(inner * (first + FB * outer))


def even_fit(function, reach, degree):
    nodes = np.cos(np.pi * (np.arange(200) + 0.5) / 200)
    points = (nodes + 1.0) / 2.0 * reach * reach
    cheb = np.polynomial.chebyshev.Chebyshev.fit(
        points, function(np.sqrt(points)), degree, domain=[0.0, reach * reach]
    )
    return [float(c) for c in cheb.convert(kind=np.polynomial.Polynomial).coef]


SIN_FIT = even_fit(lambda x: np.sin(np.pi * x) / x, 0.5, 6)
COS_FIT = even_fit(lambda x: np.cos(np.pi * x), 0.5, 7)
PEAK_FIT = even_fit(lambda x: np.sin(np.pi * x) / np.tan(np.pi * x / SUB), 0.5, 6)


def horner(coefs, x):
    total = jnp.full_like(x, coefs[-1])
    for coef in coefs[-2::-1]:
        total = total * x + coef
    return total


def cot_table():
    grid = np.arange(SUB, dtype=np.float64)
    grid[0] = 1.0
    values = 1.0 / np.tan(np.pi * grid / SUB)
    values[0] = 1e30
    return np.tile(values.astype(np.float32)[:, None], (1, LANES))


def turn(value, k, n):
    real, imag = value
    k = k % n
    if k == 0:
        return value
    if 4 * k == n:
        return (imag, -real)
    if 2 * k == n:
        return (-real, -imag)
    if 8 * k == n:
        root = math.sqrt(0.5)
        return ((real + imag) * root, (imag - real) * root)
    if 8 * k == 3 * n:
        root = math.sqrt(0.5)
        return ((imag - real) * root, (real + imag) * -root)
    cos, sin = math.cos(2.0 * math.pi * k / n), -math.sin(2.0 * math.pi * k / n)
    return (real * cos - imag * sin, real * sin + imag * cos)


def fft_list(values):
    n = len(values)
    if n == 1:
        return values
    even, odd = fft_list(values[0::2]), fft_list(values[1::2])
    first, second = [], []
    for k in range(n // 2):
        turned = turn(odd[k], k, n)
        first.append((even[k][0] + turned[0], even[k][1] + turned[1]))
        second.append((even[k][0] - turned[0], even[k][1] - turned[1]))
    return first + second


def split(x):
    high = x.astype(BF16)
    return high, (x - high.astype(F32)).astype(BF16)


def dot(a, b):
    return lax.dot_general(a, b, (((1,), (0,)), ((), ())), preferred_element_type=F32)


def dot_nt(a, b):
    return lax.dot_general(a, b, (((1,), (1,)), ((), ())), preferred_element_type=F32)


def spectra_rows_kernel(
    blocks, outputs, bits, scale, info, order, coefs, *refs
):
    raws = refs[:blocks]
    cot_ref, high_hbm, low_hbm = refs[blocks : blocks + 3]
    outs = refs[blocks + 3 : blocks + 3 + CORES]
    raw, high, low, grid, sums, rows, prep, raw_sem, tab_sem = refs[blocks + 3 + CORES :]
    step = pl.program_id(0)
    per_block = raws[0].shape[0]
    raw_copies = [
        pltpu.make_async_copy(raws[i], raw.at[pl.ds(i * per_block, per_block)], raw_sem.at[i])
        for i in range(blocks)
    ]
    tab_copies = [
        pltpu.make_async_copy(high_hbm, high, tab_sem.at[0]),
        pltpu.make_async_copy(low_hbm, low, tab_sem.at[1]),
    ]

    @pl.when(step == 0)
    def _():
        for copy in raw_copies:
            copy.start()
        for copy in tab_copies:
            copy.start()

        def clear(i, _):
            grid[:, :, pl.ds(i * 128, 128), :] = jnp.zeros((2, 2, 128, LANES), F32)
            return 0

        lax.fori_loop(0, GRID // 128, clear, 0)
        for copy in raw_copies:
            copy.wait()

    me = info[0]
    start, end = info[1 + step], info[2 + step]
    last = order.shape[0] - 1
    cell = lax.broadcasted_iota(jnp.int32, (SUB, LANES), 0).astype(F32)
    lane_part = lax.broadcasted_iota(jnp.int32, (SUB, LANES), 1) // SUB
    sub_row = lax.broadcasted_iota(jnp.int32, (BATCH, LANES), 0)

    def batch(b, _):
        base = start + b * BATCH
        words = [order[jnp.minimum(base + j, last)] for j in range(BATCH)]
        for j in range(BATCH):
            item = words[j] & ((1 << bits) - 1)
            rows[4 * j : 4 * j + 4, :] = raw[pl.ds(4 * item, 4), :]
        factor = jnp.where(sub_row + base < end, scale, 0.0)
        re = rows[pl.ds(0, BATCH, stride=4), :] * factor
        im = rows[pl.ds(1, BATCH, stride=4), :] * factor
        for axis in range(2):
            u = rows[pl.ds(2 + axis, BATCH, stride=4), :]
            near = jnp.floor(u + 0.5)
            off = u - near
            sign = 1.0 - 2.0 * (near - 2.0 * jnp.floor(near * 0.5))
            wide = (u - SUB // 2) * (1.0 / SUB)
            wide2, off2 = wide * wide, off * off
            cot = -(wide * horner(SIN_FIT, wide2)) / horner(COS_FIT, wide2)
            sine = sign * (off * horner(SIN_FIT, off2))
            at = 8 * axis
            prep[at + 0] = cot
            prep[at + 1] = sine * cot
            prep[at + 2] = sine * (1.0 + cot * cot)
            prep[at + 3] = sign * horner(PEAK_FIT, off2)
            prep[at + 4] = near
            prep[at + 5] = sine
            if axis == 0:
                prep[6] = im * sine
                prep[7] = re * sine
        prep[14] = re
        prep[15] = im

        def table(axis, j):
            at = 8 * axis
            cot, alpha, beta, peak, near = [prep[at + i, j : j + 1, :] for i in range(5)]
            gap = cot_ref[...] - cot
            inv = pl.reciprocal(gap, approx=True)
            inv = inv * (2.0 - gap * inv)
            return jnp.where(cell == near, peak, alpha + beta * inv)

        found = []
        for j in range(BATCH):
            table_u, table_v = table(0, j), table(1, j)
            re_j, im_j = prep[14, j : j + 1, :], prep[15, j : j + 1, :]
            b_re = re_j * table_u + prep[6, j : j + 1, :]
            b_im = im_j * table_u - prep[7, j : j + 1, :]
            sine = jnp.broadcast_to(prep[13, j : j + 1, :], (16, LANES))
            a_high, a_low = split(jnp.concatenate([table_v, sine], axis=0))
            b_high, b_low = split(jnp.concatenate([b_re, b_im, b_im, -b_re], axis=0))
            product = dot_nt(
                jnp.concatenate([a_high, a_low, a_high], axis=1),
                jnp.concatenate([b_high, b_high, b_low], axis=1),
            )
            extra = pltpu.roll(product[SUB : SUB + 8], 64, 1)
            found.append(product[:SUB] + jnp.concatenate([extra] * (SUB // 8), axis=0))
        for j in range(BATCH):
            word = words[j]
            tile = (word >> bits) & (LANES - 1)
            part = (word >> (bits + 7)) & 3
            half = (word >> (bits + 9)) & 1
            mask = lane_part == part
            spot = pl.ds(pl.multiple_of(tile * SUB, SUB), SUB)
            grid[0, half, spot, :] += jnp.where(mask, pltpu.roll(found[j], part * SUB, 1), 0.0)
            moved = pltpu.roll(found[j], (part * SUB + 96) & 127, 1)
            grid[1, half, spot, :] += jnp.where(mask, moved, 0.0)
        return 0

    lax.fori_loop(0, (end - start + BATCH - 1) // BATCH, batch, 0)

    @pl.when(step == 0)
    def _():
        for copy in tab_copies:
            copy.wait()

    fine = FB // outputs
    zero = jnp.zeros((LANES, LANES), F32)
    sums[...] = jnp.zeros(sums.shape, F32)

    def transform(q0, _):
        parts = []
        for q1 in range(outputs):
            q = q0 + fine * q1
            at = pl.ds(q, LANES, stride=SUB)
            x = jnp.concatenate(
                [
                    jnp.concatenate([grid[c, 0, at, :], grid[c, 1, at, :]], axis=1)
                    for c in range(2)
                ],
                axis=0,
            )
            for c in range(2):
                for half in range(2):
                    grid[c, half, at, :] = zero
            x_high, x_low = split(x)
            f_high = high[q]
            y = dot(f_high, x_high) + dot(low[q], x_high) + dot(f_high, x_low)
            parts.append((y[:LANES], y[LANES:]))
        for j, (real, imag) in enumerate(fft_list(parts)):
            cos, sin = coefs[0, q0 * outputs + j], coefs[1, q0 * outputs + j]
            sums[j, 0] += real * cos - imag * sin
            sums[j, 1] += real * sin + imag * cos
        return 0

    lax.fori_loop(0, fine, transform, 0)
    share = outputs // CORES
    for slot in range(CORES):
        dest = (me + slot) % CORES
        for k in range(share):
            for c in range(2):
                for half in range(2):
                    outs[slot][half, c, k * LANES : (k + 1) * LANES, :] = sums[
                        dest * share + k, c, :, half * LANES : (half + 1) * LANES
                    ]


def spectra_rows(raws, info, order, coefs, columns, bits, scale):
    blocks = len(raws)
    outputs = CORES * columns // LANES
    per_device = FB // CORES
    steps = per_device // 2
    high, low = row_table()
    block = pl.BlockSpec((2, 2, columns, LANES), lambda i, *_: (i, 0, 0, 0))
    anywhere = pl.BlockSpec(memory_space=pl.ANY)
    raw_rows = blocks * raws[0].shape[0]
    return pl.pallas_call(
        functools.partial(spectra_rows_kernel, blocks, outputs, bits, scale),
        grid_spec=pltpu.PrefetchScalarGridSpec(
            num_scalar_prefetch=3,
            grid=(steps,),
            in_specs=[anywhere] * blocks
            + [pl.BlockSpec((SUB, LANES), lambda i, *_: (0, 0)), anywhere, anywhere],
            out_specs=[block] * CORES,
            scratch_shapes=[
                pltpu.VMEM((raw_rows, LANES), F32),
                pltpu.VMEM(high.shape, BF16),
                pltpu.VMEM(low.shape, BF16),
                pltpu.VMEM((2, 2, GRID, LANES), F32),
                pltpu.VMEM((outputs, 2, LANES, 2 * LANES), F32),
                pltpu.VMEM((4 * BATCH, LANES), F32),
                pltpu.VMEM((16, BATCH, LANES), F32),
                pltpu.SemaphoreType.DMA((blocks,)),
                pltpu.SemaphoreType.DMA((2,)),
            ],
        ),
        out_shape=[jax.ShapeDtypeStruct((per_device, 2, columns, LANES), F32)] * CORES,
        compiler_params=pltpu.CompilerParams(
            dimension_semantics=("arbitrary",), vmem_limit_bytes=56 * 1024 * 1024
        ),
        name="spectra_rows",
    )(info, order, coefs, *raws, jnp.asarray(cot_table()), jnp.asarray(high), jnp.asarray(low))


def columns_kernel(info, *refs):
    pieces = refs[:CORES]
    high_hbm, low_hbm, out, x, high, low, piece_sem, tab_sem = refs[CORES:]
    me = info[0]
    per_device, _, columns, _ = pieces[0].shape
    copies = [
        pltpu.make_async_copy(
            pieces[slot],
            x.at[pl.ds(((me + CORES - slot) % CORES) * per_device, per_device)],
            piece_sem.at[slot],
        )
        for slot in range(CORES)
    ]
    tab_copies = [
        pltpu.make_async_copy(high_hbm, high, tab_sem.at[0]),
        pltpu.make_async_copy(low_hbm, low, tab_sem.at[1]),
    ]
    for copy in copies + tab_copies:
        copy.start()
    for copy in copies:
        copy.wait()

    def butterflies(i, _):
        at = pl.ds(pl.multiple_of(i * 8, 8), 8)
        values = []
        for r in range(FB):
            slot = (r % CORES) * per_device + r // CORES
            values.append((x[slot, 0, at, :], x[slot, 1, at, :]))
        for r, (real, imag) in enumerate(fft_list(values)):
            x[r, 0, at, :] = real
            x[r, 1, at, :] = imag
        return 0

    lax.fori_loop(0, columns // 8, butterflies, 0)
    for copy in tab_copies:
        copy.wait()

    def transform(r, _):
        z_high, z_low = split(jnp.concatenate([x[r, 0], x[r, 1]], axis=1))
        f_high = high[r]
        y = dot_nt(f_high, z_high) + dot_nt(low[r], z_high) + dot_nt(f_high, z_low)
        at = pl.ds(r, LANES, stride=FB)
        for part in range(0, columns, LANES):
            out[0, part // LANES, at, :] = y[:LANES, part : part + LANES]
            out[1, part // LANES, at, :] = y[LANES:, part : part + LANES]
        return 0

    lax.fori_loop(0, FB, transform, 0)


def column_transform(pieces, info, columns):
    high, low = column_table()
    anywhere = pl.BlockSpec(memory_space=pl.ANY)

    def kernel(info, *refs):
        inputs, out_hbm = refs[: CORES + 2], refs[CORES + 2]
        out, x, high, low, piece_sem, tab_sem, out_sem = refs[CORES + 3 :]
        columns_kernel(info, *inputs, out, x, high, low, piece_sem, tab_sem)
        copies = [
            pltpu.make_async_copy(
                out.at[:, k], out_hbm.at[:, :, pl.ds(k * LANES, LANES)], out_sem.at[k]
            )
            for k in range(columns // LANES)
        ]
        for copy in copies:
            copy.start()
        for copy in copies:
            copy.wait()

    return pl.pallas_call(
        kernel,
        grid_spec=pltpu.PrefetchScalarGridSpec(
            num_scalar_prefetch=1,
            grid=(1,),
            in_specs=[anywhere] * (CORES + 2),
            out_specs=anywhere,
            scratch_shapes=[
                pltpu.VMEM((2, columns // LANES, GRID, LANES), F32),
                pltpu.VMEM((FB, 2, columns, LANES), F32),
                pltpu.VMEM(high.shape, BF16),
                pltpu.VMEM(low.shape, BF16),
                pltpu.SemaphoreType.DMA((CORES,)),
                pltpu.SemaphoreType.DMA((2,)),
                pltpu.SemaphoreType.DMA((columns // LANES,)),
            ],
        ),
        out_shape=jax.ShapeDtypeStruct((2, GRID, columns), F32),
        compiler_params=pltpu.CompilerParams(vmem_limit_bytes=56 * 1024 * 1024),
        name="column_transform",
    )(info, *pieces, jnp.asarray(high), jnp.asarray(low))


def chip_cycle(chips):
    return list(range(0, chips, 2)) + list(range(chips - 1, 0, -2))[: chips // 2]


def gather_blocks(block, size):
    chips = size // CORES
    cycle = chip_cycle(chips)
    ahead, back = [], []
    for at in range(chips):
        here, there = cycle[at], cycle[(at + 1) % chips]
        for core in range(CORES):
            ahead.append((CORES * here + core, CORES * there + core))
            back.append((CORES * there + core, CORES * here + core))
    swap = [(i, i ^ 1) for i in range(size)]
    found = {0: block}
    forth = other = block
    for k in range(1, chips // 2 + 1):
        forth = lax.ppermute(forth, "wide", ahead)
        found[k] = forth
        if 2 * k < chips:
            other = lax.ppermute(other, "wide", back)
            found[chips - k] = other
    own = jnp.concatenate([found[k] for k in range(chips)], axis=0)
    return [own, lax.ppermute(own, "wide", swap)]


def per_device(visibilities, offsets, vis_count, owner, tile_row, tile_col):
    size = lax.axis_size("wide")
    count, _, slots = visibilities.shape
    chips = size // CORES
    columns = GRID // size
    outputs = CORES * columns // LANES
    band_tiles = GRID // (SUB * size)
    place = lax.axis_index("wide")
    core, chip = place % CORES, place // CORES
    total = size * count
    bits = max(1, (total - 1).bit_length())

    live = (jnp.arange(slots)[None, :] < vis_count[:, None])[:, None, :]
    block = jnp.concatenate([jnp.where(live, visibilities, 0.0), offsets], axis=1)
    gathered = gather_blocks(block.reshape(count * 4, slots), size)

    row = owner * band_tiles + tile_row
    group, part = row // 4, row % 4
    key = (group % CORES) * (FB // CORES) + group // CORES
    word = (((key * 4 + part) * LANES + tile_col) << bits).astype(jnp.int32)
    words = lax.all_gather(word, "wide", axis=0, tiled=True)
    cycle = chip_cycle(chips)
    spot = np.zeros(chips, np.int32)
    spot[cycle] = np.arange(chips, dtype=np.int32)
    source = np.arange(size)
    distance = (jnp.asarray(spot)[chip] - spot[source // CORES]) % chips
    slot = ((source + core) % CORES) * chips + distance
    data_at = (slot[:, None] * count + jnp.arange(count)[None, :]).reshape(-1)
    order = lax.sort(words + data_at.astype(jnp.int32), is_stable=False)
    steps = FB // CORES // 2
    shift = bits + 7 + 2 + 1
    bounds = core * steps + jnp.arange(steps + 1)
    starts = jnp.sum((words[None, :] >> shift) < bounds[:, None], axis=1)
    info = jnp.concatenate([core[None], starts]).astype(jnp.int32)

    fine = FB // outputs
    phase = (
        jnp.arange(fine)[:, None] * (outputs * chip + jnp.arange(outputs)[None, :]) % FB
    ).astype(F32) * (-2.0 * math.pi / FB)
    coefs = jnp.stack([jnp.cos(phase).reshape(-1), jnp.sin(phase).reshape(-1)])

    scale = 1.0 / (math.sqrt(slots) * SUB * GRID)
    pieces = spectra_rows(gathered, info, order, coefs, columns, bits, scale)
    swap = [(i, i ^ 1) for i in range(size)]
    received = [pieces[0], lax.ppermute(pieces[1], "wide", swap)]
    return column_transform(received, info, columns)


def solution(mesh):
    placed = (
        P(("group", "wide"), None, None),
        P(("group", "wide"), None, None),
        P(("group", "wide")),
        P(("group", "wide")),
        P(("group", "wide")),
        P(("group", "wide")),
    )
    return jax.shard_map(
        per_device, mesh=mesh, in_specs=placed, out_specs=P(None, "group", "wide"), check_vma=False
    )
```

time: 791 us -> 423 us (0.53)
  the two profiles are of different devices: /device:TPU:13 before, /device:TPU:0 now
where the time goes in v1:
time: 423 us; the launch traced here: 419 us
  Pallas kernels  294 us (70%)
  blocking collectives  60.7 us (14%)
  waiting for transfers between devices  39.1 us (9%)
  other arithmetic  10.7 us (3%)
  starting transfers between devices  9.35 us (2%)
    pallas_call x1, Pallas kernels, spectra_rows(): pl.pallas_call(functools.partial(spectra_rows_kernel, blocks, outputs, bi...  263 us
    unnamed x1, blocking collectives  60.7 us
    pallas_call x1, Pallas kernels, column_transform(): pl.pallas_call(kernel, grid_spec=pltpu.PrefetchScalarGridSpec(num_scalar_...  31.1 us
    ppermute x4, waiting for transfers between devices, gather_blocks(): forth = lax.ppermute(forth, 'wide', ahead)  30.9 us
  transfers between devices with their start and end apart: 9, of which 6 were waited for; matrix products, arithmetic and copies ran while one was open for 2% of the time, Pallas kernels for 0%

profile of v1, /device:TPU:0, one launch (start us, length us, event | category | flops | bytes accessed | tf_op | source)
XLA Modules:
  0.0 418.9 jit_solution(7414456148767106583)
XLA Ops:
  0.0 0.8 iota_compare_fusion
  0.8 1.1 broadcast_select_fusion
  1.8 1.1 pad_maximum_fusion
  3.0 3.1 collective-permute-start
  6.1 9.1 %collective-permute-done = f32[768,128]{1,0:T(8,128)S(1)} collective-permute-done((f32[768,128]{1,0:T(8,128)S(1)}, f32[768,128]{1,0:T(8,128)S(1)}, u32[]{:S(2)}, u32[]{:S(2)}) %collective-permute-start) | collective-permute-done | bytes 393248 | tf_op jit(solution)/shard_map/ppermute | solution.py:429
  15.2 1.8 collective-permute-start.1
  17.2 8.3 %collective-permute-done.1 = f32[768,128]{1,0:T(8,128)S(1)} collective-permute-done((f32[768,128]{1,0:T(8,128)S(1)}, f32[768,128]{1,0:T(8,128)S(1)}, u32[]{:S(2)}, u32[]{:S(2)}) %collective-permute-start.1) | collective-permute-done | bytes 393248 | tf_op jit(solution)/shard_map/ppermute | solution.py:429
  25.5 1.5 collective-permute-start.2
  27.0 0.5 collective-permute-start.5
  27.5 7.3 %collective-permute-done.2 = f32[768,128]{1,0:T(8,128)S(1)} collective-permute-done((f32[768,128]{1,0:T(8,128)S(1)}, f32[768,128]{1,0:T(8,128)S(1)}, u32[]{:S(2)}, u32[]{:S(2)}) %collective-permute-start.2) | collective-permute-done | bytes 393248 | tf_op jit(solution)/shard_map/ppermute | solution.py:429
  34.8 1.4 collective-permute-start.3
  36.3 0.7 collective-permute-start.6
  37.1 6.2 %collective-permute-done.3 = f32[768,128]{1,0:T(8,128)S(1)} collective-permute-done((f32[768,128]{1,0:T(8,128)S(1)}, f32[768,128]{1,0:T(8,128)S(1)}, u32[]{:S(2)}, u32[]{:S(2)}) %collective-permute-start.3) | collective-permute-done | bytes 393248 | tf_op jit(solution)/shard_map/ppermute | solution.py:429
  43.3 0.8 collective-permute-done.6
  44.6 0.9 dynamic_slice.3
  45.5 0.7 fusion.5
  46.3 0.6 dynamic-slice
  47.7 60.7 %all-reduce = s32[3072]{0:T(1024)S(1)} all-reduce(s32[3072]{0:T(1024)S(1)} %shift-left_dynamic-update-slice_fusion), channel_id=1, replica_groups=mesh['group'=2,'wide'=16] {'wide'}, use_global_device_ids=true, to_apply=%add | all-reduce | flops 3072 | bytes 24576
  108.4 5.5 %sort.7.order = s32[3072]{0:T(1024)} sort(s32[3072]{0:T(1024)S(1)} %get-tuple-element.11), dimensions={0}, to_apply=%region_1.2 | sort | flops 36864 | bytes 24576 | tf_op jit(solution)/shard_map/sort | solution.py:466
  114.2 0.6 pad_add_fusion.info
  115.3 263.1 %spectra_rows.1 = (f32[16,2,256,128]{3,2,1,0:T(8,128)}, f32[16,2,256,128]{3,2,1,0:T(8,128)}) custom-call(s32[10]{0:T(128)} %pad_add_fusion.info, s32[3072]{0:T(1024)} %sort.7.order, f32[2,32]{1,0:T(2,128)} %pad_maximum_fusion.1.coefs, f32[6144,128]{1,0:T(8,128)} %copy-done.1, f32[6144,128]{1,0:T(8,128)} %collective-permute-done.7.refs_1_, ...), custom_call_target="tpu_custom_call" | custom-call | tf_op jit(solution)/shard_map/spectra_rows/pallas_call | solution.py:292
  378.5 7.4 %collective-permute-done.8.refs_1_ = f32[16,2,256,128]{3,2,1,0:T(8,128)S(1)} collective-permute-done((f32[16,2,256,128]{3,2,1,0:T(8,128)}, f32[16,2,256,128]{3,2,1,0:T(8,128)S(1)}, u32[]{:S(2)}, u32[]{:S(2)}) %collective-permute-start.8) | collective-permute-done | bytes 4194336 | tf_op jit(solution)/shard_map/ppermute | solution.py:482
  385.8 2.0 copy-done
  387.8 31.1 %column_transform.1 = f32[2,4096,256]{2,1,0:T(8,128)} custom-call(s32[10]{0:T(128)} %pad_add_fusion.info, f32[16,2,256,128]{3,2,1,0:T(8,128)} %get-tuple-element.7.refs_0_, f32[16,2,256,128]{3,2,1,0:T(8,128)} %copy-done, bf16[32,256,256]{2,1,0:T(8,128)(2,1)} %constant.136.clone.refs_2_, bf16[32,256,256]{2,1,0:T(8,128)(2,1)} %constant.137.clone.refs_3_), custom_call_target="tpu_custom_call" | custom-call | tf_op jit(solution)/shard_map/column_transform/pallas_call | solution.py:389
  (42 shorter events, 1.9 us)
Async XLA Ops:
  3.0 41.6 %copy-start.7 = (s32[8]{0:T(128)S(1)}, s32[8]{0:T(128)}, u32[]{:S(2)}) copy-start(s32[8]{0:T(128)} %constant.131.clone) | copy-start | bytes 100
  3.0 42.5 %copy-start.5 = (s32[16]{0:T(128)S(1)}, s32[16]{0:T(128)}, u32[]{:S(2)}) copy-start(s32[16]{0:T(128)} %constant.138) | copy-start | bytes 196
  3.0 43.3 %copy-start.6 = (u32[32]{0:T(128)S(1)}, u32[32]{0:T(128)}, u32[]{:S(2)}) copy-start(u32[32]{0:T(128)} %constant.141) | copy-start | bytes 388
  3.0 44.5 %copy-start.2 = (s32[192]{0:T(256)S(1)}, s32[192]{0:T(256)}, u32[]{:S(2)}) copy-start(s32[192]{0:T(256)} %param.19) | copy-start | bytes 2308
  3.0 44.5 %copy-start.3 = (s32[192]{0:T(256)S(1)}, s32[192]{0:T(256)}, u32[]{:S(2)}) copy-start(s32[192]{0:T(256)} %param.18) | copy-start | bytes 2308
  3.0 44.5 %copy-start.4 = (s32[192]{0:T(256)S(1)}, s32[192]{0:T(256)}, u32[]{:S(2)}) copy-start(s32[192]{0:T(256)} %param.17) | copy-start | bytes 2308
  3.0 12.1 %collective-permute-start = (f32[768,128]{1,0:T(8,128)S(1)}, f32[768,128]{1,0:T(8,128)S(1)}, u32[]{:S(2)}, u32[]{:S(2)}) collective-permute-start(f32[768,128]{1,0:T(8,128)S(1)} %bitcast.4), channel_id=1, source_target_pairs={{0,4},{1,5},{4,8},{5,9},{8,12},{9,13},{12,14},{13,15},{14,10},{15,... | collective-permute-start | bytes 1179656 | tf_op jit(solution)/shard_map/ppermute | solution.py:429
  15.2 10.3 %collective-permute-start.1 = (f32[768,128]{1,0:T(8,128)S(1)}, f32[768,128]{1,0:T(8,128)S(1)}, u32[]{:S(2)}, u32[]{:S(2)}) collective-permute-start(f32[768,128]{1,0:T(8,128)S(1)} %collective-permute-done), channel_id=1, source_target_pairs={{0,4},{1,5},{4,8},{5,9},{8,12},{9,13},{12,14},{13,15},{14,10},{15,... | collective-permute-start | bytes 1179656 | tf_op jit(solution)/shard_map/ppermute | solution.py:429
  17.0 10.0 %collective-permute-start.4 = (f32[768,128]{1,0:T(8,128)S(1)}, f32[768,128]{1,0:T(8,128)S(1)}, u32[]{:S(2)}, u32[]{:S(2)}) collective-permute-start(f32[768,128]{1,0:T(8,128)S(1)} %bitcast.5), channel_id=1, source_target_pairs={{4,0},{5,1},{8,4},{9,5},{12,8},{13,9},{14,12},{15,13},{10,14},{11,... | collective-permute-start | bytes 1179656 | tf_op jit(solution)/shard_map/ppermute | solution.py:432
  25.5 9.4 %collective-permute-start.2 = (f32[768,128]{1,0:T(8,128)S(1)}, f32[768,128]{1,0:T(8,128)S(1)}, u32[]{:S(2)}, u32[]{:S(2)}) collective-permute-start(f32[768,128]{1,0:T(8,128)S(1)} %collective-permute-done.1), channel_id=1, source_target_pairs={{0,4},{1,5},{4,8},{5,9},{8,12},{9,13},{12,14},{13,15},{14,10},{15,... | collective-permute-start | bytes 1179656 | tf_op jit(solution)/shard_map/ppermute | solution.py:429
  27.0 9.3 %collective-permute-start.5 = (f32[768,128]{1,0:T(8,128)S(1)}, f32[768,128]{1,0:T(8,128)S(1)}, u32[]{:S(2)}, u32[]{:S(2)}) collective-permute-start(f32[768,128]{1,0:T(8,128)S(1)} %collective-permute-done.4), channel_id=1, source_target_pairs={{4,0},{5,1},{8,4},{9,5},{12,8},{13,9},{14,12},{15,13},{10,14},{11,... | collective-permute-start | bytes 1179656 | tf_op jit(solution)/shard_map/ppermute | solution.py:432
  34.8 8.5 %collective-permute-start.3 = (f32[768,128]{1,0:T(8,128)S(1)}, f32[768,128]{1,0:T(8,128)S(1)}, u32[]{:S(2)}, u32[]{:S(2)}) collective-permute-start(f32[768,128]{1,0:T(8,128)S(1)} %collective-permute-done.2), channel_id=1, source_target_pairs={{0,4},{1,5},{4,8},{5,9},{8,12},{9,13},{12,14},{13,15},{14,10},{15,... | collective-permute-start | bytes 1179656 | tf_op jit(solution)/shard_map/ppermute | solution.py:429
  36.3 7.9 %collective-permute-start.6 = (f32[768,128]{1,0:T(8,128)S(1)}, f32[768,128]{1,0:T(8,128)S(1)}, u32[]{:S(2)}, u32[]{:S(2)}) collective-permute-start(f32[768,128]{1,0:T(8,128)S(1)} %collective-permute-done.5), channel_id=1, source_target_pairs={{4,0},{5,1},{8,4},{9,5},{12,8},{13,9},{14,12},{15,13},{10,14},{11,... | collective-permute-start | bytes 1179656 | tf_op jit(solution)/shard_map/ppermute | solution.py:432
  44.3 71.0 %copy-start.1 = (f32[6144,128]{1,0:T(8,128)}, f32[6144,128]{1,0:T(8,128)S(1)}, u32[]{:S(2)}) copy-start(f32[6144,128]{1,0:T(8,128)S(1)} %constant_dynamic-update-slice_fusion.refs_0_) | copy-start | bytes 9437188
  44.3 71.0 %collective-permute-start.7 = (f32[6144,128]{1,0:T(8,128)S(1)}, f32[6144,128]{1,0:T(8,128)}, u32[]{:S(2)}, u32[]{:S(2)}) collective-permute-start(f32[6144,128]{1,0:T(8,128)S(1)} %constant_dynamic-update-slice_fusion.refs_0_), channel_id=1, source_target_pairs={{0,1},{1,0},{2,3},{3,2},{4,5},{5,4},{6,7},{7,6},{8,9},{9,8},{10,11... | collective-permute-start | bytes 9437192 | tf_op jit(solution)/shard_map/ppermute | solution.py:435
  378.4 7.4 %collective-permute-start.8 = (f32[16,2,256,128]{3,2,1,0:T(8,128)}, f32[16,2,256,128]{3,2,1,0:T(8,128)S(1)}, u32[]{:S(2)}, u32[]{:S(2)}) collective-permute-start(f32[16,2,256,128]{3,2,1,0:T(8,128)} %get-tuple-element.8), channel_id=1, source_target_pairs={{0,1},{1,0},{2,3},{3,2},{4,5},{5,4},{6,7},{7,6},{8,9},{9,8},{10,11... | collective-permute-start | bytes 12582920 | tf_op jit(solution)/shard_map/ppermute | solution.py:482
  385.8 2.0 copy-start

commit v2 on v1

--- a/solution.py
+++ b/solution.py
@@ -15,6 +15,7 @@
 LANES = 128
 FB = GRID // LANES
 BATCH = 8
+UNROLL = 4
 CORES = 2
 
 BF16 = jnp.bfloat16
@@ -37,11 +38,12 @@
 
 
 @functools.cache
-def row_table():
-    q = np.arange(FB)[:, None, None]
-    m = np.arange(LANES)[None, :, None]
-    t = np.arange(LANES)[None, None, :]
-    return embed(m * (FB * t + q))
+def row_table(chips):
+    count = LANES // chips
+    first = np.arange(FB)[None, :, None, None]
+    outer = np.arange(LANES).reshape(chips, 1, count, 1)
+    inner = np.arange(LANES)[None, None, None, :]
+    return np.concatenate(embed(inner * (first + FB * outer)), axis=2)
 
 
 @functools.cache
@@ -126,30 +128,25 @@
     return lax.dot_general(a, b, (((1,), (1,)), ((), ())), preferred_element_type=F32)
 
 
-def spectra_rows_kernel(
-    blocks, outputs, bits, scale, info, order, coefs, *refs
-):
+def spectra_rows_kernel(blocks, bits, scale, info, order, *refs):
     raws = refs[:blocks]
-    cot_ref, high_hbm, low_hbm = refs[blocks : blocks + 3]
-    outs = refs[blocks + 3 : blocks + 3 + CORES]
-    raw, high, low, grid, sums, rows, prep, raw_sem, tab_sem = refs[blocks + 3 + CORES :]
+    cot_ref, table_hbm = refs[blocks : blocks + 2]
+    outs = refs[blocks + 2 : blocks + 2 + CORES]
+    raw, table, grid, found, rows, prep, raw_sem, tab_sem = refs[blocks + 2 + CORES :]
     step = pl.program_id(0)
     per_block = raws[0].shape[0]
     raw_copies = [
         pltpu.make_async_copy(raws[i], raw.at[pl.ds(i * per_block, per_block)], raw_sem.at[i])
         for i in range(blocks)
     ]
-    tab_copies = [
-        pltpu.make_async_copy(high_hbm, high, tab_sem.at[0]),
-        pltpu.make_async_copy(low_hbm, low, tab_sem.at[1]),
-    ]
+    me, chip = info[0], info[1]
+    tab_copy = pltpu.make_async_copy(table_hbm.at[chip], table, tab_sem.at[0])
 
     @pl.when(step == 0)
     def _():
         for copy in raw_copies:
             copy.start()
-        for copy in tab_copies:
-            copy.start()
+        tab_copy.start()
 
         def clear(i, _):
             grid[:, :, pl.ds(i * 128, 128), :] = jnp.zeros((2, 2, 128, LANES), F32)
@@ -158,23 +155,28 @@
         lax.fori_loop(0, GRID // 128, clear, 0)
         for copy in raw_copies:
             copy.wait()
-
-    me = info[0]
-    start, end = info[1 + step], info[2 + step]
+        tab_copy.wait()
+
+    start, end = info[2 + step], info[3 + step]
     last = order.shape[0] - 1
     cell = lax.broadcasted_iota(jnp.int32, (SUB, LANES), 0).astype(F32)
     lane_part = lax.broadcasted_iota(jnp.int32, (SUB, LANES), 1) // SUB
     sub_row = lax.broadcasted_iota(jnp.int32, (BATCH, LANES), 0)
 
-    def batch(b, _):
+    def words_of(b):
         base = start + b * BATCH
-        words = [order[jnp.minimum(base + j, last)] for j in range(BATCH)]
+        return [order[jnp.clip(base + j, 0, last)] for j in range(BATCH)]
+
+    def prepare(b):
+        base = start + b * BATCH
+        words = words_of(b)
         for j in range(BATCH):
             item = words[j] & ((1 << bits) - 1)
             rows[4 * j : 4 * j + 4, :] = raw[pl.ds(4 * item, 4), :]
         factor = jnp.where(sub_row + base < end, scale, 0.0)
         re = rows[pl.ds(0, BATCH, stride=4), :] * factor
         im = rows[pl.ds(1, BATCH, stride=4), :] * factor
+        values = {14: re, 15: im}
         for axis in range(2):
             u = rows[pl.ds(2 + axis, BATCH, stride=4), :]
             near = jnp.floor(u + 0.5)
@@ -185,29 +187,30 @@
             cot = -(wide * horner(SIN_FIT, wide2)) / horner(COS_FIT, wide2)
             sine = sign * (off * horner(SIN_FIT, off2))
             at = 8 * axis
-            prep[at + 0] = cot
-            prep[at + 1] = sine * cot
-            prep[at + 2] = sine * (1.0 + cot * cot)
-            prep[at + 3] = sign * horner(PEAK_FIT, off2)
-            prep[at + 4] = near
-            prep[at + 5] = sine
+            values[at + 0] = cot
+            values[at + 1] = sine * cot
+            values[at + 2] = sine * (1.0 + cot * cot)
+            values[at + 3] = sign * horner(PEAK_FIT, off2)
+            values[at + 4] = near
+            values[at + 5] = sine
             if axis == 0:
-                prep[6] = im * sine
-                prep[7] = re * sine
-        prep[14] = re
-        prep[15] = im
-
-        def table(axis, j):
-            at = 8 * axis
-            cot, alpha, beta, peak, near = [prep[at + i, j : j + 1, :] for i in range(5)]
-            gap = cot_ref[...] - cot
-            inv = pl.reciprocal(gap, approx=True)
-            inv = inv * (2.0 - gap * inv)
-            return jnp.where(cell == near, peak, alpha + beta * inv)
-
-        found = []
+                values[6] = im * sine
+                values[7] = re * sine
+        for at, value in values.items():
+            prep[at] = value
+
+    def dirichlet(axis, j):
+        at = 8 * axis
+        cot, alpha, beta, peak, near = [prep[at + i, j : j + 1, :] for i in range(5)]
+        gap = cot_ref[...] - cot
+        inv = pl.reciprocal(gap, approx=True)
+        inv = inv * (2.0 - gap * inv)
+        return jnp.where(cell == near, peak, alpha + beta * inv)
+
+    def multiply():
+        products = []
         for j in range(BATCH):
-            table_u, table_v = table(0, j), table(1, j)
+            table_u, table_v = dirichlet(0, j), dirichlet(1, j)
             re_j, im_j = prep[14, j : j + 1, :], prep[15, j : j + 1, :]
             b_re = re_j * table_u + prep[6, j : j + 1, :]
             b_im = im_j * table_u - prep[7, j : j + 1, :]
@@ -219,7 +222,11 @@
                 jnp.concatenate([b_high, b_high, b_low], axis=1),
             )
             extra = pltpu.roll(product[SUB : SUB + 8], 64, 1)
-            found.append(product[:SUB] + jnp.concatenate([extra] * (SUB // 8), axis=0))
+            products.append(product[:SUB] + jnp.concatenate([extra] * (SUB // 8), axis=0))
+        return products
+
+    def deposit(b):
+        words = words_of(b)
         for j in range(BATCH):
             word = words[j]
             tile = (word >> bits) & (LANES - 1)
@@ -227,86 +234,106 @@
             half = (word >> (bits + 9)) & 1
             mask = lane_part == part
             spot = pl.ds(pl.multiple_of(tile * SUB, SUB), SUB)
-            grid[0, half, spot, :] += jnp.where(mask, pltpu.roll(found[j], part * SUB, 1), 0.0)
-            moved = pltpu.roll(found[j], (part * SUB + 96) & 127, 1)
+            value = found[j]
+            grid[0, half, spot, :] += jnp.where(mask, pltpu.roll(value, part * SUB, 1), 0.0)
+            moved = pltpu.roll(value, (part * SUB + 96) & 127, 1)
             grid[1, half, spot, :] += jnp.where(mask, moved, 0.0)
+
+    found[...] = jnp.zeros(found.shape, F32)
+    batches = (end - start + BATCH - 1) // BATCH
+    prepare(0)
+
+    def batch(b, _):
+        deposit(b - 1)
+        for j, product in enumerate(multiply()):
+            found[j] = product
+        prepare(b + 1)
         return 0
 
-    lax.fori_loop(0, (end - start + BATCH - 1) // BATCH, batch, 0)
-
-    @pl.when(step == 0)
-    def _():
-        for copy in tab_copies:
-            copy.wait()
-
-    fine = FB // outputs
+    lax.fori_loop(0, batches, batch, 0)
+    deposit(batches - 1)
+
+    def butterflies(i, _):
+        for half in range(2):
+            at = i * 8
+            values = [
+                tuple(grid[c, half, pl.ds(pl.multiple_of(r * LANES + at, 8), 8), :] for c in range(2))
+                for r in range(FB)
+            ]
+            for r, value in enumerate(fft_list(values)):
+                for c in range(2):
+                    grid[c, half, pl.ds(pl.multiple_of(r * LANES + at, 8), 8), :] = value[c]
+        return 0
+
+    lax.fori_loop(0, LANES // 8, butterflies, 0)
+
+    count = table.shape[1] // 4
+    share = count // CORES
     zero = jnp.zeros((LANES, LANES), F32)
-    sums[...] = jnp.zeros(sums.shape, F32)
-
-    def transform(q0, _):
-        parts = []
-        for q1 in range(outputs):
-            q = q0 + fine * q1
-            at = pl.ds(q, LANES, stride=SUB)
-            x = jnp.concatenate(
-                [
-                    jnp.concatenate([grid[c, 0, at, :], grid[c, 1, at, :]], axis=1)
-                    for c in range(2)
-                ],
-                axis=0,
-            )
-            for c in range(2):
+
+    def transform(r):
+        at = pl.ds(pl.multiple_of(r * LANES, LANES), LANES)
+        x = jnp.concatenate(
+            [jnp.concatenate([grid[c, half, at, :] for half in range(2)], axis=1) for c in range(2)],
+            axis=0,
+        )
+        x_high, x_low = split(x)
+        f = table[r]
+        y = dot(f, x_high)
+        y = y[: 2 * count] + y[2 * count :] + dot(f[: 2 * count], x_low)
+        return at, y
+
+    def place(r, at, y):
+        for c in range(2):
+            for half in range(2):
+                grid[c, half, at, :] = zero
+        for c in range(2):
+            shares = [
+                y[c * count + k * share : c * count + (k + 1) * share] for k in range(CORES)
+            ]
+            for slot in range(CORES):
+                value = shares[slot]
+                for dest in range(CORES):
+                    value = jnp.where((me + slot) % CORES == dest, shares[dest], value)
                 for half in range(2):
-                    grid[c, half, at, :] = zero
-            x_high, x_low = split(x)
-            f_high = high[q]
-            y = dot(f_high, x_high) + dot(low[q], x_high) + dot(f_high, x_low)
-            parts.append((y[:LANES], y[LANES:]))
-        for j, (real, imag) in enumerate(fft_list(parts)):
-            cos, sin = coefs[0, q0 * outputs + j], coefs[1, q0 * outputs + j]
-            sums[j, 0] += real * cos - imag * sin
-            sums[j, 1] += real * sin + imag * cos
+                    outs[slot][half, c, pl.ds(r, share, stride=FB), :] = value[
+                        :, half * LANES : (half + 1) * LANES
+                    ]
+
+    def several(i, _):
+        done = [(i * UNROLL + k, *transform(i * UNROLL + k)) for k in range(UNROLL)]
+        for item in done:
+            place(*item)
         return 0
 
-    lax.fori_loop(0, fine, transform, 0)
-    share = outputs // CORES
-    for slot in range(CORES):
-        dest = (me + slot) % CORES
-        for k in range(share):
-            for c in range(2):
-                for half in range(2):
-                    outs[slot][half, c, k * LANES : (k + 1) * LANES, :] = sums[
-                        dest * share + k, c, :, half * LANES : (half + 1) * LANES
-                    ]
-
-
-def spectra_rows(raws, info, order, coefs, columns, bits, scale):
+    lax.fori_loop(0, FB // UNROLL, several, 0)
+
+
+def spectra_rows(raws, info, order, chips, columns, bits, scale):
     blocks = len(raws)
-    outputs = CORES * columns // LANES
     per_device = FB // CORES
     steps = per_device // 2
-    high, low = row_table()
+    table = row_table(chips)
     block = pl.BlockSpec((2, 2, columns, LANES), lambda i, *_: (i, 0, 0, 0))
     anywhere = pl.BlockSpec(memory_space=pl.ANY)
     raw_rows = blocks * raws[0].shape[0]
     return pl.pallas_call(
-        functools.partial(spectra_rows_kernel, blocks, outputs, bits, scale),
+        functools.partial(spectra_rows_kernel, blocks, bits, scale),
         grid_spec=pltpu.PrefetchScalarGridSpec(
-            num_scalar_prefetch=3,
+            num_scalar_prefetch=2,
             grid=(steps,),
             in_specs=[anywhere] * blocks
-            + [pl.BlockSpec((SUB, LANES), lambda i, *_: (0, 0)), anywhere, anywhere],
+            + [pl.BlockSpec((SUB, LANES), lambda i, *_: (0, 0)), anywhere],
             out_specs=[block] * CORES,
             scratch_shapes=[
                 pltpu.VMEM((raw_rows, LANES), F32),
-                pltpu.VMEM(high.shape, BF16),
-                pltpu.VMEM(low.shape, BF16),
+                pltpu.VMEM(table.shape[1:], BF16),
                 pltpu.VMEM((2, 2, GRID, LANES), F32),
-                pltpu.VMEM((outputs, 2, LANES, 2 * LANES), F32),
+                pltpu.VMEM((BATCH, SUB, LANES), F32),
                 pltpu.VMEM((4 * BATCH, LANES), F32),
                 pltpu.VMEM((16, BATCH, LANES), F32),
                 pltpu.SemaphoreType.DMA((blocks,)),
-                pltpu.SemaphoreType.DMA((2,)),
+                pltpu.SemaphoreType.DMA((1,)),
             ],
         ),
         out_shape=[jax.ShapeDtypeStruct((per_device, 2, columns, LANES), F32)] * CORES,
@@ -314,7 +341,7 @@
             dimension_semantics=("arbitrary",), vmem_limit_bytes=56 * 1024 * 1024
         ),
         name="spectra_rows",
-    )(info, order, coefs, *raws, jnp.asarray(cot_table()), jnp.asarray(high), jnp.asarray(low))
+    )(info, order, *raws, jnp.asarray(cot_table()), jnp.asarray(table))
 
 
 def columns_kernel(info, *refs):
@@ -354,17 +381,21 @@
     for copy in tab_copies:
         copy.wait()
 
-    def transform(r, _):
+    def transform(r):
         z_high, z_low = split(jnp.concatenate([x[r, 0], x[r, 1]], axis=1))
         f_high = high[r]
-        y = dot_nt(f_high, z_high) + dot_nt(low[r], z_high) + dot_nt(f_high, z_low)
-        at = pl.ds(r, LANES, stride=FB)
-        for part in range(0, columns, LANES):
-            out[0, part // LANES, at, :] = y[:LANES, part : part + LANES]
-            out[1, part // LANES, at, :] = y[LANES:, part : part + LANES]
+        return dot_nt(f_high, z_high) + dot_nt(low[r], z_high) + dot_nt(f_high, z_low)
+
+    def several(i, _):
+        done = [(i * UNROLL + k, transform(i * UNROLL + k)) for k in range(UNROLL)]
+        for r, y in done:
+            at = pl.ds(r, LANES, stride=FB)
+            for part in range(0, columns, LANES):
+                out[0, part // LANES, at, :] = y[:LANES, part : part + LANES]
+                out[1, part // LANES, at, :] = y[LANES:, part : part + LANES]
         return 0
 
-    lax.fori_loop(0, FB, transform, 0)
+    lax.fori_loop(0, FB // UNROLL, several, 0)
 
 
 def column_transform(pieces, info, columns):
@@ -435,12 +466,23 @@
     return [own, lax.ppermute(own, "wide", swap)]
 
 
+def gather_words(words, size):
+    if size & (size - 1):
+        every = lax.all_gather(words, "wide", axis=0)
+        return every[jnp.bitwise_xor(lax.axis_index("wide"), jnp.arange(size))].reshape(-1)
+    hop = 1
+    while hop < size:
+        moved = lax.ppermute(words, "wide", [(i, i ^ hop) for i in range(size)])
+        words = jnp.concatenate([words, moved])
+        hop *= 2
+    return words
+
+
 def per_device(visibilities, offsets, vis_count, owner, tile_row, tile_col):
     size = lax.axis_size("wide")
     count, _, slots = visibilities.shape
     chips = size // CORES
     columns = GRID // size
-    outputs = CORES * columns // LANES
     band_tiles = GRID // (SUB * size)
     place = lax.axis_index("wide")
     core, chip = place % CORES, place // CORES
@@ -455,12 +497,13 @@
     group, part = row // 4, row % 4
     key = (group % CORES) * (FB // CORES) + group // CORES
     word = (((key * 4 + part) * LANES + tile_col) << bits).astype(jnp.int32)
-    words = lax.all_gather(word, "wide", axis=0, tiled=True)
+    words = gather_words(word, size)
     cycle = chip_cycle(chips)
     spot = np.zeros(chips, np.int32)
     spot[cycle] = np.arange(chips, dtype=np.int32)
-    source = np.arange(size)
-    distance = (jnp.asarray(spot)[chip] - spot[source // CORES]) % chips
+    spot = jnp.asarray(spot)
+    source = jnp.bitwise_xor(place, jnp.arange(size))
+    distance = (spot[chip] - spot[source // CORES]) % chips
     slot = ((source + core) % CORES) * chips + distance
     data_at = (slot[:, None] * count + jnp.arange(count)[None, :]).reshape(-1)
     order = lax.sort(words + data_at.astype(jnp.int32), is_stable=False)
@@ -468,16 +511,10 @@
     shift = bits + 7 + 2 + 1
     bounds = core * steps + jnp.arange(steps + 1)
     starts = jnp.sum((words[None, :] >> shift) < bounds[:, None], axis=1)
-    info = jnp.concatenate([core[None], starts]).astype(jnp.int32)
-
-    fine = FB // outputs
-    phase = (
-        jnp.arange(fine)[:, None] * (outputs * chip + jnp.arange(outputs)[None, :]) % FB
-    ).astype(F32) * (-2.0 * math.pi / FB)
-    coefs = jnp.stack([jnp.cos(phase).reshape(-1), jnp.sin(phase).reshape(-1)])
+    info = jnp.concatenate([core[None], chip[None], starts]).astype(jnp.int32)
 
     scale = 1.0 / (math.sqrt(slots) * SUB * GRID)
-    pieces = spectra_rows(gathered, info, order, coefs, columns, bits, scale)
+    pieces = spectra_rows(gathered, info, order, chips, columns, bits, scale)
     swap = [(i, i ^ 1) for i in range(size)]
     received = [pieces[0], lax.ppermute(pieces[1], "wide", swap)]
     return column_transform(received, info, columns)

time: 423 us -> 276 us (0.65)
  Pallas kernels: 294 us -> 196 us
  blocking collectives: 60.7 us -> 0 us
  waiting for transfers between devices: 39.1 us -> 47.7 us
  starting transfers between devices: 9.35 us -> 15.3 us
    pallas_call x1, Pallas kernels: 263 us -> 172 us  [spectra_rows(): pl.pallas_call(functools.partial(spectra_rows_kernel, blocks, bits, scale...]
    unnamed x1 -> x0, blocking collectives: 60.7 us -> none
    ppermute x0 -> x4, waiting for transfers between devices: none -> 8.92 us  [gather_words(): moved = lax.ppermute(words, 'wide', [(i, i ^ hop) for i in range(size)])]
    pallas_call x1, Pallas kernels: 31.1 us -> 23.3 us  [column_transform(): pl.pallas_call(kernel, grid_spec=pltpu.PrefetchScalarGridSpec(num_scalar_...]
    ppermute x0 -> x4, starting transfers between devices: none -> 5.69 us  [gather_words(): moved = lax.ppermute(words, 'wide', [(i, i ^ hop) for i in range(size)])]
  transfers between devices with their start and end apart: 9 -> 13, of which waited for: 6 -> 10; matrix products, arithmetic and copies ran while one was open for 2% -> 3% of each run, Pallas kernels for 0% -> 0%
where the time goes in v2:
time: 276 us; the launch traced here: 273 us
  Pallas kernels  196 us (71%)
  waiting for transfers between devices  47.7 us (17%)
  starting transfers between devices  15.3 us (6%)
  other arithmetic  10.3 us (4%)
  local copies, waits for them, and re-layouts  3.93 us (1%)
    pallas_call x1, Pallas kernels, spectra_rows(): pl.pallas_call(functools.partial(spectra_rows_kernel, blocks, bits, scale...  172 us
    ppermute x4, waiting for transfers between devices, gather_blocks(): forth = lax.ppermute(forth, 'wide', ahead)  30.9 us
    pallas_call x1, Pallas kernels, column_transform(): pl.pallas_call(kernel, grid_spec=pltpu.PrefetchScalarGridSpec(num_scalar_...  23.3 us
    ppermute x4, waiting for transfers between devices, gather_words(): moved = lax.ppermute(words, 'wide', [(i, i ^ hop) for i in range(size)])  8.92 us
    ppermute x4, starting transfers between devices, gather_blocks(): forth = lax.ppermute(forth, 'wide', ahead)  7.73 us
    ppermute x1, waiting for transfers between devices, per_device(): received = [pieces[0], lax.ppermute(pieces[1], 'wide', swap)]  7.07 us
    ppermute x4, starting transfers between devices, gather_words(): moved = lax.ppermute(words, 'wide', [(i, i ^ hop) for i in range(size)])  5.69 us
    sort x1, other arithmetic, per_device(): order = lax.sort(words + data_at.astype(jnp.int32), is_stable=False)  5.52 us
  transfers between devices with their start and end apart: 13, of which 10 were waited for; matrix products, arithmetic and copies ran while one was open for 3% of the time, Pallas kernels for 0%

profile of v2, /device:TPU:0, one launch (start us, length us, event | category | flops | bytes accessed | tf_op | source)
XLA Modules:
  0.0 273.0 jit_solution(17898326504436244848)
XLA Ops:
  0.8 1.1 broadcast_select_fusion
  1.8 1.1 pad_maximum_fusion
  3.0 3.1 %collective-permute-start.4 = (f32[768,128]{1,0:T(8,128)S(1)}, f32[768,128]{1,0:T(8,128)S(1)}, u32[]{:S(2)}, u32[]{:S(2)}) collective-permute-start(f32[768,128]{1,0:T(8,128)S(1)} %bitcast.6), channel_id=1, source_target_pairs={{0,4},{1,5},{4,8},{5,9},{8,12},{9,13},{12,14},{13,15},{14,10},{15,... | collective-permute-start | bytes 1179656 | tf_op jit(solution)/shard_map/ppermute | solution.py:460
  6.1 9.1 %collective-permute-done.4 = f32[768,128]{1,0:T(8,128)S(1)} collective-permute-done((f32[768,128]{1,0:T(8,128)S(1)}, f32[768,128]{1,0:T(8,128)S(1)}, u32[]{:S(2)}, u32[]{:S(2)}) %collective-permute-start.4) | collective-permute-done | bytes 393248 | tf_op jit(solution)/shard_map/ppermute | solution.py:460
  15.1 1.8 collective-permute-start.5
  17.2 8.3 %collective-permute-done.5 = f32[768,128]{1,0:T(8,128)S(1)} collective-permute-done((f32[768,128]{1,0:T(8,128)S(1)}, f32[768,128]{1,0:T(8,128)S(1)}, u32[]{:S(2)}, u32[]{:S(2)}) %collective-permute-start.5) | collective-permute-done | bytes 393248 | tf_op jit(solution)/shard_map/ppermute | solution.py:460
  25.4 1.5 collective-permute-start.6
  27.5 7.3 %collective-permute-done.6 = f32[768,128]{1,0:T(8,128)S(1)} collective-permute-done((f32[768,128]{1,0:T(8,128)S(1)}, f32[768,128]{1,0:T(8,128)S(1)}, u32[]{:S(2)}, u32[]{:S(2)}) %collective-permute-start.6) | collective-permute-done | bytes 393248 | tf_op jit(solution)/shard_map/ppermute | solution.py:460
  34.8 1.4 collective-permute-start.7
  37.0 6.2 %collective-permute-done.7 = f32[768,128]{1,0:T(8,128)S(1)} collective-permute-done((f32[768,128]{1,0:T(8,128)S(1)}, f32[768,128]{1,0:T(8,128)S(1)}, u32[]{:S(2)}, u32[]{:S(2)}) %collective-permute-start.7) | collective-permute-done | bytes 393248 | tf_op jit(solution)/shard_map/ppermute | solution.py:460
  43.3 0.8 collective-permute-done.10
  45.0 0.8 dynamic_slice.3
  46.5 3.1 %collective-permute-done = s32[192]{0:T(256)S(1)} collective-permute-done((s32[192]{0:T(256)S(1)}, s32[192]{0:T(256)S(1)}, u32[]{:S(2)}, u32[]{:S(2)}) %collective-permute-start) | collective-permute-done | bytes 800 | tf_op jit(solution)/shard_map/ppermute | solution.py:475
  49.7 1.0 collective-permute-start.1
  51.3 1.9 collective-permute-done.1
  53.3 1.6 collective-permute-start.2
  55.0 2.0 collective-permute-done.2
  57.0 2.6 collective-permute-start.3
  59.7 1.9 collective-permute-done.3
  61.7 5.5 %sort.7.order = s32[3072]{0:T(1024)} sort(s32[3072]{0:T(1024)S(1)} %get-tuple-element.9), dimensions={0}, to_apply=%region_1.2 | sort | flops 36864 | bytes 24576 | tf_op jit(solution)/shard_map/sort | solution.py:509
  68.1 172.2 %spectra_rows.1 = (f32[16,2,256,128]{3,2,1,0:T(8,128)}, f32[16,2,256,128]{3,2,1,0:T(8,128)}) custom-call(s32[11]{0:T(128)} %pad_add_fusion.2.info, s32[3072]{0:T(1024)} %sort.7.order, f32[6144,128]{1,0:T(8,128)} %copy-done.2, f32[6144,128]{1,0:T(8,128)} %collective-permute-done.11.refs_1_, f32[32,128]{1,0:T(8,128)} %constant.120.clone.refs_2_, ...), custom_call_target="tpu_custom_call" | custom-call | tf_op jit(solution)/shard_map/spectra_rows/pallas_call | solution.py:320
  240.7 7.1 %collective-permute-done.12.refs_1_ = f32[16,2,256,128]{3,2,1,0:T(8,128)S(1)} collective-permute-done((f32[16,2,256,128]{3,2,1,0:T(8,128)}, f32[16,2,256,128]{3,2,1,0:T(8,128)S(1)}, u32[]{:S(2)}, u32[]{:S(2)}) %collective-permute-start.12) | collective-permute-done | bytes 4194336 | tf_op jit(solution)/shard_map/ppermute | solution.py:519
  247.7 2.0 copy-done.1
  249.7 23.3 %column_transform.1 = f32[2,4096,256]{2,1,0:T(8,128)} custom-call(s32[11]{0:T(128)} %pad_add_fusion.2.info, f32[16,2,256,128]{3,2,1,0:T(8,128)} %get-tuple-element.7.refs_0_, f32[16,2,256,128]{3,2,1,0:T(8,128)} %copy-done.1, bf16[32,256,256]{2,1,0:T(8,128)(2,1)} %constant.122.clone.refs_2_, bf16[32,256,256]{2,1,0:T(8,128)(2,1)} %constant.123.clone.refs_3_), custom_call_target="tpu_custom_call" | custom-call | tf_op jit(solution)/shard_map/column_transform/pallas_call | solution.py:420
  (44 shorter events, 6.2 us)
Async XLA Ops:
  3.0 41.4 %copy-start.3 = (s32[192]{0:T(256)S(1)}, s32[192]{0:T(256)}, u32[]{:S(2)}) copy-start(s32[192]{0:T(256)} %param.16) | copy-start | bytes 2308
  3.0 41.4 %copy-start.4 = (s32[192]{0:T(256)S(1)}, s32[192]{0:T(256)}, u32[]{:S(2)}) copy-start(s32[192]{0:T(256)} %param.15) | copy-start | bytes 2308
  3.0 41.4 %copy-start.5 = (s32[192]{0:T(256)S(1)}, s32[192]{0:T(256)}, u32[]{:S(2)}) copy-start(s32[192]{0:T(256)} %param.14) | copy-start | bytes 2308
  3.0 42.0 %copy-start = (s32[8]{0:T(128)S(1)}, s32[8]{0:T(128)}, u32[]{:S(2)}) copy-start(s32[8]{0:T(128)} %constant.119.clone) | copy-start | bytes 100
  3.0 12.1 %collective-permute-start.4 = (f32[768,128]{1,0:T(8,128)S(1)}, f32[768,128]{1,0:T(8,128)S(1)}, u32[]{:S(2)}, u32[]{:S(2)}) collective-permute-start(f32[768,128]{1,0:T(8,128)S(1)} %bitcast.6), channel_id=1, source_target_pairs={{0,4},{1,5},{4,8},{5,9},{8,12},{9,13},{12,14},{13,15},{14,10},{15,... | collective-permute-start | bytes 1179656 | tf_op jit(solution)/shard_map/ppermute | solution.py:460
  15.1 10.3 %collective-permute-start.5 = (f32[768,128]{1,0:T(8,128)S(1)}, f32[768,128]{1,0:T(8,128)S(1)}, u32[]{:S(2)}, u32[]{:S(2)}) collective-permute-start(f32[768,128]{1,0:T(8,128)S(1)} %collective-permute-done.4), channel_id=1, source_target_pairs={{0,4},{1,5},{4,8},{5,9},{8,12},{9,13},{12,14},{13,15},{14,10},{15,... | collective-permute-start | bytes 1179656 | tf_op jit(solution)/shard_map/ppermute | solution.py:460
  16.9 10.0 %collective-permute-start.8 = (f32[768,128]{1,0:T(8,128)S(1)}, f32[768,128]{1,0:T(8,128)S(1)}, u32[]{:S(2)}, u32[]{:S(2)}) collective-permute-start(f32[768,128]{1,0:T(8,128)S(1)} %bitcast.7), channel_id=1, source_target_pairs={{4,0},{5,1},{8,4},{9,5},{12,8},{13,9},{14,12},{15,13},{10,14},{11,... | collective-permute-start | bytes 1179656 | tf_op jit(solution)/shard_map/ppermute | solution.py:463
  25.4 9.4 %collective-permute-start.6 = (f32[768,128]{1,0:T(8,128)S(1)}, f32[768,128]{1,0:T(8,128)S(1)}, u32[]{:S(2)}, u32[]{:S(2)}) collective-permute-start(f32[768,128]{1,0:T(8,128)S(1)} %collective-permute-done.5), channel_id=1, source_target_pairs={{0,4},{1,5},{4,8},{5,9},{8,12},{9,13},{12,14},{13,15},{14,10},{15,... | collective-permute-start | bytes 1179656 | tf_op jit(solution)/shard_map/ppermute | solution.py:460
  26.9 9.3 %collective-permute-start.9 = (f32[768,128]{1,0:T(8,128)S(1)}, f32[768,128]{1,0:T(8,128)S(1)}, u32[]{:S(2)}, u32[]{:S(2)}) collective-permute-start(f32[768,128]{1,0:T(8,128)S(1)} %collective-permute-done.8), channel_id=1, source_target_pairs={{4,0},{5,1},{8,4},{9,5},{12,8},{13,9},{14,12},{15,13},{10,14},{11,... | collective-permute-start | bytes 1179656 | tf_op jit(solution)/shard_map/ppermute | solution.py:463
  34.8 8.5 %collective-permute-start.7 = (f32[768,128]{1,0:T(8,128)S(1)}, f32[768,128]{1,0:T(8,128)S(1)}, u32[]{:S(2)}, u32[]{:S(2)}) collective-permute-start(f32[768,128]{1,0:T(8,128)S(1)} %collective-permute-done.6), channel_id=1, source_target_pairs={{0,4},{1,5},{4,8},{5,9},{8,12},{9,13},{12,14},{13,15},{14,10},{15,... | collective-permute-start | bytes 1179656 | tf_op jit(solution)/shard_map/ppermute | solution.py:460
  36.2 7.9 %collective-permute-start.10 = (f32[768,128]{1,0:T(8,128)S(1)}, f32[768,128]{1,0:T(8,128)S(1)}, u32[]{:S(2)}, u32[]{:S(2)}) collective-permute-start(f32[768,128]{1,0:T(8,128)S(1)} %collective-permute-done.9), channel_id=1, source_target_pairs={{4,0},{5,1},{8,4},{9,5},{12,8},{13,9},{14,12},{15,13},{10,14},{11,... | collective-permute-start | bytes 1179656 | tf_op jit(solution)/shard_map/ppermute | solution.py:463
  44.2 23.8 %copy-start.2 = (f32[6144,128]{1,0:T(8,128)}, f32[6144,128]{1,0:T(8,128)S(1)}, u32[]{:S(2)}) copy-start(f32[6144,128]{1,0:T(8,128)S(1)} %constant_dynamic-update-slice_fusion.refs_0_) | copy-start | bytes 9437188
  44.2 23.8 %collective-permute-start.11 = (f32[6144,128]{1,0:T(8,128)S(1)}, f32[6144,128]{1,0:T(8,128)}, u32[]{:S(2)}, u32[]{:S(2)}) collective-permute-start(f32[6144,128]{1,0:T(8,128)S(1)} %constant_dynamic-update-slice_fusion.refs_0_), channel_id=1, source_target_pairs={{0,1},{1,0},{2,3},{3,2},{4,5},{5,4},{6,7},{7,6},{8,9},{9,8},{10,11... | collective-permute-start | bytes 9437192 | tf_op jit(solution)/shard_map/ppermute | solution.py:466
  44.4 5.2 %collective-permute-start = (s32[192]{0:T(256)S(1)}, s32[192]{0:T(256)S(1)}, u32[]{:S(2)}, u32[]{:S(2)}) collective-permute-start(s32[192]{0:T(256)S(1)} %add_shift-left_fusion), channel_id=1, source_target_pairs={{0,1},{1,0},{2,3},{3,2},{4,5},{5,4},{6,7},{7,6},{8,9},{9,8},{10,11... | collective-permute-start | bytes 2312 | tf_op jit(solution)/shard_map/ppermute | solution.py:475
  49.7 3.6 %collective-permute-start.1 = (s32[384]{0:T(512)S(1)}, s32[384]{0:T(512)S(1)}, u32[]{:S(2)}, u32[]{:S(2)}) collective-permute-start(s32[384]{0:T(512)S(1)} %pad_add_fusion.1), channel_id=1, source_target_pairs={{0,2},{1,3},{2,0},{3,1},{4,6},{5,7},{6,4},{7,5},{8,10},{9,11},{10,... | collective-permute-start | bytes 4616 | tf_op jit(solution)/shard_map/ppermute | solution.py:475
  53.3 3.6 %collective-permute-start.2 = (s32[768]{0:T(1024)S(1)}, s32[768]{0:T(1024)S(1)}, u32[]{:S(2)}, u32[]{:S(2)}) collective-permute-start(s32[768]{0:T(1024)S(1)} %pad_add_fusion), channel_id=1, source_target_pairs={{0,4},{1,5},{2,6},{3,7},{4,0},{5,1},{6,2},{7,3},{8,12},{9,13},{10,... | collective-permute-start | bytes 9224 | tf_op jit(solution)/shard_map/ppermute | solution.py:475
  57.0 4.5 %collective-permute-start.3 = (s32[1536]{0:T(1024)S(1)}, s32[1536]{0:T(1024)S(1)}, u32[]{:S(2)}, u32[]{:S(2)}) collective-permute-start(s32[1536]{0:T(1024)S(1)} %concatenate.30), channel_id=1, source_target_pairs={{0,8},{1,9},{2,10},{3,11},{4,12},{5,13},{6,14},{7,15},{8,0},{9,1},... | collective-permute-start | bytes 18440 | tf_op jit(solution)/shard_map/ppermute | solution.py:475
  240.3 7.4 %collective-permute-start.12 = (f32[16,2,256,128]{3,2,1,0:T(8,128)}, f32[16,2,256,128]{3,2,1,0:T(8,128)S(1)}, u32[]{:S(2)}, u32[]{:S(2)}) collective-permute-start(f32[16,2,256,128]{3,2,1,0:T(8,128)} %get-tuple-element.8), channel_id=1, source_target_pairs={{0,1},{1,0},{2,3},{3,2},{4,5},{5,4},{6,7},{7,6},{8,9},{9,8},{10,11... | collective-permute-start | bytes 12582920 | tf_op jit(solution)/shard_map/ppermute | solution.py:519
  247.7 2.0 copy-start.1

commit v3 on v2

--- a/solution.py
+++ b/solution.py
@@ -14,8 +14,10 @@
 GRID = 4096
 LANES = 128
 FB = GRID // LANES
-BATCH = 8
-UNROLL = 4
+BATCH = 16
+UNROLL = 8
+RADIX = 8
+REST = FB // RADIX
 CORES = 2
 
 BF16 = jnp.bfloat16
@@ -38,12 +40,30 @@
 
 
 @functools.cache
-def row_table(chips):
+def row_base(chips):
     count = LANES // chips
-    first = np.arange(FB)[None, :, None, None]
-    outer = np.arange(LANES).reshape(chips, 1, count, 1)
-    inner = np.arange(LANES)[None, None, None, :]
-    return np.concatenate(embed(inner * (first + FB * outer)), axis=2)
+    first = np.arange(RADIX)[:, None, None, None]
+    output = first + RADIX * np.arange(REST * count)[None, :, None, None]
+    inner = np.arange(REST * LANES).reshape(1, 1, REST, LANES)
+    values = np.exp(-2j * np.pi * (output * inner % GRID) / GRID)
+
+    def embedded(x):
+        top = np.stack([x.real, -x.imag], axis=3)
+        bottom = np.stack([x.imag, x.real], axis=3)
+        full = np.concatenate([top, bottom], axis=1)
+        return full.reshape(RADIX, 2 * REST * count, -1).astype(np.float32)
+
+    return embedded(values), embedded(1j * values)
+
+
+def row_table(chips, chip):
+    plain, turned = row_base(chips)
+    inner = np.arange(LANES) * (FB * (LANES // chips)) % GRID
+    angle = (jnp.asarray(inner) * chip % GRID).astype(F32) * (-2.0 * math.pi / GRID)
+    angle = jnp.tile(angle, 2 * REST)
+    full = plain * jnp.cos(angle) + turned * jnp.sin(angle)
+    high = lax.reduce_precision(full, 8, 7)
+    return high.astype(BF16), (full - high).astype(BF16)
 
 
 @functools.cache
@@ -130,23 +150,28 @@
 
 def spectra_rows_kernel(blocks, bits, scale, info, order, *refs):
     raws = refs[:blocks]
-    cot_ref, table_hbm = refs[blocks : blocks + 2]
-    outs = refs[blocks + 2 : blocks + 2 + CORES]
-    raw, table, grid, found, rows, prep, raw_sem, tab_sem = refs[blocks + 2 + CORES :]
+    cot_ref, high_hbm, low_hbm = refs[blocks : blocks + 3]
+    outs = refs[blocks + 3 : blocks + 3 + CORES]
+    raw, table, grid, mixed_high, mixed_low, found, rows, prep, raw_sem, tab_sem = refs[blocks + 3 + CORES :]
     step = pl.program_id(0)
-    per_block = raws[0].shape[0]
-    raw_copies = [
-        pltpu.make_async_copy(raws[i], raw.at[pl.ds(i * per_block, per_block)], raw_sem.at[i])
-        for i in range(blocks)
+    raw_copies, at = [], 0
+    for i in range(blocks):
+        size = raws[i].shape[0]
+        raw_copies.append(pltpu.make_async_copy(raws[i], raw.at[pl.ds(at, size)], raw_sem.at[i]))
+        at += size
+    me = info[0]
+    both = high_hbm.shape[1]
+    tab_copies = [
+        pltpu.make_async_copy(high_hbm, table.at[:, pl.ds(0, both)], tab_sem.at[0]),
+        pltpu.make_async_copy(low_hbm, table.at[:, pl.ds(both, both)], tab_sem.at[1]),
     ]
-    me, chip = info[0], info[1]
-    tab_copy = pltpu.make_async_copy(table_hbm.at[chip], table, tab_sem.at[0])
 
     @pl.when(step == 0)
     def _():
         for copy in raw_copies:
             copy.start()
-        tab_copy.start()
+        for copy in tab_copies:
+            copy.start()
 
         def clear(i, _):
             grid[:, :, pl.ds(i * 128, 128), :] = jnp.zeros((2, 2, 128, LANES), F32)
@@ -155,9 +180,8 @@
         lax.fori_loop(0, GRID // 128, clear, 0)
         for copy in raw_copies:
             copy.wait()
-        tab_copy.wait()
-
-    start, end = info[2 + step], info[3 + step]
+
+    start, end = info[1 + step], info[2 + step]
     last = order.shape[0] - 1
     cell = lax.broadcasted_iota(jnp.int32, (SUB, LANES), 0).astype(F32)
     lane_part = lax.broadcasted_iota(jnp.int32, (SUB, LANES), 1) // SUB
@@ -204,7 +228,6 @@
         cot, alpha, beta, peak, near = [prep[at + i, j : j + 1, :] for i in range(5)]
         gap = cot_ref[...] - cot
         inv = pl.reciprocal(gap, approx=True)
-        inv = inv * (2.0 - gap * inv)
         return jnp.where(cell == near, peak, alpha + beta * inv)
 
     def multiply():
@@ -216,12 +239,14 @@
             b_im = im_j * table_u - prep[7, j : j + 1, :]
             sine = jnp.broadcast_to(prep[13, j : j + 1, :], (16, LANES))
             a_high, a_low = split(jnp.concatenate([table_v, sine], axis=0))
-            b_high, b_low = split(jnp.concatenate([b_re, b_im, b_im, -b_re], axis=0))
+            b_high, b_low = split(jnp.concatenate([b_re, b_im], axis=0))
             product = dot_nt(
                 jnp.concatenate([a_high, a_low, a_high], axis=1),
                 jnp.concatenate([b_high, b_high, b_low], axis=1),
             )
-            extra = pltpu.roll(product[SUB : SUB + 8], 64, 1)
+            product = jnp.concatenate([product, jnp.zeros_like(product)], axis=1)
+            extra = product[SUB : SUB + 8]
+            extra = jnp.where(lane_part[:8] == 0, pltpu.roll(extra, 96, 1), -pltpu.roll(extra, 32, 1))
             products.append(product[:SUB] + jnp.concatenate([extra] * (SUB // 8), axis=0))
         return products
 
@@ -253,87 +278,90 @@
     lax.fori_loop(0, batches, batch, 0)
     deposit(batches - 1)
 
+    @pl.when(step == 0)
+    def _():
+        for copy in tab_copies:
+            copy.wait()
+
+    zero = jnp.zeros((16, LANES), F32)
+
     def butterflies(i, _):
-        for half in range(2):
-            at = i * 8
-            values = [
-                tuple(grid[c, half, pl.ds(pl.multiple_of(r * LANES + at, 8), 8), :] for c in range(2))
-                for r in range(FB)
+        half, at = i % 2, pl.multiple_of(i // 2 * 16, 16)
+        for b in range(REST):
+            places = [
+                pl.ds(pl.multiple_of((REST * a + b) * LANES + at, 16), 16) for a in range(RADIX)
             ]
+            values = [tuple(grid[c, half, p, :] for c in range(2)) for p in places]
+            for p in places:
+                for c in range(2):
+                    grid[c, half, p, :] = zero
             for r, value in enumerate(fft_list(values)):
                 for c in range(2):
-                    grid[c, half, pl.ds(pl.multiple_of(r * LANES + at, 8), 8), :] = value[c]
+                    spot = pl.ds(pl.multiple_of((2 * b + c) * LANES + at, 16), 16)
+                    mixed_high[r, half, spot, :], mixed_low[r, half, spot, :] = split(value[c])
         return 0
 
-    lax.fori_loop(0, LANES // 8, butterflies, 0)
-
-    count = table.shape[1] // 4
-    share = count // CORES
-    zero = jnp.zeros((LANES, LANES), F32)
+    lax.fori_loop(0, 2 * LANES // 16, butterflies, 0)
+
+    outputs = table.shape[1] // 4
+    share = outputs // CORES
 
     def transform(r):
-        at = pl.ds(pl.multiple_of(r * LANES, LANES), LANES)
-        x = jnp.concatenate(
-            [jnp.concatenate([grid[c, half, at, :] for half in range(2)], axis=1) for c in range(2)],
-            axis=0,
-        )
-        x_high, x_low = split(x)
+        x_high = jnp.concatenate([mixed_high[r, 0], mixed_high[r, 1]], axis=1)
+        x_low = jnp.concatenate([mixed_low[r, 0], mixed_low[r, 1]], axis=1)
         f = table[r]
         y = dot(f, x_high)
-        y = y[: 2 * count] + y[2 * count :] + dot(f[: 2 * count], x_low)
-        return at, y
-
-    def place(r, at, y):
-        for c in range(2):
-            for half in range(2):
-                grid[c, half, at, :] = zero
+        return y[: 2 * outputs] + y[2 * outputs :] + dot(f[: 2 * outputs], x_low)
+
+    def place(r, y):
         for c in range(2):
             shares = [
-                y[c * count + k * share : c * count + (k + 1) * share] for k in range(CORES)
+                y[c * outputs + k * share : c * outputs + (k + 1) * share] for k in range(CORES)
             ]
             for slot in range(CORES):
                 value = shares[slot]
                 for dest in range(CORES):
                     value = jnp.where((me + slot) % CORES == dest, shares[dest], value)
                 for half in range(2):
-                    outs[slot][half, c, pl.ds(r, share, stride=FB), :] = value[
+                    outs[slot][half, c, pl.ds(r, share, stride=RADIX), :] = value[
                         :, half * LANES : (half + 1) * LANES
                     ]
 
     def several(i, _):
-        done = [(i * UNROLL + k, *transform(i * UNROLL + k)) for k in range(UNROLL)]
+        done = [(2 * i + k, transform(2 * i + k)) for k in range(2)]
         for item in done:
             place(*item)
         return 0
 
-    lax.fori_loop(0, FB // UNROLL, several, 0)
-
-
-def spectra_rows(raws, info, order, chips, columns, bits, scale):
+    lax.fori_loop(0, RADIX // 2, several, 0)
+
+
+def spectra_rows(raws, info, order, table, columns, bits, scale):
     blocks = len(raws)
     per_device = FB // CORES
     steps = per_device // 2
-    table = row_table(chips)
     block = pl.BlockSpec((2, 2, columns, LANES), lambda i, *_: (i, 0, 0, 0))
     anywhere = pl.BlockSpec(memory_space=pl.ANY)
-    raw_rows = blocks * raws[0].shape[0]
+    raw_rows = sum(x.shape[0] for x in raws)
     return pl.pallas_call(
         functools.partial(spectra_rows_kernel, blocks, bits, scale),
         grid_spec=pltpu.PrefetchScalarGridSpec(
             num_scalar_prefetch=2,
             grid=(steps,),
             in_specs=[anywhere] * blocks
-            + [pl.BlockSpec((SUB, LANES), lambda i, *_: (0, 0)), anywhere],
+            + [pl.BlockSpec((SUB, LANES), lambda i, *_: (0, 0)), anywhere, anywhere],
             out_specs=[block] * CORES,
             scratch_shapes=[
                 pltpu.VMEM((raw_rows, LANES), F32),
-                pltpu.VMEM(table.shape[1:], BF16),
+                pltpu.VMEM((RADIX, 2 * table[0].shape[1], table[0].shape[2]), BF16),
                 pltpu.VMEM((2, 2, GRID, LANES), F32),
+                pltpu.VMEM((RADIX, 2, 2 * REST * LANES, LANES), BF16),
+                pltpu.VMEM((RADIX, 2, 2 * REST * LANES, LANES), BF16),
                 pltpu.VMEM((BATCH, SUB, LANES), F32),
                 pltpu.VMEM((4 * BATCH, LANES), F32),
                 pltpu.VMEM((16, BATCH, LANES), F32),
                 pltpu.SemaphoreType.DMA((blocks,)),
-                pltpu.SemaphoreType.DMA((1,)),
+                pltpu.SemaphoreType.DMA((2,)),
             ],
         ),
         out_shape=[jax.ShapeDtypeStruct((per_device, 2, columns, LANES), F32)] * CORES,
@@ -341,7 +369,7 @@
             dimension_semantics=("arbitrary",), vmem_limit_bytes=56 * 1024 * 1024
         ),
         name="spectra_rows",
-    )(info, order, *raws, jnp.asarray(cot_table()), jnp.asarray(table))
+    )(info, order, *raws, jnp.asarray(cot_table()), *table)
 
 
 def columns_kernel(info, *refs):
@@ -444,7 +472,7 @@
     return list(range(0, chips, 2)) + list(range(chips - 1, 0, -2))[: chips // 2]
 
 
-def gather_blocks(block, size):
+def gather_all(block, size, half, beside):
     chips = size // CORES
     cycle = chip_cycle(chips)
     ahead, back = [], []
@@ -454,28 +482,38 @@
             ahead.append((CORES * here + core, CORES * there + core))
             back.append((CORES * there + core, CORES * here + core))
     swap = [(i, i ^ 1) for i in range(size)]
-    found = {0: block}
+    found = [[block]]
     forth = other = block
-    for k in range(1, chips // 2 + 1):
-        forth = lax.ppermute(forth, "wide", ahead)
-        found[k] = forth
-        if 2 * k < chips:
+    for k in range(1, (chips + 2) // 2):
+        if k == 3:
+            forth, other, beside = lax.optimization_barrier((forth, other, beside))
+        if 2 * k == chips:
+            upper = lax.ppermute(forth[:half], "wide", ahead)
+            lower = lax.ppermute(other[half:], "wide", back)
+            found.append([upper, lower])
+        else:
+            forth = lax.ppermute(forth, "wide", ahead)
             other = lax.ppermute(other, "wide", back)
-            found[chips - k] = other
-    own = jnp.concatenate([found[k] for k in range(chips)], axis=0)
-    return [own, lax.ppermute(own, "wide", swap)]
-
-
-def gather_words(words, size):
-    if size & (size - 1):
-        every = lax.all_gather(words, "wide", axis=0)
-        return every[jnp.bitwise_xor(lax.axis_index("wide"), jnp.arange(size))].reshape(-1)
-    hop = 1
-    while hop < size:
-        moved = lax.ppermute(words, "wide", [(i, i ^ hop) for i in range(size)])
-        words = jnp.concatenate([words, moved])
-        hop *= 2
-    return words
+            found.append([forth, other])
+    swapped = []
+    for some in (found[:-2], found[-2:-1], found[-1:]):
+        arrays = [x for each in some for x in each]
+        if arrays:
+            together = jnp.concatenate(arrays, axis=0) if len(arrays) > 1 else arrays[0]
+            swapped.append(lax.ppermute(together, "wide", swap))
+    return [x for each in found for x in each] + swapped, beside
+
+
+def tags_of(arrays, rows, first, count):
+    tag_rows = -(-count // LANES)
+    parts, base = [], 0
+    for array in arrays:
+        end = base + array.shape[0]
+        for at in range(-(-(base - first) // rows) * rows + first, end, rows):
+            parts.append(array[at - base : at - base + tag_rows])
+        base = end
+    tags = jnp.stack(parts).reshape(len(parts), -1)[:, :count]
+    return tags.astype(jnp.int32)
 
 
 def per_device(visibilities, offsets, vis_count, owner, tile_row, tile_col):
@@ -486,35 +524,32 @@
     band_tiles = GRID // (SUB * size)
     place = lax.axis_index("wide")
     core, chip = place % CORES, place // CORES
-    total = size * count
-    bits = max(1, (total - 1).bit_length())
+    first = 4 * count
+    rows = first + 8 * -(-count // (8 * LANES))
+    bits = (size * rows // 4 - 1).bit_length()
 
     live = (jnp.arange(slots)[None, :] < vis_count[:, None])[:, None, :]
-    block = jnp.concatenate([jnp.where(live, visibilities, 0.0), offsets], axis=1)
-    gathered = gather_blocks(block.reshape(count * 4, slots), size)
-
-    row = owner * band_tiles + tile_row
-    group, part = row // 4, row % 4
+    items = jnp.concatenate([jnp.where(live, visibilities, 0.0), offsets], axis=1)
+    tiles = ((owner * band_tiles + tile_row) * LANES + tile_col).astype(F32)
+    tiles = jnp.pad(tiles, (0, (rows - first) * LANES - count)).reshape(-1, LANES)
+    block = jnp.concatenate([items.reshape(first, slots), tiles], axis=0)
+    table = row_table(chips, chip)
+    gathered, table = gather_all(block, size, rows // 16 * 8, table)
+
+    tiles = tags_of(gathered, rows, first, count)
+    group, part, tile_at = tiles // (4 * LANES), tiles // LANES % 4, tiles % LANES
     key = (group % CORES) * (FB // CORES) + group // CORES
-    word = (((key * 4 + part) * LANES + tile_col) << bits).astype(jnp.int32)
-    words = gather_words(word, size)
-    cycle = chip_cycle(chips)
-    spot = np.zeros(chips, np.int32)
-    spot[cycle] = np.arange(chips, dtype=np.int32)
-    spot = jnp.asarray(spot)
-    source = jnp.bitwise_xor(place, jnp.arange(size))
-    distance = (spot[chip] - spot[source // CORES]) % chips
-    slot = ((source + core) % CORES) * chips + distance
-    data_at = (slot[:, None] * count + jnp.arange(count)[None, :]).reshape(-1)
-    order = lax.sort(words + data_at.astype(jnp.int32), is_stable=False)
+    data_at = jnp.arange(size)[:, None] * (rows // 4) + jnp.arange(count)[None, :]
+    word = (((key * 4 + part) * LANES + tile_at) << bits) + data_at
+    order = lax.sort(word.reshape(-1).astype(jnp.int32), is_stable=False)
     steps = FB // CORES // 2
     shift = bits + 7 + 2 + 1
     bounds = core * steps + jnp.arange(steps + 1)
-    starts = jnp.sum((words[None, :] >> shift) < bounds[:, None], axis=1)
-    info = jnp.concatenate([core[None], chip[None], starts]).astype(jnp.int32)
+    starts = jnp.sum((order[None, :] >> shift) < bounds[:, None], axis=1)
+    info = jnp.concatenate([core[None], starts]).astype(jnp.int32)
 
     scale = 1.0 / (math.sqrt(slots) * SUB * GRID)
-    pieces = spectra_rows(gathered, info, order, chips, columns, bits, scale)
+    pieces = spectra_rows(gathered, info, order, table, columns, bits, scale)
     swap = [(i, i ^ 1) for i in range(size)]
     received = [pieces[0], lax.ppermute(pieces[1], "wide", swap)]
     return column_transform(received, info, columns)

time: 276 us -> 212 us (0.77)
  Pallas kernels: 196 us -> 132 us
  waiting for transfers between devices: 47.7 us -> 38.3 us
  other arithmetic: 10.3 us -> 18.9 us
  local copies, waits for them, and re-layouts: 3.93 us -> 10.9 us
  starting transfers between devices: 15.3 us -> 9.93 us
    pallas_call x1, Pallas kernels: 172 us -> 109 us  [spectra_rows(): pl.pallas_call(functools.partial(spectra_rows_kernel, blocks, bits, scale...]
    ppermute x12 -> x11, waiting for transfers between devices: 40.7 us -> 31.3 us  [the longest x3 24.2 us: gather_all(): forth = lax.ppermute(forth, 'wide', ahead)]
    convert_element_type x0 -> x2, other arithmetic: none -> 7.52 us  [the longest x1 6.81 us: row_table(): return (high.astype(BF16), (full - high).astype(BF16))]
    ppermute x12 -> x11, starting transfers between devices: 15 us -> 9.38 us  [the longest x3 5.31 us: gather_all(): other = lax.ppermute(other, 'wide', back)]
    unnamed x19 -> x29, local copies, waits for them, and re-layouts: 2.19 us -> 6.44 us
    slice x0 -> x13, local copies, waits for them, and re-layouts: none -> 3.43 us  [the longest x11 3.4 us: tags_of(): parts.append(array[at - base:at - base + tag_rows])]
  transfers between devices with their start and end apart: 13 -> 12, of which waited for: 10 -> 7; matrix products, arithmetic and copies ran while one was open for 3% -> 8% of each run, Pallas kernels for 0% -> 0%
where the time goes in v3:
time: 212 us; the launch traced here: 210 us
  Pallas kernels  132 us (62%)
  waiting for transfers between devices  38.3 us (18%)
  other arithmetic  18.9 us (9%)
  local copies, waits for them, and re-layouts  10.9 us (5%)
  starting transfers between devices  9.93 us (5%)
    pallas_call x1, Pallas kernels, spectra_rows(): pl.pallas_call(functools.partial(spectra_rows_kernel, blocks, bits, scale...  109 us
    ppermute x3, waiting for transfers between devices, gather_all(): forth = lax.ppermute(forth, 'wide', ahead)  24.2 us
    pallas_call x1, Pallas kernels, column_transform(): pl.pallas_call(kernel, grid_spec=pltpu.PrefetchScalarGridSpec(num_scalar_...  22.6 us
    ppermute x1, waiting for transfers between devices, per_device(): received = [pieces[0], lax.ppermute(pieces[1], 'wide', swap)]  7 us
    convert_element_type x1, other arithmetic, row_table(): return (high.astype(BF16), (full - high).astype(BF16))  6.81 us
    unnamed x29, local copies, waits for them, and re-layouts  6.44 us
    ppermute x1, waiting for transfers between devices, gather_all(): upper = lax.ppermute(forth[:half], 'wide', ahead)  5.67 us
    ppermute x3, starting transfers between devices, gather_all(): other = lax.ppermute(other, 'wide', back)  5.31 us
  transfers between devices with their start and end apart: 12, of which 7 were waited for; matrix products, arithmetic and copies ran while one was open for 8% of the time, Pallas kernels for 0%

profile of v3, /device:TPU:0, one launch (start us, length us, event | category | flops | bytes accessed | tf_op | source)
XLA Modules:
  0.0 210.3 jit_solution(17717947919404720208)
XLA Ops:
  1.5 1.1 broadcast_select_fusion
  2.6 1.1 pad_maximum_fusion.3
  3.7 3.0 %collective-permute-start.1 = (f32[776,128]{1,0:T(8,128)S(1)}, f32[776,128]{1,0:T(8,128)S(1)}, u32[]{:S(2)}, u32[]{:S(2)}) collective-permute-start(f32[776,128]{1,0:T(8,128)S(1)} %pad_maximum_fusion.1.refs_0_), channel_id=1, source_target_pairs={{4,0},{5,1},{8,4},{9,5},{12,8},{13,9},{14,12},{15,13},{10,14},{11,... | collective-permute-start | bytes 1191944 | tf_op jit(solution)/shard_map/ppermute | solution.py:496
  7.6 9.8 %collective-permute-done.refs_1_ = f32[776,128]{1,0:T(8,128)S(1)} collective-permute-done((f32[776,128]{1,0:T(8,128)S(1)}, f32[776,128]{1,0:T(8,128)S(1)}, u32[]{:S(2)}, u32[]{:S(2)}) %collective-permute-start) | collective-permute-done | bytes 397344 | tf_op jit(solution)/shard_map/ppermute | solution.py:495
  17.8 0.8 constant_dynamic-update-slice_fusion.5
  18.6 1.6 collective-permute-start.3
  20.8 0.8 constant_dynamic-update-slice_fusion.3
  21.6 0.8 constant_dynamic-update-slice_fusion.2
  22.4 4.8 %collective-permute-done.2.refs_3_ = f32[776,128]{1,0:T(8,128)S(1)} collective-permute-done((f32[776,128]{1,0:T(8,128)S(1)}, f32[776,128]{1,0:T(8,128)S(1)}, u32[]{:S(2)}, u32[]{:S(2)}) %collective-permute-start.2) | collective-permute-done | bytes 397344 | tf_op jit(solution)/shard_map/ppermute | solution.py:495
  27.2 0.8 constant_dynamic-update-slice_fusion.1
  28.4 0.8 constant_dynamic-update-slice_fusion
  29.2 6.8 %fusion = (bf16[8,128,1024]{2,1,0:T(8,128)(2,1)}, bf16[8,128,1024]{2,1,0:T(8,128)(2,1)}) fusion(f32[8,128,1024]{2,1,0:T(8,128)} %constant.135.clone, f32[8,128,1024]{2,1,0:T(8,128)} %constant.134.clone, f32[1024]{0:T(1024)S(1)} %get-tuple-element.28, f32[1024]{0:T(1024)S(1)} %get-tuple-element.29), kind=kLoop, calls=%fused_computation.2 | loop fusion | flops 7340032 | bytes 12591104 | tf_op jit(solution)/shard_map/convert_element_type | solution.py:66
  36.0 1.4 collective-permute-start.4
  38.1 9.6 %collective-permute-done.4.refs_5_ = f32[776,128]{1,0:T(8,128)S(1)} collective-permute-done((f32[776,128]{1,0:T(8,128)S(1)}, f32[776,128]{1,0:T(8,128)S(1)}, u32[]{:S(2)}, u32[]{:S(2)}) %collective-permute-start.4) | collective-permute-done | bytes 397344 | tf_op jit(solution)/shard_map/ppermute | solution.py:495
  47.7 1.1 collective-permute-done.5.refs_6_
  48.8 1.1 pad_maximum_fusion
  50.6 1.4 collective-permute-start.9
  52.0 5.7 %collective-permute-done.9.refs_7_ = f32[384,128]{1,0:T(8,128)S(1)} collective-permute-done((f32[384,128]{1,0:T(8,128)S(1)}, f32[384,128]{1,0:T(8,128)S(1)}, u32[]{:S(2)}, u32[]{:S(2)}) %collective-permute-start.9) | collective-permute-done | bytes 196640 | tf_op jit(solution)/shard_map/ppermute | solution.py:491
  58.4 0.8 pad_maximum_fusion.2
  62.9 4.9 %sort.7.order = s32[3072]{0:T(1024)S(1)} sort(s32[3072]{0:T(1024)S(1)} %reshape.89), dimensions={0}, to_apply=%region_0.1 | sort | flops 36864 | bytes 24576 | tf_op jit(solution)/shard_map/sort | solution.py:544
  68.7 109.5 %spectra_rows.1 = (f32[16,2,256,128]{3,2,1,0:T(8,128)}, f32[16,2,256,128]{3,2,1,0:T(8,128)}) custom-call(s32[10]{0:T(128)} %pad_add_fusion.info, s32[3072]{0:T(1024)} %copy-done.11, f32[776,128]{1,0:T(8,128)} %copy-done.8, f32[776,128]{1,0:T(8,128)} %copy-done.5, f32[776,128]{1,0:T(8,128)} %copy-done.4, f32[776,128]{1,0:T(8,128)} %copy-done.6, ...), custom_call_target="tpu_custom_call" | custom-call | tf_op jit(solution)/shard_map/spectra_rows/pallas_call | solution.py:346
  178.7 7.0 %collective-permute-done.11.refs_1_ = f32[16,2,256,128]{3,2,1,0:T(8,128)S(1)} collective-permute-done((f32[16,2,256,128]{3,2,1,0:T(8,128)}, f32[16,2,256,128]{3,2,1,0:T(8,128)S(1)}, u32[]{:S(2)}, u32[]{:S(2)}) %collective-permute-start.11) | collective-permute-done | bytes 4194336 | tf_op jit(solution)/shard_map/ppermute | solution.py:554
  185.7 2.0 copy-done
  187.7 22.6 %column_transform.1 = f32[2,4096,256]{2,1,0:T(8,128)} custom-call(s32[10]{0:T(128)} %pad_add_fusion.info, f32[16,2,256,128]{3,2,1,0:T(8,128)} %get-tuple-element.15.refs_0_, f32[16,2,256,128]{3,2,1,0:T(8,128)} %copy-done, bf16[32,256,256]{2,1,0:T(8,128)(2,1)} %constant.137.clone.refs_2_, bf16[32,256,256]{2,1,0:T(8,128)(2,1)} %constant.138.clone.refs_3_), custom_call_target="tpu_custom_call" | custom-call | tf_op jit(solution)/shard_map/column_transform/pallas_call | solution.py:448
  (66 shorter events, 10.9 us)
Async XLA Ops:
  3.7 24.7 %copy-start.8 = (f32[776,128]{1,0:T(8,128)}, f32[776,128]{1,0:T(8,128)S(1)}, u32[]{:S(2)}) copy-start(f32[776,128]{1,0:T(8,128)S(1)} %pad_maximum_fusion.1.refs_0_) | copy-start | bytes 1191940
  3.7 14.9 %collective-permute-start.1 = (f32[776,128]{1,0:T(8,128)S(1)}, f32[776,128]{1,0:T(8,128)S(1)}, u32[]{:S(2)}, u32[]{:S(2)}) collective-permute-start(f32[776,128]{1,0:T(8,128)S(1)} %pad_maximum_fusion.1.refs_0_), channel_id=1, source_target_pairs={{4,0},{5,1},{8,4},{9,5},{12,8},{13,9},{14,12},{15,13},{10,14},{11,... | collective-permute-start | bytes 1191944 | tf_op jit(solution)/shard_map/ppermute | solution.py:496
  6.7 10.7 %collective-permute-start = (f32[776,128]{1,0:T(8,128)S(1)}, f32[776,128]{1,0:T(8,128)S(1)}, u32[]{:S(2)}, u32[]{:S(2)}) collective-permute-start(f32[776,128]{1,0:T(8,128)S(1)} %pad_maximum_fusion.1.refs_0_), channel_id=1, source_target_pairs={{0,4},{1,5},{4,8},{5,9},{8,12},{9,13},{12,14},{13,15},{14,10},{15,... | collective-permute-start | bytes 1191944 | tf_op jit(solution)/shard_map/ppermute | solution.py:495
  17.4 18.6 %copy-start.5 = (f32[776,128]{1,0:T(8,128)}, f32[776,128]{1,0:T(8,128)S(1)}, u32[]{:S(2)}) copy-start(f32[776,128]{1,0:T(8,128)S(1)} %collective-permute-done.refs_1_) | copy-start | bytes 1191940
  17.4 9.8 %collective-permute-start.2 = (f32[776,128]{1,0:T(8,128)S(1)}, f32[776,128]{1,0:T(8,128)S(1)}, u32[]{:S(2)}, u32[]{:S(2)}) collective-permute-start(f32[776,128]{1,0:T(8,128)S(1)} %collective-permute-done.refs_1_), channel_id=1, source_target_pairs={{0,4},{1,5},{4,8},{5,9},{8,12},{9,13},{12,14},{13,15},{14,10},{15,... | collective-permute-start | bytes 1191944 | tf_op jit(solution)/shard_map/ppermute | solution.py:495
  18.6 40.7 %copy-start.4 = (f32[776,128]{1,0:T(8,128)}, f32[776,128]{1,0:T(8,128)S(1)}, u32[]{:S(2)}) copy-start(f32[776,128]{1,0:T(8,128)S(1)} %collective-permute-done.1.refs_2_) | copy-start | bytes 1191940
  18.6 9.8 %collective-permute-start.3 = (f32[776,128]{1,0:T(8,128)S(1)}, f32[776,128]{1,0:T(8,128)S(1)}, u32[]{:S(2)}, u32[]{:S(2)}) collective-permute-start(f32[776,128]{1,0:T(8,128)S(1)} %collective-permute-done.1.refs_2_), channel_id=1, source_target_pairs={{4,0},{5,1},{8,4},{9,5},{12,8},{13,9},{14,12},{15,13},{10,14},{11,... | collective-permute-start | bytes 1191944 | tf_op jit(solution)/shard_map/ppermute | solution.py:496
  27.2 8.9 %copy-start.6 = (f32[776,128]{1,0:T(8,128)}, f32[776,128]{1,0:T(8,128)S(1)}, u32[]{:S(2)}) copy-start(f32[776,128]{1,0:T(8,128)S(1)} %collective-permute-done.2.refs_3_) | copy-start | bytes 1191940
  28.4 9.1 %copy-start.7 = (f32[776,128]{1,0:T(8,128)}, f32[776,128]{1,0:T(8,128)S(1)}, u32[]{:S(2)}) copy-start(f32[776,128]{1,0:T(8,128)S(1)} %collective-permute-done.3.refs_4_) | copy-start | bytes 1191940
  29.2 33.5 %collective-permute-start.7 = (f32[3880,128]{1,0:T(8,128)}, f32[3880,128]{1,0:T(8,128)S(1)}, u32[]{:S(2)}, u32[]{:S(2)}) collective-permute-start(f32[3880,128]{1,0:T(8,128)} %constant_dynamic-update-slice_fusion), channel_id=1, source_target_pairs={{0,1},{1,0},{2,3},{3,2},{4,5},{5,4},{6,7},{7,6},{8,9},{9,8},{10,11... | collective-permute-start | bytes 5959688 | tf_op jit(solution)/shard_map/ppermute | solution.py:503
  36.0 11.7 %collective-permute-start.4 = (f32[776,128]{1,0:T(8,128)S(1)}, f32[776,128]{1,0:T(8,128)S(1)}, u32[]{:S(2)}, u32[]{:S(2)}) collective-permute-start(f32[776,128]{1,0:T(8,128)S(1)} %collective-permute-done.2.refs_3_), channel_id=1, source_target_pairs={{0,4},{1,5},{4,8},{5,9},{8,12},{9,13},{12,14},{13,15},{14,10},{15,... | collective-permute-start | bytes 1191944 | tf_op jit(solution)/shard_map/ppermute | solution.py:495
  37.4 11.3 %collective-permute-start.5 = (f32[776,128]{1,0:T(8,128)S(1)}, f32[776,128]{1,0:T(8,128)S(1)}, u32[]{:S(2)}, u32[]{:S(2)}) collective-permute-start(f32[776,128]{1,0:T(8,128)S(1)} %collective-permute-done.3.refs_4_), channel_id=1, source_target_pairs={{4,0},{5,1},{8,4},{9,5},{12,8},{13,9},{14,12},{15,13},{10,14},{11,... | collective-permute-start | bytes 1191944 | tf_op jit(solution)/shard_map/ppermute | solution.py:496
  47.7 21.0 %copy-start.2 = (f32[776,128]{1,0:T(8,128)}, f32[776,128]{1,0:T(8,128)S(1)}, u32[]{:S(2)}) copy-start(f32[776,128]{1,0:T(8,128)S(1)} %collective-permute-done.4.refs_5_) | copy-start | bytes 1191940
  48.8 19.9 %copy-start.1 = (f32[776,128]{1,0:T(8,128)}, f32[776,128]{1,0:T(8,128)S(1)}, u32[]{:S(2)}) copy-start(f32[776,128]{1,0:T(8,128)S(1)} %collective-permute-done.5.refs_6_) | copy-start | bytes 1191940
  49.9 12.1 %collective-permute-start.8 = (f32[1552,128]{1,0:T(8,128)}, f32[1552,128]{1,0:T(8,128)}, u32[]{:S(2)}, u32[]{:S(2)}) collective-permute-start(f32[1552,128]{1,0:T(8,128)} %pad_maximum_fusion), channel_id=1, source_target_pairs={{0,1},{1,0},{2,3},{3,2},{4,5},{5,4},{6,7},{7,6},{8,9},{9,8},{10,11... | collective-permute-start | bytes 2383880 | tf_op jit(solution)/shard_map/ppermute | solution.py:503
  49.9 7.8 %collective-permute-start.6 = (f32[392,128]{1,0:T(8,128)S(1)}, f32[392,128]{1,0:T(8,128)S(1)}, u32[]{:S(2)}, u32[]{:S(2)}) collective-permute-start(f32[392,128]{1,0:T(8,128)S(1)} %slice.85), channel_id=1, source_target_pairs={{4,0},{5,1},{8,4},{9,5},{12,8},{13,9},{14,12},{15,13},{10,14},{11,... | collective-permute-start | bytes 602120 | tf_op jit(solution)/shard_map/ppermute | solution.py:492
  50.6 7.1 %collective-permute-start.9 = (f32[384,128]{1,0:T(8,128)S(1)}, f32[384,128]{1,0:T(8,128)S(1)}, u32[]{:S(2)}, u32[]{:S(2)}) collective-permute-start(f32[384,128]{1,0:T(8,128)S(1)} %slice.94), channel_id=1, source_target_pairs={{0,4},{1,5},{4,8},{5,9},{8,12},{9,13},{12,14},{13,15},{14,10},{15,... | collective-permute-start | bytes 589832 | tf_op jit(solution)/shard_map/ppermute | solution.py:491
  57.7 0.7 copy-start.10
  58.4 10.2 %copy-start.9 = (f32[392,128]{1,0:T(8,128)}, f32[392,128]{1,0:T(8,128)S(1)}, u32[]{:S(2)}) copy-start(f32[392,128]{1,0:T(8,128)S(1)} %collective-permute-done.6.refs_8_) | copy-start | bytes 602116
  59.2 2.1 collective-permute-start.10
  62.7 6.0 %copy-start.3 = (f32[3880,128]{1,0:T(8,128)}, f32[3880,128]{1,0:T(8,128)S(1)}, u32[]{:S(2)}) copy-start(f32[3880,128]{1,0:T(8,128)S(1)} %collective-permute-done.7.refs_9_) | copy-start | bytes 5959684
  67.8 0.8 copy-start.11
  178.1 7.5 %collective-permute-start.11 = (f32[16,2,256,128]{3,2,1,0:T(8,128)}, f32[16,2,256,128]{3,2,1,0:T(8,128)S(1)}, u32[]{:S(2)}, u32[]{:S(2)}) collective-permute-start(f32[16,2,256,128]{3,2,1,0:T(8,128)} %get-tuple-element.16), channel_id=1, source_target_pairs={{0,1},{1,0},{2,3},{3,2},{4,5},{5,4},{6,7},{7,6},{8,9},{9,8},{10,11... | collective-permute-start | bytes 12582920 | tf_op jit(solution)/shard_map/ppermute | solution.py:554
  185.7 2.0 copy-start

commit v4 on v3

--- a/solution.py
+++ b/solution.py
@@ -14,7 +14,7 @@
 GRID = 4096
 LANES = 128
 FB = GRID // LANES
-BATCH = 16
+BATCH = 32
 UNROLL = 8
 RADIX = 8
 REST = FB // RADIX
@@ -40,30 +40,20 @@
 
 
 @functools.cache
-def row_base(chips):
+def row_table(chips):
     count = LANES // chips
-    first = np.arange(RADIX)[:, None, None, None]
-    output = first + RADIX * np.arange(REST * count)[None, :, None, None]
-    inner = np.arange(REST * LANES).reshape(1, 1, REST, LANES)
-    values = np.exp(-2j * np.pi * (output * inner % GRID) / GRID)
-
-    def embedded(x):
-        top = np.stack([x.real, -x.imag], axis=3)
-        bottom = np.stack([x.imag, x.real], axis=3)
-        full = np.concatenate([top, bottom], axis=1)
-        return full.reshape(RADIX, 2 * REST * count, -1).astype(np.float32)
-
-    return embedded(values), embedded(1j * values)
-
-
-def row_table(chips, chip):
-    plain, turned = row_base(chips)
-    inner = np.arange(LANES) * (FB * (LANES // chips)) % GRID
-    angle = (jnp.asarray(inner) * chip % GRID).astype(F32) * (-2.0 * math.pi / GRID)
-    angle = jnp.tile(angle, 2 * REST)
-    full = plain * jnp.cos(angle) + turned * jnp.sin(angle)
-    high = lax.reduce_precision(full, 8, 7)
-    return high.astype(BF16), (full - high).astype(BF16)
+    chip = np.arange(chips)[:, None, None, None, None]
+    first = np.arange(RADIX)[None, :, None, None, None]
+    output = np.arange(REST * count)[None, None, :, None, None] + REST * count * chip
+    inner = np.arange(REST * LANES).reshape(1, 1, 1, REST, LANES)
+    phase = (first + RADIX * output) * inner % GRID
+    roots = np.exp(-2j * np.pi * np.arange(GRID) / GRID)
+    real, imag = roots.real.astype(np.float32)[phase], roots.imag.astype(np.float32)[phase]
+    top = np.stack([real, -imag], axis=4)
+    bottom = np.stack([imag, real], axis=4)
+    full = np.concatenate([top, bottom], axis=2)
+    full = full.reshape(chips, RADIX, 2 * REST * count, -1)
+    return np.concatenate(split_np(full), axis=2)
 
 
 @functools.cache
@@ -150,9 +140,9 @@
 
 def spectra_rows_kernel(blocks, bits, scale, info, order, *refs):
     raws = refs[:blocks]
-    cot_ref, high_hbm, low_hbm = refs[blocks : blocks + 3]
-    outs = refs[blocks + 3 : blocks + 3 + CORES]
-    raw, table, grid, mixed_high, mixed_low, found, rows, prep, raw_sem, tab_sem = refs[blocks + 3 + CORES :]
+    cot_ref, table_hbm = refs[blocks : blocks + 2]
+    outs = refs[blocks + 2 : blocks + 2 + CORES]
+    raw, table, grid, mixed_high, mixed_low, found, rows, prep, raw_sem, tab_sem = refs[blocks + 2 + CORES :]
     step = pl.program_id(0)
     raw_copies, at = [], 0
     for i in range(blocks):
@@ -160,18 +150,13 @@
         raw_copies.append(pltpu.make_async_copy(raws[i], raw.at[pl.ds(at, size)], raw_sem.at[i]))
         at += size
     me = info[0]
-    both = high_hbm.shape[1]
-    tab_copies = [
-        pltpu.make_async_copy(high_hbm, table.at[:, pl.ds(0, both)], tab_sem.at[0]),
-        pltpu.make_async_copy(low_hbm, table.at[:, pl.ds(both, both)], tab_sem.at[1]),
-    ]
+    tab_copy = pltpu.make_async_copy(table_hbm.at[info[1]], table, tab_sem.at[0])
 
     @pl.when(step == 0)
     def _():
         for copy in raw_copies:
             copy.start()
-        for copy in tab_copies:
-            copy.start()
+        tab_copy.start()
 
         def clear(i, _):
             grid[:, :, pl.ds(i * 128, 128), :] = jnp.zeros((2, 2, 128, LANES), F32)
@@ -181,7 +166,7 @@
         for copy in raw_copies:
             copy.wait()
 
-    start, end = info[1 + step], info[2 + step]
+    start, end = info[2 + step], info[3 + step]
     last = order.shape[0] - 1
     cell = lax.broadcasted_iota(jnp.int32, (SUB, LANES), 0).astype(F32)
     lane_part = lax.broadcasted_iota(jnp.int32, (SUB, LANES), 1) // SUB
@@ -280,8 +265,7 @@
 
     @pl.when(step == 0)
     def _():
-        for copy in tab_copies:
-            copy.wait()
+        tab_copy.wait()
 
     zero = jnp.zeros((16, LANES), F32)
 
@@ -336,8 +320,9 @@
     lax.fori_loop(0, RADIX // 2, several, 0)
 
 
-def spectra_rows(raws, info, order, table, columns, bits, scale):
+def spectra_rows(raws, info, order, chips, columns, bits, scale):
     blocks = len(raws)
+    table = row_table(chips)
     per_device = FB // CORES
     steps = per_device // 2
     block = pl.BlockSpec((2, 2, columns, LANES), lambda i, *_: (i, 0, 0, 0))
@@ -349,11 +334,11 @@
             num_scalar_prefetch=2,
             grid=(steps,),
             in_specs=[anywhere] * blocks
-            + [pl.BlockSpec((SUB, LANES), lambda i, *_: (0, 0)), anywhere, anywhere],
+            + [pl.BlockSpec((SUB, LANES), lambda i, *_: (0, 0)), anywhere],
             out_specs=[block] * CORES,
             scratch_shapes=[
                 pltpu.VMEM((raw_rows, LANES), F32),
-                pltpu.VMEM((RADIX, 2 * table[0].shape[1], table[0].shape[2]), BF16),
+                pltpu.VMEM(table.shape[1:], BF16),
                 pltpu.VMEM((2, 2, GRID, LANES), F32),
                 pltpu.VMEM((RADIX, 2, 2 * REST * LANES, LANES), BF16),
                 pltpu.VMEM((RADIX, 2, 2 * REST * LANES, LANES), BF16),
@@ -369,12 +354,12 @@
             dimension_semantics=("arbitrary",), vmem_limit_bytes=56 * 1024 * 1024
         ),
         name="spectra_rows",
-    )(info, order, *raws, jnp.asarray(cot_table()), *table)
+    )(info, order, *raws, jnp.asarray(cot_table()), jnp.asarray(table))
 
 
 def columns_kernel(info, *refs):
     pieces = refs[:CORES]
-    high_hbm, low_hbm, out, x, high, low, piece_sem, tab_sem = refs[CORES:]
+    high_hbm, low_hbm, out_hbm, out, x, high, low, piece_sem, tab_sem, out_sem = refs[CORES:]
     me = info[0]
     per_device, _, columns, _ = pieces[0].shape
     copies = [
@@ -414,46 +399,52 @@
         f_high = high[r]
         return dot_nt(f_high, z_high) + dot_nt(low[r], z_high) + dot_nt(f_high, z_low)
 
+    def store(i):
+        at = pl.ds(pl.multiple_of(i * UNROLL, UNROLL), UNROLL)
+        return [
+            pltpu.make_async_copy(
+                out.at[:, part, :, at, :],
+                out_hbm.at[:, :, at, pl.ds(part * LANES, LANES)],
+                out_sem.at[part],
+            )
+            for part in range(columns // LANES)
+        ]
+
     def several(i, _):
         done = [(i * UNROLL + k, transform(i * UNROLL + k)) for k in range(UNROLL)]
         for r, y in done:
-            at = pl.ds(r, LANES, stride=FB)
-            for part in range(0, columns, LANES):
-                out[0, part // LANES, at, :] = y[:LANES, part : part + LANES]
-                out[1, part // LANES, at, :] = y[LANES:, part : part + LANES]
+            for part in range(columns // LANES):
+                for c in range(2):
+                    out[c, part, :, r, :] = y[
+                        c * LANES : (c + 1) * LANES, part * LANES : (part + 1) * LANES
+                    ]
+        @pl.when(i > 0)
+        def _():
+            for copy in store(i - 1):
+                copy.wait()
+
+        for copy in store(i):
+            copy.start()
         return 0
 
     lax.fori_loop(0, FB // UNROLL, several, 0)
+    for copy in store(FB // UNROLL - 1):
+        copy.wait()
 
 
 def column_transform(pieces, info, columns):
     high, low = column_table()
     anywhere = pl.BlockSpec(memory_space=pl.ANY)
 
-    def kernel(info, *refs):
-        inputs, out_hbm = refs[: CORES + 2], refs[CORES + 2]
-        out, x, high, low, piece_sem, tab_sem, out_sem = refs[CORES + 3 :]
-        columns_kernel(info, *inputs, out, x, high, low, piece_sem, tab_sem)
-        copies = [
-            pltpu.make_async_copy(
-                out.at[:, k], out_hbm.at[:, :, pl.ds(k * LANES, LANES)], out_sem.at[k]
-            )
-            for k in range(columns // LANES)
-        ]
-        for copy in copies:
-            copy.start()
-        for copy in copies:
-            copy.wait()
-
     return pl.pallas_call(
-        kernel,
+        columns_kernel,
         grid_spec=pltpu.PrefetchScalarGridSpec(
             num_scalar_prefetch=1,
             grid=(1,),
             in_specs=[anywhere] * (CORES + 2),
             out_specs=anywhere,
             scratch_shapes=[
-                pltpu.VMEM((2, columns // LANES, GRID, LANES), F32),
+                pltpu.VMEM((2, columns // LANES, LANES, FB, LANES), F32),
                 pltpu.VMEM((FB, 2, columns, LANES), F32),
                 pltpu.VMEM(high.shape, BF16),
                 pltpu.VMEM(low.shape, BF16),
@@ -462,8 +453,8 @@
                 pltpu.SemaphoreType.DMA((columns // LANES,)),
             ],
         ),
-        out_shape=jax.ShapeDtypeStruct((2, GRID, columns), F32),
-        compiler_params=pltpu.CompilerParams(vmem_limit_bytes=56 * 1024 * 1024),
+        out_shape=jax.ShapeDtypeStruct((2, LANES, FB, columns), F32),
+        compiler_params=pltpu.CompilerParams(vmem_limit_bytes=62 * 1024 * 1024),
         name="column_transform",
     )(info, *pieces, jnp.asarray(high), jnp.asarray(low))
 
@@ -472,7 +463,7 @@
     return list(range(0, chips, 2)) + list(range(chips - 1, 0, -2))[: chips // 2]
 
 
-def gather_all(block, size, half, beside):
+def gather_all(block, size, half):
     chips = size // CORES
     cycle = chip_cycle(chips)
     ahead, back = [], []
@@ -485,8 +476,6 @@
     found = [[block]]
     forth = other = block
     for k in range(1, (chips + 2) // 2):
-        if k == 3:
-            forth, other, beside = lax.optimization_barrier((forth, other, beside))
         if 2 * k == chips:
             upper = lax.ppermute(forth[:half], "wide", ahead)
             lower = lax.ppermute(other[half:], "wide", back)
@@ -501,19 +490,38 @@
         if arrays:
             together = jnp.concatenate(arrays, axis=0) if len(arrays) > 1 else arrays[0]
             swapped.append(lax.ppermute(together, "wide", swap))
-    return [x for each in found for x in each] + swapped, beside
+    return [x for each in found for x in each] + swapped
 
 
 def tags_of(arrays, rows, first, count):
-    tag_rows = -(-count // LANES)
-    parts, base = [], 0
-    for array in arrays:
+    spots, base = [], 0
+    for i, array in enumerate(arrays):
         end = base + array.shape[0]
         for at in range(-(-(base - first) // rows) * rows + first, end, rows):
-            parts.append(array[at - base : at - base + tag_rows])
+            spots.append((i, at - base))
         base = end
-    tags = jnp.stack(parts).reshape(len(parts), -1)[:, :count]
-    return tags.astype(jnp.int32)
+    tag_rows = rows - first
+
+    def kernel(*refs):
+        inputs, out, sems = refs[: len(arrays)], refs[-2], refs[-1]
+        copies = [
+            pltpu.make_async_copy(inputs[i].at[pl.ds(at, tag_rows)], out.at[k], sems.at[k])
+            for k, (i, at) in enumerate(spots)
+        ]
+        for copy in copies:
+            copy.start()
+        for copy in copies:
+            copy.wait()
+
+    tags = pl.pallas_call(
+        kernel,
+        in_specs=[pl.BlockSpec(memory_space=pl.ANY)] * len(arrays),
+        out_specs=pl.BlockSpec(memory_space=pltpu.VMEM),
+        scratch_shapes=[pltpu.SemaphoreType.DMA((len(spots),))],
+        out_shape=jax.ShapeDtypeStruct((len(spots), tag_rows, LANES), F32),
+        name="tags",
+    )(*arrays)
+    return tags.reshape(len(spots), -1)[:, :count].astype(jnp.int32)
 
 
 def per_device(visibilities, offsets, vis_count, owner, tile_row, tile_col):
@@ -533,8 +541,7 @@
     tiles = ((owner * band_tiles + tile_row) * LANES + tile_col).astype(F32)
     tiles = jnp.pad(tiles, (0, (rows - first) * LANES - count)).reshape(-1, LANES)
     block = jnp.concatenate([items.reshape(first, slots), tiles], axis=0)
-    table = row_table(chips, chip)
-    gathered, table = gather_all(block, size, rows // 16 * 8, table)
+    gathered = gather_all(block, size, rows // 16 * 8)
 
     tiles = tags_of(gathered, rows, first, count)
     group, part, tile_at = tiles // (4 * LANES), tiles // LANES % 4, tiles % LANES
@@ -546,13 +553,13 @@
     shift = bits + 7 + 2 + 1
     bounds = core * steps + jnp.arange(steps + 1)
     starts = jnp.sum((order[None, :] >> shift) < bounds[:, None], axis=1)
-    info = jnp.concatenate([core[None], starts]).astype(jnp.int32)
+    info = jnp.concatenate([core[None], chip[None], starts]).astype(jnp.int32)
 
     scale = 1.0 / (math.sqrt(slots) * SUB * GRID)
-    pieces = spectra_rows(gathered, info, order, table, columns, bits, scale)
+    pieces = spectra_rows(gathered, info, order, chips, columns, bits, scale)
     swap = [(i, i ^ 1) for i in range(size)]
     received = [pieces[0], lax.ppermute(pieces[1], "wide", swap)]
-    return column_transform(received, info, columns)
+    return column_transform(received, info, columns).reshape(2, GRID, columns)
 
 
 def solution(mesh):

time: 212 us -> 194 us (0.915)
  Pallas kernels: 132 us -> 124 us
  other arithmetic: 18.9 us -> 11.3 us
  local copies, waits for them, and re-layouts: 10.9 us -> 6.83 us
  waiting for transfers between devices: 38.3 us -> 41.4 us
    ppermute x3, waiting for transfers between devices: 24.2 us -> 14.8 us  [gather_all(): forth = lax.ppermute(forth, 'wide', ahead)]
    ppermute x3, waiting for transfers between devices: 1.48 us -> 10.7 us  [gather_all(): other = lax.ppermute(other, 'wide', back)]
    pallas_call x1, Pallas kernels: 109 us -> 102 us  [spectra_rows(): pl.pallas_call(functools.partial(spectra_rows_kernel, blocks, bits, scale...]
    convert_element_type x1 -> x0, other arithmetic: 6.81 us -> none  [row_table(): return (high.astype(BF16), (full - high).astype(BF16))]
    ppermute x3, starting transfers between devices: 5.31 us -> 0.78 us  [gather_all(): other = lax.ppermute(other, 'wide', back)]
    ppermute x3, starting transfers between devices: 1.93 us -> 6.35 us  [gather_all(): forth = lax.ppermute(forth, 'wide', ahead)]
    slice x11 -> x0, local copies, waits for them, and re-layouts: 3.4 us -> none  [tags_of(): parts.append(array[at - base:at - base + tag_rows])]
    pallas_call x1 -> x2, Pallas kernels: 22.6 us -> 21.9 us  [the longest x1 20.4 us: column_transform(): pl.pallas_call(columns_kernel, grid_spec=pltpu.PrefetchScalarGridSpec(num...]
  transfers between devices with their start and end apart: 12 -> 12, of which waited for: 7 -> 8; matrix products, arithmetic and copies ran while one was open for 8% -> 3% of each run, Pallas kernels for 0% -> 0%
where the time goes in v4:
time: 194 us; the launch traced here: 193 us
  Pallas kernels  124 us (64%)
  waiting for transfers between devices  41.4 us (21%)
  other arithmetic  11.3 us (6%)
  starting transfers between devices  9.45 us (5%)
  local copies, waits for them, and re-layouts  6.83 us (4%)
    pallas_call x1, Pallas kernels, spectra_rows(): pl.pallas_call(functools.partial(spectra_rows_kernel, blocks, bits, scale...  102 us
    pallas_call x1, Pallas kernels, column_transform(): pl.pallas_call(columns_kernel, grid_spec=pltpu.PrefetchScalarGridSpec(num...  20.4 us
    ppermute x3, waiting for transfers between devices, gather_all(): forth = lax.ppermute(forth, 'wide', ahead)  14.8 us
    ppermute x3, waiting for transfers between devices, gather_all(): other = lax.ppermute(other, 'wide', back)  10.7 us
    ppermute x1, waiting for transfers between devices, per_device(): received = [pieces[0], lax.ppermute(pieces[1], 'wide', swap)]  7.39 us
    ppermute x1, waiting for transfers between devices, gather_all(): upper = lax.ppermute(forth[:half], 'wide', ahead)  6.43 us
    ppermute x3, starting transfers between devices, gather_all(): forth = lax.ppermute(forth, 'wide', ahead)  6.35 us
    unnamed x28, local copies, waits for them, and re-layouts  5.9 us
  transfers between devices with their start and end apart: 12, of which 8 were waited for; matrix products, arithmetic and copies ran while one was open for 3% of the time, Pallas kernels for 0%

profile of v4, /device:TPU:0, one launch (start us, length us, event | category | flops | bytes accessed | tf_op | source)
XLA Modules:
  0.0 193.1 jit_solution(10084892505823138320)
XLA Ops:
  1.5 1.1 broadcast_select_fusion
  2.6 1.1 pad_maximum_fusion.3
  3.7 3.1 %collective-permute-start = (f32[776,128]{1,0:T(8,128)S(1)}, f32[776,128]{1,0:T(8,128)S(1)}, u32[]{:S(2)}, u32[]{:S(2)}) collective-permute-start(f32[776,128]{1,0:T(8,128)S(1)} %pad_maximum_fusion.1.refs_0_), channel_id=1, source_target_pairs={{0,4},{1,5},{4,8},{5,9},{8,12},{9,13},{12,14},{13,15},{14,10},{15,... | collective-permute-start | bytes 1191944 | tf_op jit(solution)/shard_map/ppermute | solution.py:484
  6.8 9.1 %collective-permute-done.refs_1_ = f32[776,128]{1,0:T(8,128)S(1)} collective-permute-done((f32[776,128]{1,0:T(8,128)S(1)}, f32[776,128]{1,0:T(8,128)S(1)}, u32[]{:S(2)}, u32[]{:S(2)}) %collective-permute-start) | collective-permute-done | bytes 397344 | tf_op jit(solution)/shard_map/ppermute | solution.py:484
  16.0 1.8 collective-permute-start.2
  19.4 0.8 constant_dynamic-update-slice_fusion.3
  20.9 5.4 %collective-permute-done.2.refs_3_ = f32[776,128]{1,0:T(8,128)S(1)} collective-permute-done((f32[776,128]{1,0:T(8,128)S(1)}, f32[776,128]{1,0:T(8,128)S(1)}, u32[]{:S(2)}, u32[]{:S(2)}) %collective-permute-start.2) | collective-permute-done | bytes 397344 | tf_op jit(solution)/shard_map/ppermute | solution.py:484
  26.3 0.8 constant_dynamic-update-slice_fusion.1
  27.2 1.2 collective-permute-done.3.refs_4_
  28.3 0.8 constant_dynamic-update-slice_fusion
  29.7 1.5 collective-permute-start.4
  31.2 9.6 %collective-permute-done.5.refs_6_ = f32[776,128]{1,0:T(8,128)S(1)} collective-permute-done((f32[776,128]{1,0:T(8,128)S(1)}, f32[776,128]{1,0:T(8,128)S(1)}, u32[]{:S(2)}, u32[]{:S(2)}) %collective-permute-start.5) | collective-permute-done | bytes 397344 | tf_op jit(solution)/shard_map/ppermute | solution.py:485
  41.0 1.0 pad_maximum_fusion
  42.0 1.5 collective-permute-start.7
  44.2 6.4 %collective-permute-done.6.refs_7_ = f32[384,128]{1,0:T(8,128)S(1)} collective-permute-done((f32[384,128]{1,0:T(8,128)S(1)}, f32[384,128]{1,0:T(8,128)S(1)}, u32[]{:S(2)}, u32[]{:S(2)}) %collective-permute-start.6) | collective-permute-done | bytes 196640 | tf_op jit(solution)/shard_map/ppermute | solution.py:480
  50.6 0.9 pad_maximum_fusion.2
  51.5 2.1 %collective-permute-done.10.refs_11_ = f32[776,128]{1,0:T(8,128)} collective-permute-done((f32[776,128]{1,0:T(8,128)}, f32[776,128]{1,0:T(8,128)}, u32[]{:S(2)}, u32[]{:S(2)}) %collective-permute-start.10) | collective-permute-done | bytes 397344 | tf_op jit(solution)/shard_map/ppermute | solution.py:492
  53.6 1.3 copy-done
  54.9 1.5 tags.1
  56.4 0.9 copy.13
  57.4 4.9 %sort.7.order = s32[3072]{0:T(1024)S(1)} sort(s32[3072]{0:T(1024)S(1)} %reshape.46), dimensions={0}, to_apply=%region_0.1 | sort | flops 36864 | bytes 24576 | tf_op jit(solution)/shard_map/sort | solution.py:551
  63.1 102.1 %spectra_rows.1 = (f32[16,2,256,128]{3,2,1,0:T(8,128)}, f32[16,2,256,128]{3,2,1,0:T(8,128)}) custom-call(s32[11]{0:T(128)} %pad_add_fusion.info, s32[3072]{0:T(1024)} %copy-done.10, f32[776,128]{1,0:T(8,128)} %copy-done.3, f32[776,128]{1,0:T(8,128)} %copy-done.4, f32[776,128]{1,0:T(8,128)} %copy-done.5, f32[776,128]{1,0:T(8,128)} %copy-done.6, ...), custom_call_target="tpu_custom_call" | custom-call | tf_op jit(solution)/shard_map/spectra_rows/pallas_call | solution.py:331
  165.4 7.4 %collective-permute-done.11.refs_1_ = f32[16,2,256,128]{3,2,1,0:T(8,128)} collective-permute-done((f32[16,2,256,128]{3,2,1,0:T(8,128)}, f32[16,2,256,128]{3,2,1,0:T(8,128)}, u32[]{:S(2)}, u32[]{:S(2)}) %collective-permute-start.11) | collective-permute-done | bytes 4194336 | tf_op jit(solution)/shard_map/ppermute | solution.py:561
  172.8 20.4 %column_transform.1 = f32[2,128,32,256]{3,2,1,0:T(8,128)} custom-call(s32[11]{0:T(128)} %pad_add_fusion.info, f32[16,2,256,128]{3,2,1,0:T(8,128)} %get-tuple-element.7.refs_0_, f32[16,2,256,128]{3,2,1,0:T(8,128)} %collective-permute-done.11.refs_1_, bf16[32,256,256]{2,1,0:T(8,128)(2,1)} %constant.115.clone.refs_2_, bf16[32,256,256]{2,1,0:T(8,128)(2,1)} %constant.116.clone.refs_3_), custom_call_target="tpu_custom_call" | custom-call | tf_op jit(solution)/shard_map/column_transform/pallas_call | solution.py:439
  (50 shorter events, 6.6 us)
Async XLA Ops:
  3.7 38.3 %copy-start.3 = (f32[776,128]{1,0:T(8,128)}, f32[776,128]{1,0:T(8,128)S(1)}, u32[]{:S(2)}) copy-start(f32[776,128]{1,0:T(8,128)S(1)} %pad_maximum_fusion.1.refs_0_) | copy-start | bytes 1191940
  3.7 12.2 %collective-permute-start = (f32[776,128]{1,0:T(8,128)S(1)}, f32[776,128]{1,0:T(8,128)S(1)}, u32[]{:S(2)}, u32[]{:S(2)}) collective-permute-start(f32[776,128]{1,0:T(8,128)S(1)} %pad_maximum_fusion.1.refs_0_), channel_id=1, source_target_pairs={{0,4},{1,5},{4,8},{5,9},{8,12},{9,13},{12,14},{13,15},{14,10},{15,... | collective-permute-start | bytes 1191944 | tf_op jit(solution)/shard_map/ppermute | solution.py:484
  6.8 11.7 %collective-permute-start.1 = (f32[776,128]{1,0:T(8,128)S(1)}, f32[776,128]{1,0:T(8,128)S(1)}, u32[]{:S(2)}, u32[]{:S(2)}) collective-permute-start(f32[776,128]{1,0:T(8,128)S(1)} %pad_maximum_fusion.1.refs_0_), channel_id=1, source_target_pairs={{4,0},{5,1},{8,4},{9,5},{12,8},{13,9},{14,12},{15,13},{10,14},{11,... | collective-permute-start | bytes 1191944 | tf_op jit(solution)/shard_map/ppermute | solution.py:485
  16.0 24.8 %copy-start.4 = (f32[776,128]{1,0:T(8,128)}, f32[776,128]{1,0:T(8,128)S(1)}, u32[]{:S(2)}) copy-start(f32[776,128]{1,0:T(8,128)S(1)} %collective-permute-done.refs_1_) | copy-start | bytes 1191940
  16.0 10.4 %collective-permute-start.2 = (f32[776,128]{1,0:T(8,128)S(1)}, f32[776,128]{1,0:T(8,128)S(1)}, u32[]{:S(2)}, u32[]{:S(2)}) collective-permute-start(f32[776,128]{1,0:T(8,128)S(1)} %collective-permute-done.refs_1_), channel_id=1, source_target_pairs={{0,4},{1,5},{4,8},{5,9},{8,12},{9,13},{12,14},{13,15},{14,10},{15,... | collective-permute-start | bytes 1191944 | tf_op jit(solution)/shard_map/ppermute | solution.py:484
  18.5 22.2 %copy-start.5 = (f32[776,128]{1,0:T(8,128)}, f32[776,128]{1,0:T(8,128)S(1)}, u32[]{:S(2)}) copy-start(f32[776,128]{1,0:T(8,128)S(1)} %collective-permute-done.1.refs_2_) | copy-start | bytes 1191940
  18.5 9.8 %collective-permute-start.3 = (f32[776,128]{1,0:T(8,128)S(1)}, f32[776,128]{1,0:T(8,128)S(1)}, u32[]{:S(2)}, u32[]{:S(2)}) collective-permute-start(f32[776,128]{1,0:T(8,128)S(1)} %collective-permute-done.1.refs_2_), channel_id=1, source_target_pairs={{4,0},{5,1},{8,4},{9,5},{12,8},{13,9},{14,12},{15,13},{10,14},{11,... | collective-permute-start | bytes 1191944 | tf_op jit(solution)/shard_map/ppermute | solution.py:485
  26.3 14.4 %copy-start.6 = (f32[776,128]{1,0:T(8,128)}, f32[776,128]{1,0:T(8,128)S(1)}, u32[]{:S(2)}) copy-start(f32[776,128]{1,0:T(8,128)S(1)} %collective-permute-done.2.refs_3_) | copy-start | bytes 1191940
  28.3 12.5 %copy-start.7 = (f32[776,128]{1,0:T(8,128)}, f32[776,128]{1,0:T(8,128)S(1)}, u32[]{:S(2)}) copy-start(f32[776,128]{1,0:T(8,128)S(1)} %collective-permute-done.3.refs_4_) | copy-start | bytes 1191940
  29.1 24.4 %collective-permute-start.8 = (f32[3880,128]{1,0:T(8,128)}, f32[3880,128]{1,0:T(8,128)S(1)}, u32[]{:S(2)}, u32[]{:S(2)}) collective-permute-start(f32[3880,128]{1,0:T(8,128)} %constant_dynamic-update-slice_fusion), channel_id=1, source_target_pairs={{0,1},{1,0},{2,3},{3,2},{4,5},{5,4},{6,7},{7,6},{8,9},{9,8},{10,11... | collective-permute-start | bytes 5959688 | tf_op jit(solution)/shard_map/ppermute | solution.py:492
  29.1 11.6 %collective-permute-start.5 = (f32[776,128]{1,0:T(8,128)S(1)}, f32[776,128]{1,0:T(8,128)S(1)}, u32[]{:S(2)}, u32[]{:S(2)}) collective-permute-start(f32[776,128]{1,0:T(8,128)S(1)} %collective-permute-done.3.refs_4_), channel_id=1, source_target_pairs={{4,0},{5,1},{8,4},{9,5},{12,8},{13,9},{14,12},{15,13},{10,14},{11,... | collective-permute-start | bytes 1191944 | tf_op jit(solution)/shard_map/ppermute | solution.py:485
  29.7 11.3 %collective-permute-start.4 = (f32[776,128]{1,0:T(8,128)S(1)}, f32[776,128]{1,0:T(8,128)S(1)}, u32[]{:S(2)}, u32[]{:S(2)}) collective-permute-start(f32[776,128]{1,0:T(8,128)S(1)} %collective-permute-done.2.refs_3_), channel_id=1, source_target_pairs={{0,4},{1,5},{4,8},{5,9},{8,12},{9,13},{12,14},{13,15},{14,10},{15,... | collective-permute-start | bytes 1191944 | tf_op jit(solution)/shard_map/ppermute | solution.py:484
  40.8 12.8 %copy-start.1 = (f32[776,128]{1,0:T(8,128)}, f32[776,128]{1,0:T(8,128)S(1)}, u32[]{:S(2)}) copy-start(f32[776,128]{1,0:T(8,128)S(1)} %collective-permute-done.5.refs_6_) | copy-start | bytes 1191940
  41.0 12.5 %copy-start.2 = (f32[776,128]{1,0:T(8,128)}, f32[776,128]{1,0:T(8,128)S(1)}, u32[]{:S(2)}) copy-start(f32[776,128]{1,0:T(8,128)S(1)} %collective-permute-done.4.refs_5_) | copy-start | bytes 1191940
  42.0 11.5 %collective-permute-start.9 = (f32[1552,128]{1,0:T(8,128)}, f32[1552,128]{1,0:T(8,128)}, u32[]{:S(2)}, u32[]{:S(2)}) collective-permute-start(f32[1552,128]{1,0:T(8,128)} %pad_maximum_fusion), channel_id=1, source_target_pairs={{0,1},{1,0},{2,3},{3,2},{4,5},{5,4},{6,7},{7,6},{8,9},{9,8},{10,11... | collective-permute-start | bytes 2383880 | tf_op jit(solution)/shard_map/ppermute | solution.py:492
  42.0 8.6 %collective-permute-start.7 = (f32[392,128]{1,0:T(8,128)S(1)}, f32[392,128]{1,0:T(8,128)S(1)}, u32[]{:S(2)}, u32[]{:S(2)}) collective-permute-start(f32[392,128]{1,0:T(8,128)S(1)} %slice.13), channel_id=1, source_target_pairs={{4,0},{5,1},{8,4},{9,5},{12,8},{13,9},{14,12},{15,13},{10,14},{11,... | collective-permute-start | bytes 602120 | tf_op jit(solution)/shard_map/ppermute | solution.py:481
  43.5 7.1 %collective-permute-start.6 = (f32[384,128]{1,0:T(8,128)S(1)}, f32[384,128]{1,0:T(8,128)S(1)}, u32[]{:S(2)}, u32[]{:S(2)}) collective-permute-start(f32[384,128]{1,0:T(8,128)S(1)} %slice.12), channel_id=1, source_target_pairs={{0,4},{1,5},{4,8},{5,9},{8,12},{9,13},{12,14},{13,15},{14,10},{15,... | collective-permute-start | bytes 589832 | tf_op jit(solution)/shard_map/ppermute | solution.py:480
  50.6 3.0 %copy-start.9 = (f32[384,128]{1,0:T(8,128)}, f32[384,128]{1,0:T(8,128)S(1)}, u32[]{:S(2)}) copy-start(f32[384,128]{1,0:T(8,128)S(1)} %collective-permute-done.6.refs_7_) | copy-start | bytes 589828
  50.6 3.0 %copy-start.8 = (f32[392,128]{1,0:T(8,128)}, f32[392,128]{1,0:T(8,128)S(1)}, u32[]{:S(2)}) copy-start(f32[392,128]{1,0:T(8,128)S(1)} %collective-permute-done.7.refs_8_) | copy-start | bytes 602116
  51.5 2.1 %collective-permute-start.10 = (f32[776,128]{1,0:T(8,128)}, f32[776,128]{1,0:T(8,128)}, u32[]{:S(2)}, u32[]{:S(2)}) collective-permute-start(f32[776,128]{1,0:T(8,128)} %pad_maximum_fusion.2), channel_id=1, source_target_pairs={{0,1},{1,0},{2,3},{3,2},{4,5},{5,4},{6,7},{7,6},{8,9},{9,8},{10,11... | collective-permute-start | bytes 1191944 | tf_op jit(solution)/shard_map/ppermute | solution.py:492
  53.6 1.3 copy-start
  62.3 0.8 copy-start.10
  165.2 7.6 %collective-permute-start.11 = (f32[16,2,256,128]{3,2,1,0:T(8,128)}, f32[16,2,256,128]{3,2,1,0:T(8,128)}, u32[]{:S(2)}, u32[]{:S(2)}) collective-permute-start(f32[16,2,256,128]{3,2,1,0:T(8,128)} %get-tuple-element.8), channel_id=1, source_target_pairs={{0,1},{1,0},{2,3},{3,2},{4,5},{5,4},{6,7},{7,6},{8,9},{9,8},{10,11... | collective-permute-start | bytes 12582920 | tf_op jit(solution)/shard_map/ppermute | solution.py:561

commit v5 on v4

--- a/solution.py
+++ b/solution.py
@@ -16,6 +16,7 @@
 FB = GRID // LANES
 BATCH = 32
 UNROLL = 8
+QUARTERS = 4
 RADIX = 8
 REST = FB // RADIX
 CORES = 2
@@ -61,7 +62,7 @@
     first = np.arange(FB)[:, None, None]
     outer = np.arange(LANES)[None, :, None]
     inner = np.arange(LANES)[None, None, :]
-    return embed(inner * (first + FB * outer))
+    return np.concatenate(embed(inner * (first + FB * outer)), axis=1)
 
 
 def even_fit(function, reach, degree):
@@ -312,12 +313,12 @@
                     ]
 
     def several(i, _):
-        done = [(2 * i + k, transform(2 * i + k)) for k in range(2)]
+        done = [(4 * i + k, transform(4 * i + k)) for k in range(4)]
         for item in done:
             place(*item)
         return 0
 
-    lax.fori_loop(0, RADIX // 2, several, 0)
+    lax.fori_loop(0, RADIX // 4, several, 0)
 
 
 def spectra_rows(raws, info, order, chips, columns, bits, scale):
@@ -359,25 +360,27 @@
 
 def columns_kernel(info, *refs):
     pieces = refs[:CORES]
-    high_hbm, low_hbm, out_hbm, out, x, high, low, piece_sem, tab_sem, out_sem = refs[CORES:]
+    table_hbm, out_hbm, out, x, table, piece_sem, tab_sem, out_sem = refs[CORES:]
     me = info[0]
     per_device, _, columns, _ = pieces[0].shape
-    copies = [
-        pltpu.make_async_copy(
-            pieces[slot],
-            x.at[pl.ds(((me + CORES - slot) % CORES) * per_device, per_device)],
-            piece_sem.at[slot],
-        )
-        for slot in range(CORES)
-    ]
-    tab_copies = [
-        pltpu.make_async_copy(high_hbm, high, tab_sem.at[0]),
-        pltpu.make_async_copy(low_hbm, low, tab_sem.at[1]),
-    ]
-    for copy in copies + tab_copies:
-        copy.start()
-    for copy in copies:
-        copy.wait()
+    quarter = columns // QUARTERS
+
+    def fetch(i):
+        at = pl.ds(pl.multiple_of(i * quarter, quarter), quarter)
+        return [
+            pltpu.make_async_copy(
+                pieces[slot].at[:, :, at],
+                x.at[pl.ds(((me + CORES - slot) % CORES) * per_device, per_device), :, at],
+                piece_sem.at[slot, i],
+            )
+            for slot in range(CORES)
+        ]
+
+    tab_copy = pltpu.make_async_copy(table_hbm, table, tab_sem.at[0])
+    for i in range(QUARTERS):
+        for copy in fetch(i):
+            copy.start()
+    tab_copy.start()
 
     def butterflies(i, _):
         at = pl.ds(pl.multiple_of(i * 8, 8), 8)
@@ -390,14 +393,17 @@
             x[r, 1, at, :] = imag
         return 0
 
-    lax.fori_loop(0, columns // 8, butterflies, 0)
-    for copy in tab_copies:
-        copy.wait()
+    for i in range(QUARTERS):
+        for copy in fetch(i):
+            copy.wait()
+        lax.fori_loop(i * quarter // 8, (i + 1) * quarter // 8, butterflies, 0)
+    tab_copy.wait()
 
     def transform(r):
         z_high, z_low = split(jnp.concatenate([x[r, 0], x[r, 1]], axis=1))
-        f_high = high[r]
-        return dot_nt(f_high, z_high) + dot_nt(low[r], z_high) + dot_nt(f_high, z_low)
+        f = table[r]
+        y = dot_nt(f, z_high)
+        return y[: 2 * LANES] + y[2 * LANES :] + dot_nt(f[: 2 * LANES], z_low)
 
     def store(i):
         at = pl.ds(pl.multiple_of(i * UNROLL, UNROLL), UNROLL)
@@ -433,7 +439,7 @@
 
 
 def column_transform(pieces, info, columns):
-    high, low = column_table()
+    table = column_table()
     anywhere = pl.BlockSpec(memory_space=pl.ANY)
 
     return pl.pallas_call(
@@ -441,22 +447,21 @@
         grid_spec=pltpu.PrefetchScalarGridSpec(
             num_scalar_prefetch=1,
             grid=(1,),
-            in_specs=[anywhere] * (CORES + 2),
+            in_specs=[anywhere] * (CORES + 1),
             out_specs=anywhere,
             scratch_shapes=[
                 pltpu.VMEM((2, columns // LANES, LANES, FB, LANES), F32),
                 pltpu.VMEM((FB, 2, columns, LANES), F32),
-                pltpu.VMEM(high.shape, BF16),
-                pltpu.VMEM(low.shape, BF16),
-                pltpu.SemaphoreType.DMA((CORES,)),
-                pltpu.SemaphoreType.DMA((2,)),
+                pltpu.VMEM(table.shape, BF16),
+                pltpu.SemaphoreType.DMA((CORES, QUARTERS)),
+                pltpu.SemaphoreType.DMA((1,)),
                 pltpu.SemaphoreType.DMA((columns // LANES,)),
             ],
         ),
         out_shape=jax.ShapeDtypeStruct((2, LANES, FB, columns), F32),
         compiler_params=pltpu.CompilerParams(vmem_limit_bytes=62 * 1024 * 1024),
         name="column_transform",
-    )(info, *pieces, jnp.asarray(high), jnp.asarray(low))
+    )(info, *pieces, jnp.asarray(table))
 
 
 def chip_cycle(chips):
@@ -519,6 +524,7 @@
         out_specs=pl.BlockSpec(memory_space=pltpu.VMEM),
         scratch_shapes=[pltpu.SemaphoreType.DMA((len(spots),))],
         out_shape=jax.ShapeDtypeStruct((len(spots), tag_rows, LANES), F32),
+        compiler_params=pltpu.CompilerParams(vmem_limit_bytes=62 * 1024 * 1024),
         name="tags",
     )(*arrays)
     return tags.reshape(len(spots), -1)[:, :count].astype(jnp.int32)

time: 194 us -> 191 us (0.985)
  Pallas kernels: 124 us -> 117 us
  starting transfers between devices: 9.45 us -> 12.6 us
    pallas_call x1, Pallas kernels: 102 us -> 97.4 us  [spectra_rows(): pl.pallas_call(functools.partial(spectra_rows_kernel, blocks, bits, scale...]
    ppermute x1, starting transfers between devices: 0.18 us -> 3.22 us  [per_device(): received = [pieces[0], lax.ppermute(pieces[1], 'wide', swap)]]
    pallas_call x1, Pallas kernels: 20.4 us -> 18.3 us  [column_transform(): pl.pallas_call(columns_kernel, grid_spec=pltpu.PrefetchScalarGridSpec(num...]
    unnamed x28 -> x30, local copies, waits for them, and re-layouts: 5.9 us -> 7.06 us
  transfers between devices with their start and end apart: 12 -> 12, of which waited for: 8 -> 8; matrix products, arithmetic and copies ran while one was open for 3% -> 2% of each run, Pallas kernels for 0% -> 0%
where the time goes in v5:
time: 191 us; the launch traced here: 189 us
  Pallas kernels  117 us (61%)
  waiting for transfers between devices  40.6 us (21%)
  starting transfers between devices  12.6 us (7%)
  other arithmetic  10.4 us (5%)
  local copies, waits for them, and re-layouts  7.99 us (4%)
    pallas_call x1, Pallas kernels, spectra_rows(): pl.pallas_call(functools.partial(spectra_rows_kernel, blocks, bits, scale...  97.4 us
    pallas_call x1, Pallas kernels, column_transform(): pl.pallas_call(columns_kernel, grid_spec=pltpu.PrefetchScalarGridSpec(num...  18.3 us
    ppermute x3, waiting for transfers between devices, gather_all(): forth = lax.ppermute(forth, 'wide', ahead)  14.8 us
    ppermute x3, waiting for transfers between devices, gather_all(): other = lax.ppermute(other, 'wide', back)  10.8 us
    ppermute x1, waiting for transfers between devices, per_device(): received = [pieces[0], lax.ppermute(pieces[1], 'wide', swap)]  7.13 us
    unnamed x30, local copies, waits for them, and re-layouts  7.06 us
    ppermute x3, starting transfers between devices, gather_all(): forth = lax.ppermute(forth, 'wide', ahead)  6.35 us
    ppermute x1, waiting for transfers between devices, gather_all(): upper = lax.ppermute(forth[:half], 'wide', ahead)  6.04 us
  transfers between devices with their start and end apart: 12, of which 8 were waited for; matrix products, arithmetic and copies ran while one was open for 2% of the time, Pallas kernels for 0%

profile of v5, /device:TPU:0, one launch (start us, length us, event | category | flops | bytes accessed | tf_op | source)
XLA Modules:
  0.0 188.9 jit_solution(3269317463803325705)
XLA Ops:
  1.5 1.1 broadcast_select_fusion
  2.6 1.1 pad_maximum_fusion.3
  3.7 3.1 %collective-permute-start = (f32[776,128]{1,0:T(8,128)S(1)}, f32[776,128]{1,0:T(8,128)S(1)}, u32[]{:S(2)}, u32[]{:S(2)}) collective-permute-start(f32[776,128]{1,0:T(8,128)S(1)} %pad_maximum_fusion.1.refs_0_), channel_id=1, source_target_pairs={{0,4},{1,5},{4,8},{5,9},{8,12},{9,13},{12,14},{13,15},{14,10},{15,... | collective-permute-start | bytes 1191944 | tf_op jit(solution)/shard_map/ppermute | solution.py:489
  6.8 9.1 %collective-permute-done.refs_1_ = f32[776,128]{1,0:T(8,128)S(1)} collective-permute-done((f32[776,128]{1,0:T(8,128)S(1)}, f32[776,128]{1,0:T(8,128)S(1)}, u32[]{:S(2)}, u32[]{:S(2)}) %collective-permute-start) | collective-permute-done | bytes 397344 | tf_op jit(solution)/shard_map/ppermute | solution.py:489
  16.0 1.8 collective-permute-start.2
  20.9 5.4 %collective-permute-done.2.refs_3_ = f32[776,128]{1,0:T(8,128)S(1)} collective-permute-done((f32[776,128]{1,0:T(8,128)S(1)}, f32[776,128]{1,0:T(8,128)S(1)}, u32[]{:S(2)}, u32[]{:S(2)}) %collective-permute-start.2) | collective-permute-done | bytes 397344 | tf_op jit(solution)/shard_map/ppermute | solution.py:489
  26.3 0.8 constant_dynamic-update-slice_fusion.1
  27.2 1.2 collective-permute-done.3.refs_4_
  28.3 0.8 constant_dynamic-update-slice_fusion
  29.7 1.5 collective-permute-start.4
  31.2 9.6 %collective-permute-done.5.refs_6_ = f32[776,128]{1,0:T(8,128)S(1)} collective-permute-done((f32[776,128]{1,0:T(8,128)S(1)}, f32[776,128]{1,0:T(8,128)S(1)}, u32[]{:S(2)}, u32[]{:S(2)}) %collective-permute-start.5) | collective-permute-done | bytes 397344 | tf_op jit(solution)/shard_map/ppermute | solution.py:490
  41.6 1.1 collective-permute-start.7
  42.7 1.0 collective-permute-start.6
  43.7 6.0 %collective-permute-done.6.refs_7_ = f32[384,128]{1,0:T(8,128)S(1)} collective-permute-done((f32[384,128]{1,0:T(8,128)S(1)}, f32[384,128]{1,0:T(8,128)S(1)}, u32[]{:S(2)}, u32[]{:S(2)}) %collective-permute-start.6) | collective-permute-done | bytes 196640 | tf_op jit(solution)/shard_map/ppermute | solution.py:485
  49.8 0.8 pad_maximum_fusion.2
  50.7 1.9 collective-permute-done.10.refs_11_
  53.3 1.3 copy-done
  54.6 1.5 tags.1
  56.1 0.9 copy.12
  57.1 4.9 %sort.7.order = s32[3072]{0:T(1024)S(1)} sort(s32[3072]{0:T(1024)S(1)} %reshape.46), dimensions={0}, to_apply=%region_0.1 | sort | flops 36864 | bytes 24576 | tf_op jit(solution)/shard_map/sort | solution.py:557
  62.9 97.4 %spectra_rows.1 = (f32[16,2,256,128]{3,2,1,0:T(8,128)}, f32[16,2,256,128]{3,2,1,0:T(8,128)}) custom-call(s32[11]{0:T(128)} %pad_add_fusion.info, s32[3072]{0:T(1024)} %copy-done.11, f32[776,128]{1,0:T(8,128)} %copy-done.3, f32[776,128]{1,0:T(8,128)} %copy-done.4, f32[776,128]{1,0:T(8,128)} %copy-done.5, f32[776,128]{1,0:T(8,128)} %copy-done.6, ...), custom_call_target="tpu_custom_call" | custom-call | tf_op jit(solution)/shard_map/spectra_rows/pallas_call | solution.py:332
  160.2 3.2 %collective-permute-start.11 = (f32[16,2,256,128]{3,2,1,0:T(8,128)}, f32[16,2,256,128]{3,2,1,0:T(8,128)}, u32[]{:S(2)}, u32[]{:S(2)}) collective-permute-start(f32[16,2,256,128]{3,2,1,0:T(8,128)} %get-tuple-element.8), channel_id=1, source_target_pairs={{0,1},{1,0},{2,3},{3,2},{4,5},{5,4},{6,7},{7,6},{8,9},{9,8},{10,11... | collective-permute-start | bytes 12582920 | tf_op jit(solution)/shard_map/ppermute | solution.py:567
  163.5 7.1 %collective-permute-done.11.refs_1_ = f32[16,2,256,128]{3,2,1,0:T(8,128)} collective-permute-done((f32[16,2,256,128]{3,2,1,0:T(8,128)}, f32[16,2,256,128]{3,2,1,0:T(8,128)}, u32[]{:S(2)}, u32[]{:S(2)}) %collective-permute-start.11) | collective-permute-done | bytes 4194336 | tf_op jit(solution)/shard_map/ppermute | solution.py:567
  170.6 18.3 %column_transform.1 = f32[2,128,32,256]{3,2,1,0:T(8,128)} custom-call(s32[11]{0:T(128)} %pad_add_fusion.info, f32[16,2,256,128]{3,2,1,0:T(8,128)} %get-tuple-element.7.refs_0_, f32[16,2,256,128]{3,2,1,0:T(8,128)} %collective-permute-done.11.refs_1_, bf16[32,512,256]{2,1,0:T(8,128)(2,1)} %constant.113.clone.refs_2_), custom_call_target="tpu_custom_call" | custom-call | tf_op jit(solution)/shard_map/column_transform/pallas_call | solution.py:445
  (52 shorter events, 7.8 us)
Async XLA Ops:
  3.7 37.1 %copy-start.3 = (f32[776,128]{1,0:T(8,128)}, f32[776,128]{1,0:T(8,128)S(1)}, u32[]{:S(2)}) copy-start(f32[776,128]{1,0:T(8,128)S(1)} %pad_maximum_fusion.1.refs_0_) | copy-start | bytes 1191940
  3.7 12.2 %collective-permute-start = (f32[776,128]{1,0:T(8,128)S(1)}, f32[776,128]{1,0:T(8,128)S(1)}, u32[]{:S(2)}, u32[]{:S(2)}) collective-permute-start(f32[776,128]{1,0:T(8,128)S(1)} %pad_maximum_fusion.1.refs_0_), channel_id=1, source_target_pairs={{0,4},{1,5},{4,8},{5,9},{8,12},{9,13},{12,14},{13,15},{14,10},{15,... | collective-permute-start | bytes 1191944 | tf_op jit(solution)/shard_map/ppermute | solution.py:489
  6.8 11.7 %collective-permute-start.1 = (f32[776,128]{1,0:T(8,128)S(1)}, f32[776,128]{1,0:T(8,128)S(1)}, u32[]{:S(2)}, u32[]{:S(2)}) collective-permute-start(f32[776,128]{1,0:T(8,128)S(1)} %pad_maximum_fusion.1.refs_0_), channel_id=1, source_target_pairs={{4,0},{5,1},{8,4},{9,5},{12,8},{13,9},{14,12},{15,13},{10,14},{11,... | collective-permute-start | bytes 1191944 | tf_op jit(solution)/shard_map/ppermute | solution.py:490
  16.0 24.8 %copy-start.4 = (f32[776,128]{1,0:T(8,128)}, f32[776,128]{1,0:T(8,128)S(1)}, u32[]{:S(2)}) copy-start(f32[776,128]{1,0:T(8,128)S(1)} %collective-permute-done.refs_1_) | copy-start | bytes 1191940
  16.0 10.4 %collective-permute-start.2 = (f32[776,128]{1,0:T(8,128)S(1)}, f32[776,128]{1,0:T(8,128)S(1)}, u32[]{:S(2)}, u32[]{:S(2)}) collective-permute-start(f32[776,128]{1,0:T(8,128)S(1)} %collective-permute-done.refs_1_), channel_id=1, source_target_pairs={{0,4},{1,5},{4,8},{5,9},{8,12},{9,13},{12,14},{13,15},{14,10},{15,... | collective-permute-start | bytes 1191944 | tf_op jit(solution)/shard_map/ppermute | solution.py:489
  18.5 22.2 %copy-start.5 = (f32[776,128]{1,0:T(8,128)}, f32[776,128]{1,0:T(8,128)S(1)}, u32[]{:S(2)}) copy-start(f32[776,128]{1,0:T(8,128)S(1)} %collective-permute-done.1.refs_2_) | copy-start | bytes 1191940
  18.5 9.8 %collective-permute-start.3 = (f32[776,128]{1,0:T(8,128)S(1)}, f32[776,128]{1,0:T(8,128)S(1)}, u32[]{:S(2)}, u32[]{:S(2)}) collective-permute-start(f32[776,128]{1,0:T(8,128)S(1)} %collective-permute-done.1.refs_2_), channel_id=1, source_target_pairs={{4,0},{5,1},{8,4},{9,5},{12,8},{13,9},{14,12},{15,13},{10,14},{11,... | collective-permute-start | bytes 1191944 | tf_op jit(solution)/shard_map/ppermute | solution.py:490
  26.3 24.3 %copy-start.6 = (f32[776,128]{1,0:T(8,128)}, f32[776,128]{1,0:T(8,128)S(1)}, u32[]{:S(2)}) copy-start(f32[776,128]{1,0:T(8,128)S(1)} %collective-permute-done.2.refs_3_) | copy-start | bytes 1191940
  28.3 22.3 %copy-start.7 = (f32[776,128]{1,0:T(8,128)}, f32[776,128]{1,0:T(8,128)S(1)}, u32[]{:S(2)}) copy-start(f32[776,128]{1,0:T(8,128)S(1)} %collective-permute-done.3.refs_4_) | copy-start | bytes 1191940
  29.1 24.2 %collective-permute-start.8 = (f32[3880,128]{1,0:T(8,128)}, f32[3880,128]{1,0:T(8,128)S(1)}, u32[]{:S(2)}, u32[]{:S(2)}) collective-permute-start(f32[3880,128]{1,0:T(8,128)} %constant_dynamic-update-slice_fusion), channel_id=1, source_target_pairs={{0,1},{1,0},{2,3},{3,2},{4,5},{5,4},{6,7},{7,6},{8,9},{9,8},{10,11... | collective-permute-start | bytes 5959688 | tf_op jit(solution)/shard_map/ppermute | solution.py:497
  29.2 11.6 %collective-permute-start.5 = (f32[776,128]{1,0:T(8,128)S(1)}, f32[776,128]{1,0:T(8,128)S(1)}, u32[]{:S(2)}, u32[]{:S(2)}) collective-permute-start(f32[776,128]{1,0:T(8,128)S(1)} %collective-permute-done.3.refs_4_), channel_id=1, source_target_pairs={{4,0},{5,1},{8,4},{9,5},{12,8},{13,9},{14,12},{15,13},{10,14},{11,... | collective-permute-start | bytes 1191944 | tf_op jit(solution)/shard_map/ppermute | solution.py:490
  29.7 11.3 %collective-permute-start.4 = (f32[776,128]{1,0:T(8,128)S(1)}, f32[776,128]{1,0:T(8,128)S(1)}, u32[]{:S(2)}, u32[]{:S(2)}) collective-permute-start(f32[776,128]{1,0:T(8,128)S(1)} %collective-permute-done.2.refs_3_), channel_id=1, source_target_pairs={{0,4},{1,5},{4,8},{5,9},{8,12},{9,13},{12,14},{13,15},{14,10},{15,... | collective-permute-start | bytes 1191944 | tf_op jit(solution)/shard_map/ppermute | solution.py:489
  40.8 0.8 copy-start.1
  41.0 1.6 copy-start.2
  41.1 12.2 %collective-permute-start.9 = (f32[1552,128]{1,0:T(8,128)S(1)}, f32[1552,128]{1,0:T(8,128)}, u32[]{:S(2)}, u32[]{:S(2)}) collective-permute-start(f32[1552,128]{1,0:T(8,128)S(1)} %pad_maximum_fusion), channel_id=1, source_target_pairs={{0,1},{1,0},{2,3},{3,2},{4,5},{5,4},{6,7},{7,6},{8,9},{9,8},{10,11... | collective-permute-start | bytes 2383880 | tf_op jit(solution)/shard_map/ppermute | solution.py:497
  41.6 8.2 %collective-permute-start.7 = (f32[392,128]{1,0:T(8,128)S(1)}, f32[392,128]{1,0:T(8,128)S(1)}, u32[]{:S(2)}, u32[]{:S(2)}) collective-permute-start(f32[392,128]{1,0:T(8,128)S(1)} %slice.13), channel_id=1, source_target_pairs={{4,0},{5,1},{8,4},{9,5},{12,8},{13,9},{14,12},{15,13},{10,14},{11,... | collective-permute-start | bytes 602120 | tf_op jit(solution)/shard_map/ppermute | solution.py:486
  42.7 7.1 %collective-permute-start.6 = (f32[384,128]{1,0:T(8,128)S(1)}, f32[384,128]{1,0:T(8,128)S(1)}, u32[]{:S(2)}, u32[]{:S(2)}) collective-permute-start(f32[384,128]{1,0:T(8,128)S(1)} %slice.12), channel_id=1, source_target_pairs={{0,4},{1,5},{4,8},{5,9},{8,12},{9,13},{12,14},{13,15},{14,10},{15,... | collective-permute-start | bytes 589832 | tf_op jit(solution)/shard_map/ppermute | solution.py:485
  49.8 0.9 copy-start.9
  49.8 0.9 copy-start.8
  50.6 1.9 %collective-permute-start.10 = (f32[776,128]{1,0:T(8,128)}, f32[776,128]{1,0:T(8,128)S(1)}, u32[]{:S(2)}, u32[]{:S(2)}) collective-permute-start(f32[776,128]{1,0:T(8,128)} %pad_maximum_fusion.2), channel_id=1, source_target_pairs={{0,1},{1,0},{2,3},{3,2},{4,5},{5,4},{6,7},{7,6},{8,9},{9,8},{10,11... | collective-permute-start | bytes 1191944 | tf_op jit(solution)/shard_map/ppermute | solution.py:497
  52.6 0.7 copy-start.10
  53.3 1.3 copy-start
  62.0 0.8 copy-start.11
  160.2 10.3 %collective-permute-start.11 = (f32[16,2,256,128]{3,2,1,0:T(8,128)}, f32[16,2,256,128]{3,2,1,0:T(8,128)}, u32[]{:S(2)}, u32[]{:S(2)}) collective-permute-start(f32[16,2,256,128]{3,2,1,0:T(8,128)} %get-tuple-element.8), channel_id=1, source_target_pairs={{0,1},{1,0},{2,3},{3,2},{4,5},{5,4},{6,7},{7,6},{8,9},{9,8},{10,11... | collective-permute-start | bytes 12582920 | tf_op jit(solution)/shard_map/ppermute | solution.py:567

commit v6 on v5

--- a/solution.py
+++ b/solution.py
@@ -490,7 +490,7 @@
             other = lax.ppermute(other, "wide", back)
             found.append([forth, other])
     swapped = []
-    for some in (found[:-2], found[-2:-1], found[-1:]):
+    for some in (found[:-1], found[-1:]):
         arrays = [x for each in some for x in each]
         if arrays:
             together = jnp.concatenate(arrays, axis=0) if len(arrays) > 1 else arrays[0]

time: 191 us -> 185 us (0.969)
  waiting for transfers between devices: 40.6 us -> 35.8 us
  Pallas kernels: 117 us -> 121 us
  starting transfers between devices: 12.6 us -> 9.41 us
    ppermute x3, waiting for transfers between devices: 10.8 us -> 0.84 us  [gather_all(): other = lax.ppermute(other, 'wide', back)]
    ppermute x3, waiting for transfers between devices: 14.8 us -> 20.5 us  [gather_all(): forth = lax.ppermute(forth, 'wide', ahead)]
    pallas_call x1, Pallas kernels: 97.4 us -> 101 us  [spectra_rows(): pl.pallas_call(functools.partial(spectra_rows_kernel, blocks, bits, scale...]
    ppermute x1, starting transfers between devices: 3.22 us -> 0.07 us  [per_device(): received = [pieces[0], lax.ppermute(pieces[1], 'wide', swap)]]
  transfers between devices with their start and end apart: 12 -> 11, of which waited for: 8 -> 7; matrix products, arithmetic and copies ran while one was open for 2% -> 3% of each run, Pallas kernels for 0% -> 0%
where the time goes in v6:
time: 185 us
  Pallas kernels  121 us (65%)
  waiting for transfers between devices  35.8 us (19%)
  other arithmetic  9.55 us (5%)
  starting transfers between devices  9.41 us (5%)
  local copies, waits for them, and re-layouts  8.42 us (5%)
    pallas_call x1, Pallas kernels, spectra_rows(): pl.pallas_call(functools.partial(spectra_rows_kernel, blocks, bits, scale...  101 us
    ppermute x3, waiting for transfers between devices, gather_all(): forth = lax.ppermute(forth, 'wide', ahead)  20.5 us
    pallas_call x1, Pallas kernels, column_transform(): pl.pallas_call(columns_kernel, grid_spec=pltpu.PrefetchScalarGridSpec(num...  18.3 us
    ppermute x1, waiting for transfers between devices, per_device(): received = [pieces[0], lax.ppermute(pieces[1], 'wide', swap)]  7.49 us
    unnamed x30, local copies, waits for them, and re-layouts  7.48 us
    ppermute x3, starting transfers between devices, gather_all(): forth = lax.ppermute(forth, 'wide', ahead)  6.35 us
    ppermute x1, waiting for transfers between devices, gather_all(): upper = lax.ppermute(forth[:half], 'wide', ahead)  5.87 us
    sort x1, other arithmetic, per_device(): order = lax.sort(word.reshape(-1).astype(jnp.int32), is_stable=False)  4.9 us
  transfers between devices with their start and end apart: 11, of which 7 were waited for; matrix products, arithmetic and copies ran while one was open for 3% of the time, Pallas kernels for 0%

profile of v6, /device:TPU:0, one launch (start us, length us, event | category | flops | bytes accessed | tf_op | source)
XLA Modules:
  0.0 184.6 jit_solution(9015240976860709976)
XLA Ops:
  1.5 1.1 broadcast_select_fusion
  2.6 1.1 pad_maximum_fusion.2
  3.7 3.1 %collective-permute-start = (f32[776,128]{1,0:T(8,128)S(1)}, f32[776,128]{1,0:T(8,128)S(1)}, u32[]{:S(2)}, u32[]{:S(2)}) collective-permute-start(f32[776,128]{1,0:T(8,128)S(1)} %pad_maximum_fusion.refs_0_), channel_id=1, source_target_pairs={{0,4},{1,5},{4,8},{5,9},{8,12},{9,13},{12,14},{13,15},{14,10},{15,... | collective-permute-start | bytes 1191944 | tf_op jit(solution)/shard_map/ppermute | solution.py:489
  6.8 9.1 %collective-permute-done.refs_1_ = f32[776,128]{1,0:T(8,128)S(1)} collective-permute-done((f32[776,128]{1,0:T(8,128)S(1)}, f32[776,128]{1,0:T(8,128)S(1)}, u32[]{:S(2)}, u32[]{:S(2)}) %collective-permute-start) | collective-permute-done | bytes 397344 | tf_op jit(solution)/shard_map/ppermute | solution.py:489
  16.0 1.8 collective-permute-start.2
  19.4 7.0 %collective-permute-done.2.refs_3_ = f32[776,128]{1,0:T(8,128)S(1)} collective-permute-done((f32[776,128]{1,0:T(8,128)S(1)}, f32[776,128]{1,0:T(8,128)S(1)}, u32[]{:S(2)}, u32[]{:S(2)}) %collective-permute-start.2) | collective-permute-done | bytes 397344 | tf_op jit(solution)/shard_map/ppermute | solution.py:489
  26.3 1.5 collective-permute-start.4
  29.2 0.8 constant_dynamic-update-slice_fusion.4
  29.9 0.8 constant_dynamic-update-slice_fusion.3
  30.7 0.8 constant_dynamic-update-slice_fusion.2
  31.5 4.3 %collective-permute-done.4.refs_5_ = f32[776,128]{1,0:T(8,128)S(1)} collective-permute-done((f32[776,128]{1,0:T(8,128)S(1)}, f32[776,128]{1,0:T(8,128)S(1)}, u32[]{:S(2)}, u32[]{:S(2)}) %collective-permute-start.4) | collective-permute-done | bytes 397344 | tf_op jit(solution)/shard_map/ppermute | solution.py:489
  35.8 0.8 constant_dynamic-update-slice_fusion.1
  36.6 0.8 collective-permute-done.5.refs_6_
  37.5 0.8 constant_dynamic-update-slice_fusion
  38.4 0.9 collective-permute-start.7
  39.3 1.2 collective-permute-start.6
  40.5 5.9 %collective-permute-done.6.refs_7_ = f32[384,128]{1,0:T(8,128)S(1)} collective-permute-done((f32[384,128]{1,0:T(8,128)S(1)}, f32[384,128]{1,0:T(8,128)S(1)}, u32[]{:S(2)}, u32[]{:S(2)}) %collective-permute-start.6) | collective-permute-done | bytes 196640 | tf_op jit(solution)/shard_map/ppermute | solution.py:485
  47.1 1.1 collective-permute-done.9.refs_10_
  49.0 1.5 tags.1
  50.5 0.9 copy.12
  51.5 4.9 %sort.7.order = s32[3072]{0:T(1024)S(1)} sort(s32[3072]{0:T(1024)S(1)} %reshape.46), dimensions={0}, to_apply=%region_0.1 | sort | flops 36864 | bytes 24576 | tf_op jit(solution)/shard_map/sort | solution.py:557
  57.3 101.4 %spectra_rows.1 = (f32[16,2,256,128]{3,2,1,0:T(8,128)}, f32[16,2,256,128]{3,2,1,0:T(8,128)}) custom-call(s32[11]{0:T(128)} %pad_add_fusion.info, s32[3072]{0:T(1024)} %copy-done.10, f32[776,128]{1,0:T(8,128)} %copy-done.2, f32[776,128]{1,0:T(8,128)} %copy-done.3, f32[776,128]{1,0:T(8,128)} %copy-done.4, f32[776,128]{1,0:T(8,128)} %copy-done.5, ...), custom_call_target="tpu_custom_call" | custom-call | tf_op jit(solution)/shard_map/spectra_rows/pallas_call | solution.py:332
  158.8 7.5 %collective-permute-done.10.refs_1_ = f32[16,2,256,128]{3,2,1,0:T(8,128)} collective-permute-done((f32[16,2,256,128]{3,2,1,0:T(8,128)}, f32[16,2,256,128]{3,2,1,0:T(8,128)}, u32[]{:S(2)}, u32[]{:S(2)}) %collective-permute-start.10) | collective-permute-done | bytes 4194336 | tf_op jit(solution)/shard_map/ppermute | solution.py:567
  166.3 18.3 %column_transform.1 = f32[2,128,32,256]{3,2,1,0:T(8,128)} custom-call(s32[11]{0:T(128)} %pad_add_fusion.info, f32[16,2,256,128]{3,2,1,0:T(8,128)} %get-tuple-element.7.refs_0_, f32[16,2,256,128]{3,2,1,0:T(8,128)} %collective-permute-done.10.refs_1_, bf16[32,512,256]{2,1,0:T(8,128)(2,1)} %constant.113.clone.refs_2_), custom_call_target="tpu_custom_call" | custom-call | tf_op jit(solution)/shard_map/column_transform/pallas_call | solution.py:445
  (49 shorter events, 7.0 us)
Async XLA Ops:
  3.7 34.6 %copy-start.2 = (f32[776,128]{1,0:T(8,128)}, f32[776,128]{1,0:T(8,128)S(1)}, u32[]{:S(2)}) copy-start(f32[776,128]{1,0:T(8,128)S(1)} %pad_maximum_fusion.refs_0_) | copy-start | bytes 1191940
  3.7 12.2 %collective-permute-start = (f32[776,128]{1,0:T(8,128)S(1)}, f32[776,128]{1,0:T(8,128)S(1)}, u32[]{:S(2)}, u32[]{:S(2)}) collective-permute-start(f32[776,128]{1,0:T(8,128)S(1)} %pad_maximum_fusion.refs_0_), channel_id=1, source_target_pairs={{0,4},{1,5},{4,8},{5,9},{8,12},{9,13},{12,14},{13,15},{14,10},{15,... | collective-permute-start | bytes 1191944 | tf_op jit(solution)/shard_map/ppermute | solution.py:489
  6.8 10.9 %collective-permute-start.1 = (f32[776,128]{1,0:T(8,128)S(1)}, f32[776,128]{1,0:T(8,128)S(1)}, u32[]{:S(2)}, u32[]{:S(2)}) collective-permute-start(f32[776,128]{1,0:T(8,128)S(1)} %pad_maximum_fusion.refs_0_), channel_id=1, source_target_pairs={{4,0},{5,1},{8,4},{9,5},{12,8},{13,9},{14,12},{15,13},{10,14},{11,... | collective-permute-start | bytes 1191944 | tf_op jit(solution)/shard_map/ppermute | solution.py:490
  16.0 22.4 %copy-start.3 = (f32[776,128]{1,0:T(8,128)}, f32[776,128]{1,0:T(8,128)S(1)}, u32[]{:S(2)}) copy-start(f32[776,128]{1,0:T(8,128)S(1)} %collective-permute-done.refs_1_) | copy-start | bytes 1191940
  16.0 10.4 %collective-permute-start.2 = (f32[776,128]{1,0:T(8,128)S(1)}, f32[776,128]{1,0:T(8,128)S(1)}, u32[]{:S(2)}, u32[]{:S(2)}) collective-permute-start(f32[776,128]{1,0:T(8,128)S(1)} %collective-permute-done.refs_1_), channel_id=1, source_target_pairs={{0,4},{1,5},{4,8},{5,9},{8,12},{9,13},{12,14},{13,15},{14,10},{15,... | collective-permute-start | bytes 1191944 | tf_op jit(solution)/shard_map/ppermute | solution.py:489
  17.8 20.6 %copy-start.4 = (f32[776,128]{1,0:T(8,128)}, f32[776,128]{1,0:T(8,128)S(1)}, u32[]{:S(2)}) copy-start(f32[776,128]{1,0:T(8,128)S(1)} %collective-permute-done.1.refs_2_) | copy-start | bytes 1191940
  17.8 10.8 %collective-permute-start.3 = (f32[776,128]{1,0:T(8,128)S(1)}, f32[776,128]{1,0:T(8,128)S(1)}, u32[]{:S(2)}, u32[]{:S(2)}) collective-permute-start(f32[776,128]{1,0:T(8,128)S(1)} %collective-permute-done.1.refs_2_), channel_id=1, source_target_pairs={{4,0},{5,1},{8,4},{9,5},{12,8},{13,9},{14,12},{15,13},{10,14},{11,... | collective-permute-start | bytes 1191944 | tf_op jit(solution)/shard_map/ppermute | solution.py:490
  26.3 20.1 %copy-start.5 = (f32[776,128]{1,0:T(8,128)}, f32[776,128]{1,0:T(8,128)S(1)}, u32[]{:S(2)}) copy-start(f32[776,128]{1,0:T(8,128)S(1)} %collective-permute-done.2.refs_3_) | copy-start | bytes 1191940
  26.3 9.5 %collective-permute-start.4 = (f32[776,128]{1,0:T(8,128)S(1)}, f32[776,128]{1,0:T(8,128)S(1)}, u32[]{:S(2)}, u32[]{:S(2)}) collective-permute-start(f32[776,128]{1,0:T(8,128)S(1)} %collective-permute-done.2.refs_3_), channel_id=1, source_target_pairs={{0,4},{1,5},{4,8},{5,9},{8,12},{9,13},{12,14},{13,15},{14,10},{15,... | collective-permute-start | bytes 1191944 | tf_op jit(solution)/shard_map/ppermute | solution.py:489
  28.6 17.9 %copy-start.6 = (f32[776,128]{1,0:T(8,128)}, f32[776,128]{1,0:T(8,128)S(1)}, u32[]{:S(2)}) copy-start(f32[776,128]{1,0:T(8,128)S(1)} %collective-permute-done.3.refs_4_) | copy-start | bytes 1191940
  28.6 8.9 %collective-permute-start.5 = (f32[776,128]{1,0:T(8,128)S(1)}, f32[776,128]{1,0:T(8,128)S(1)}, u32[]{:S(2)}, u32[]{:S(2)}) collective-permute-start(f32[776,128]{1,0:T(8,128)S(1)} %collective-permute-done.3.refs_4_), channel_id=1, source_target_pairs={{4,0},{5,1},{8,4},{9,5},{12,8},{13,9},{14,12},{15,13},{10,14},{11,... | collective-permute-start | bytes 1191944 | tf_op jit(solution)/shard_map/ppermute | solution.py:490
  35.8 12.4 %copy-start.1 = (f32[776,128]{1,0:T(8,128)}, f32[776,128]{1,0:T(8,128)S(1)}, u32[]{:S(2)}) copy-start(f32[776,128]{1,0:T(8,128)S(1)} %collective-permute-done.4.refs_5_) | copy-start | bytes 1191940
  37.5 10.8 %copy-start = (f32[776,128]{1,0:T(8,128)}, f32[776,128]{1,0:T(8,128)S(1)}, u32[]{:S(2)}) copy-start(f32[776,128]{1,0:T(8,128)S(1)} %collective-permute-done.5.refs_6_) | copy-start | bytes 1191940
  38.3 9.9 %collective-permute-start.8 = (f32[5432,128]{1,0:T(8,128)}, f32[5432,128]{1,0:T(8,128)}, u32[]{:S(2)}, u32[]{:S(2)}) collective-permute-start(f32[5432,128]{1,0:T(8,128)} %constant_dynamic-update-slice_fusion), channel_id=1, source_target_pairs={{0,1},{1,0},{2,3},{3,2},{4,5},{5,4},{6,7},{7,6},{8,9},{9,8},{10,11... | collective-permute-start | bytes 8343560 | tf_op jit(solution)/shard_map/ppermute | solution.py:497
  38.4 8.0 %collective-permute-start.7 = (f32[392,128]{1,0:T(8,128)S(1)}, f32[392,128]{1,0:T(8,128)S(1)}, u32[]{:S(2)}, u32[]{:S(2)}) collective-permute-start(f32[392,128]{1,0:T(8,128)S(1)} %slice.13), channel_id=1, source_target_pairs={{4,0},{5,1},{8,4},{9,5},{12,8},{13,9},{14,12},{15,13},{10,14},{11,... | collective-permute-start | bytes 602120 | tf_op jit(solution)/shard_map/ppermute | solution.py:486
  39.3 7.1 %collective-permute-start.6 = (f32[384,128]{1,0:T(8,128)S(1)}, f32[384,128]{1,0:T(8,128)S(1)}, u32[]{:S(2)}, u32[]{:S(2)}) collective-permute-start(f32[384,128]{1,0:T(8,128)S(1)} %slice.12), channel_id=1, source_target_pairs={{0,4},{1,5},{4,8},{5,9},{8,12},{9,13},{12,14},{13,15},{14,10},{15,... | collective-permute-start | bytes 589832 | tf_op jit(solution)/shard_map/ppermute | solution.py:485
  46.4 1.9 %copy-start.8 = (f32[384,128]{1,0:T(8,128)}, f32[384,128]{1,0:T(8,128)S(1)}, u32[]{:S(2)}) copy-start(f32[384,128]{1,0:T(8,128)S(1)} %collective-permute-done.6.refs_7_) | copy-start | bytes 589828
  46.4 0.7 copy-start.7
  46.4 1.8 collective-permute-start.9
  48.2 0.7 copy-start.9
  56.4 0.9 copy-start.10
  158.7 7.6 %collective-permute-start.10 = (f32[16,2,256,128]{3,2,1,0:T(8,128)}, f32[16,2,256,128]{3,2,1,0:T(8,128)}, u32[]{:S(2)}, u32[]{:S(2)}) collective-permute-start(f32[16,2,256,128]{3,2,1,0:T(8,128)} %get-tuple-element.8), channel_id=1, source_target_pairs={{0,1},{1,0},{2,3},{3,2},{4,5},{5,4},{6,7},{7,6},{8,9},{9,8},{10,11... | collective-permute-start | bytes 12582920 | tf_op jit(solution)/shard_map/ppermute | solution.py:567
